TPU v7x, 32 devices: a whole 2x2x4 slice. The times are simulated.
32 devices in a mesh: row: 4 (over y, x), grp: 4 (over z), col: 2 (over core).
Axes of the slice: x: 2, y: 2, z: 4, core: 2. Of those that a mesh axis runs over, the one named last changes fastest.
Arguments:
- state: float32 [64, 128, 256], P('row', ('grp', 'col')), may hold values from -6 to 6
- rate: float32 [64, 128], P('row', ('grp', 'col')), may hold values from 0.02 to 0.24
- cotangent: bfloat16 [64, 128, 256], P('row', ('grp', 'col')), may hold values from -6 to 6
- dest: int32 [4, 8, 256, 1], P('row', ('grp', 'col')), may hold values from 0 to 3; in each aligned block of 256 rows (0 to 255, 256 to 511, ..., all dimensions but the last counted through in order) at most 128 rows name the same one
- w_in: bfloat16 [4, 256, 1024], P('grp'), may hold values from -0.375 to 0.375
- w_out: bfloat16 [4, 256, 1024], P('grp'), may hold values from -0.1875 to 0.1875
Outputs:
- new_state: float32 [64, 128, 256], P('row', ('grp', 'col'))
- column_adjoint: bfloat16 [64, 128, 256], P('row', ('grp', 'col'))
- weight_grads: float32 [4, 4096, 128], P('grp', ('row', 'col'))
Inputs may be any that keep to these rules, and one draw needn't show every extreme that they name: `dest`: within one block no owner receives more than 128 columns, and some owner receives exactly 128 in some block.
All inputs are finite; a program needn't handle non-finite values.
Results may differ from a plain program's by a relative error of at most 0.0053.
Values may be sent and summed in bfloat16 or wider, within the bound.
No kernel may reach another device: no remote copies, remote signals or barrier semaphores. Data moves between devices by JAX's collectives and lax.ppermute only.
A program may use at most 64 MiB of HBM per device.

v0:
```python
import jax
import jax.numpy as jnp
from jax import lax
from jax.sharding import PartitionSpec as P

STEPS = 4


def padded_2(cells, sides, width):
    for axis, dim in sides:
        count = lax.axis_size(axis)
        head = lax.slice_in_dim(cells, 0, width, axis=dim)
        tail = lax.slice_in_dim(cells, cells.shape[dim] - width, cells.shape[dim], axis=dim)
        cells = jnp.concatenate(
            [
                lax.ppermute(tail, axis, [(i, (i + 1) % count) for i in range(count)]),
                cells,
                lax.ppermute(head, axis, [((i + 1) % count, i) for i in range(count)]),
            ],
            axis=dim,
        )
    return cells


def silu_slope(value):
    logistic = jax.nn.sigmoid(value)
    return logistic * (1.0 + value * (1.0 - logistic))


def local(state, rate, cotangent, dest, w_in, w_out):
    rows_blk, cols_blk, feats = state.shape
    count = rows_blk * cols_blk
    owners = lax.axis_size("grp")
    capacity = 2 * count // owners
    routes = dest.reshape(count)
    onehot = (routes[:, None] == jnp.arange(owners, dtype=jnp.int32)[None, :]).astype(jnp.int32)
    ranks = jnp.cumsum(onehot, axis=0) - 1
    places = routes * capacity + jnp.sum(ranks * onehot, axis=1)
    placing = (jnp.arange(owners * capacity, dtype=jnp.int32)[:, None] == places[None, :]).astype(
        jnp.bfloat16
    )
    columns = state.astype(jnp.bfloat16).reshape(count, feats)
    cotans = cotangent.reshape(count, feats)
    packed_cols = jnp.dot(placing, columns, preferred_element_type=jnp.float32).astype(jnp.bfloat16)
    packed_cots = jnp.dot(placing, cotans, preferred_element_type=jnp.float32).astype(jnp.bfloat16)
    recv_cols, recv_cots = (
        lax.all_to_all(
            packed_cols.reshape(owners, capacity, feats),
            "grp",
            split_axis=0,
            concat_axis=0,
            tiled=True,
        ),
        lax.all_to_all(
            packed_cots.reshape(owners, capacity, feats),
            "grp",
            split_axis=0,
            concat_axis=0,
            tiled=True,
        ),
    )
    owner_cols = recv_cols.reshape(owners * capacity, feats)
    owner_cots = recv_cots.reshape(owners * capacity, feats)
    field = state
    for step in range(STEPS):
        padded = padded_2(field.astype(jnp.bfloat16), (("row", 0), (("grp", "col"), 1)), 1).astype(
            field.dtype
        )
        beside = padded[2:, 1:-1] + padded[:-2, 1:-1] + padded[1:-1, 2:] + padded[1:-1, :-2]
        field = field + rate[:, :, None] * (beside - 4.0 * field)
    weight_in = w_in[0]
    weight_out = w_out[0]
    pre = jnp.dot(owner_cols, weight_in, preferred_element_type=jnp.float32)
    act = jax.nn.silu(pre).astype(jnp.bfloat16)
    tend = lax.dot_general(
        act, weight_out, (((1,), (1,)), ((), ())), preferred_element_type=jnp.float32
    ).astype(jnp.bfloat16)
    dtend = (0.5 * owner_cots.astype(jnp.float32)).astype(jnp.bfloat16)
    dact = jnp.dot(dtend, weight_out, preferred_element_type=jnp.float32)
    dpre = (dact * silu_slope(pre)).astype(jnp.bfloat16)
    adjoint = lax.dot_general(
        dpre, weight_in, (((1,), (1,)), ((), ())), preferred_element_type=jnp.float32
    ).astype(jnp.bfloat16)
    back_tend, back_adj = (
        lax.all_to_all(
            tend.reshape(owners, capacity, feats), "grp", split_axis=0, concat_axis=0, tiled=True
        ),
        lax.all_to_all(
            adjoint.reshape(owners, capacity, feats), "grp", split_axis=0, concat_axis=0, tiled=True
        ),
    )
    grad_in = lax.dot_general(
        owner_cols, dpre, (((0,), (0,)), ((), ())), preferred_element_type=jnp.float32
    )
    grad_out = lax.dot_general(
        dtend, act, (((0,), (0,)), ((), ())), preferred_element_type=jnp.float32
    )
    flat = jnp.stack([grad_in, grad_out], axis=0).reshape(-1, 128)
    summed = lax.psum_scatter(flat, ("row", "col"), scatter_dimension=0, tiled=True)
    tendency = jnp.take(back_tend.reshape(owners * capacity, feats), places, axis=0)
    column_adjoint = jnp.take(back_adj.reshape(owners * capacity, feats), places, axis=0)
    new_state = field + 0.5 * tendency.astype(jnp.float32).reshape(rows_blk, cols_blk, feats)
    return (new_state, column_adjoint.reshape(rows_blk, cols_blk, feats), summed[None])


def solution(mesh):
    in_specs = (
        P("row", ("grp", "col"), None),
        P("row", ("grp", "col")),
        P("row", ("grp", "col"), None),
        P("row", ("grp", "col"), None, None),
        P("grp", None, None),
        P("grp", None, None),
    )
    out_specs = (
        P("row", ("grp", "col"), None),
        P("row", ("grp", "col"), None),
        P("grp", ("row", "col"), None),
    )
    return jax.shard_map(local, mesh=mesh, in_specs=in_specs, out_specs=out_specs, check_vma=False)
```

profile of v0, /device:TPU:0, one launch (start us, length us, event | category | flops | bytes accessed | tf_op | source)
XLA Modules:
  0.0 99.7 jit_solution(5127164071173445638)
XLA Ops:
  7.2 0.0 copy-start
  7.2 1.0 %convert_element_type.64 = bf16[16,16,256]{2,1,0:T(8,128)(2,1)S(1)} convert(f32[16,16,256]{2,1,0:T(8,128)} %param.8) | non-fusion elementwise | flops 65536 | bytes 393216 | tf_op jit(solution)/shard_map/convert_element_type | solution.py:66
  8.3 3.9 %collective-permute-start.1 = (bf16[1,16,256]{2,1,0:T(8,128)(2,1)S(1)}, bf16[1,16,256]{2,1,0:T(8,128)(2,1)S(1)}, u32[]{:S(2)}, u32[]{:S(2)}) collective-permute-start(bf16[1,16,256]{2,1,0:T(8,128)(2,1)S(1)} %get-tuple-element.27), channel_id=1, source_target_pairs={{8,0},{16,8},{24,16},{0,24},{9,1},{17,9},{25,17},{1,25},{10,2},{18... | collective-permute-start | bytes 24584 | tf_op jit(solution)/shard_map/ppermute | solution.py:18
  12.2 0.7 compare_convert_fusion
  12.9 1.2 %reduce-window.6 = s32[4,2,128]{2,1,0:T(2,128)S(1)} reduce-window(s32[4,2,128]{2,1,0:T(2,128)S(1)} %compare_convert_fusion, s32[]{:T(128)} %constant.16.clone.1), window={size=1x1x128 pad=0_0x0_0x127_0}, to_apply=%region_0.0 | reduce-window | flops 130048 | bytes 8196 | tf_op jit(solution)/shard_map/reduce-window
  14.1 0.1 slice.164
  14.2 0.1 copy.9
  14.3 0.1 copy.10
  14.4 0.1 add_bitcast_fusion
  14.5 0.7 fusion.21
  15.2 0.7 compare_and_fusion
  15.9 0.9 collective-permute-done
  16.8 2.0 %collective-permute-start.3 = (bf16[18,1,256]{2,1,0:T(2,128)(2,1)S(1)}, bf16[18,1,256]{2,1,0:T(2,128)(2,1)S(1)}, u32[]{:S(2)}, u32[]{:S(2)}) collective-permute-start(bf16[18,1,256]{2,1,0:T(2,128)(2,1)S(1)} %get-tuple-element.19), channel_id=1, source_target_pairs={{1,0},{2,1},{3,2},{4,3},{5,4},{6,5},{7,6},{0,7},{9,8},{10,9},{11,1... | collective-permute-start | bytes 27656 | tf_op jit(solution)/shard_map/ppermute | solution.py:18
  18.8 0.9 convolution_convert_fusion.3
  19.7 3.5 %all-to-all-start = ((bf16[4,128,256]{2,1,0:T(8,128)(2,1)}), bf16[4,128,256]{2,1,0:T(8,128)(2,1)S(1)}, u32[]{:S(2)}, u32[]{:S(2)}) async-start(bf16[4,128,256]{2,1,0:T(8,128)(2,1)} %bitcast.5), calls=%async_computation | async-start | bytes 524288 | tf_op jit(solution)/shard_map/all_to_all | solution.py:47
  23.2 0.6 collective-permute-done.2
  23.7 0.1 maximum_convert_fusion
  23.9 0.1 fusion.26
  24.0 2.7 %collective-permute-start.5 = (bf16[1,16,256]{2,1,0:T(8,128)(2,1)S(1)}, bf16[1,16,256]{2,1,0:T(8,128)(2,1)S(1)}, u32[]{:S(2)}, u32[]{:S(2)}) collective-permute-start(bf16[1,16,256]{2,1,0:T(8,128)(2,1)S(1)} %get-tuple-element.25), channel_id=1, source_target_pairs={{8,0},{16,8},{24,16},{0,24},{9,1},{17,9},{25,17},{1,25},{10,2},{18... | collective-permute-start | bytes 24584 | tf_op jit(solution)/shard_map/ppermute | solution.py:18
  26.7 0.9 convolution_convert_fusion.1
  27.6 4.4 %all-to-all-done = bf16[4,128,256]{2,1,0:T(8,128)(2,1)S(1)} async-done(((bf16[4,128,256]{2,1,0:T(8,128)(2,1)}), bf16[4,128,256]{2,1,0:T(8,128)(2,1)S(1)}, u32[]{:S(2)}, u32[]{:S(2)}) %all-to-all-start) | async-done | bytes 262176 | tf_op jit(solution)/shard_map/all_to_all | solution.py:47
  32.1 3.8 %all-to-all-start.2 = ((bf16[4,128,256]{2,1,0:T(8,128)(2,1)}), bf16[4,128,256]{2,1,0:T(8,128)(2,1)S(1)}, u32[]{:S(2)}, u32[]{:S(2)}) async-start(bf16[4,128,256]{2,1,0:T(8,128)(2,1)} %bitcast.13), calls=%async_computation.2 | async-start | bytes 524288 | tf_op jit(solution)/shard_map/all_to_all | solution.py:54
  36.0 4.0 %collective-permute-start.7 = (bf16[18,1,256]{2,1,0:T(2,128)(2,1)S(1)}, bf16[18,1,256]{2,1,0:T(2,128)(2,1)S(1)}, u32[]{:S(2)}, u32[]{:S(2)}) collective-permute-start(bf16[18,1,256]{2,1,0:T(2,128)(2,1)S(1)} %get-tuple-element.17), channel_id=1, source_target_pairs={{1,0},{2,1},{3,2},{4,3},{5,4},{6,5},{7,6},{0,7},{9,8},{10,9},{11,1... | collective-permute-start | bytes 27656 | tf_op jit(solution)/shard_map/ppermute | solution.py:18
  39.9 2.0 %multiply_convert_fusion.1 = (bf16[512,1024]{1,0:T(8,128)(2,1)S(1)}, f32[512,1024]{1,0:T(8,128)}) fusion(bf16[512,256]{1,0:T(8,128)(2,1)S(1)} %bitcast.59, bf16[1,256,1024]{2,1,0:T(8,128)(2,1)S(1)} %copy-done), kind=kOutput, calls=%fused_computation.4 | convolution fusion | flops 271056896 | bytes 3932160 | tf_op jit(solution)/shard_map/dot_general | solution.py:73
  41.9 4.2 %all-to-all-done.2 = bf16[4,128,256]{2,1,0:T(8,128)(2,1)S(1)} async-done(((bf16[4,128,256]{2,1,0:T(8,128)(2,1)}), bf16[4,128,256]{2,1,0:T(8,128)(2,1)S(1)}, u32[]{:S(2)}, u32[]{:S(2)}) %all-to-all-start.2) | async-done | bytes 262176 | tf_op jit(solution)/shard_map/all_to_all | solution.py:54
  46.2 0.5 convolution_bitcast_fusion
  46.7 0.5 copy-done.8
  47.2 0.7 copy-done.10
  48.0 0.8 multiply_convert_fusion
  48.8 1.0 copy-done.1
  49.8 0.5 convolution_bitcast_fusion.1
  50.3 0.2 pad_maximum_fusion
  50.5 1.5 %reshape.96 = f32[4096,128]{1,0:T(8,128)} reshape(f32[2,256,1024]{2,1,0:T(8,128)S(1)} %pad_maximum_fusion) | data formatting | bytes 4194304 | tf_op jit(solution)/shard_map/reshape | solution.py:98
  52.0 0.0 reduce-scatter.2.cloned.1.call-update
  52.1 0.1 maximum_convert_fusion.1
  52.2 0.1 fusion.24
  52.3 2.6 %collective-permute-start.9 = (bf16[1,16,256]{2,1,0:T(8,128)(2,1)S(1)}, bf16[1,16,256]{2,1,0:T(8,128)(2,1)S(1)}, u32[]{:S(2)}, u32[]{:S(2)}) collective-permute-start(bf16[1,16,256]{2,1,0:T(8,128)(2,1)S(1)} %get-tuple-element.23), channel_id=1, source_target_pairs={{8,0},{16,8},{24,16},{0,24},{9,1},{17,9},{25,17},{1,25},{10,2},{18... | collective-permute-start | bytes 24584 | tf_op jit(solution)/shard_map/ppermute | solution.py:18
  54.9 1.4 %collective-permute-done.9 = bf16[1,16,256]{2,1,0:T(8,128)(2,1)S(1)} collective-permute-done((bf16[1,16,256]{2,1,0:T(8,128)(2,1)S(1)}, bf16[1,16,256]{2,1,0:T(8,128)(2,1)S(1)}, u32[]{:S(2)}, u32[]{:S(2)}) %collective-permute-start.9) | collective-permute-done | bytes 8224 | tf_op jit(solution)/shard_map/ppermute | solution.py:18
  56.3 3.2 %collective-permute-done.8 = bf16[1,16,256]{2,1,0:T(8,128)(2,1)S(1)} collective-permute-done((bf16[1,16,256]{2,1,0:T(8,128)(2,1)S(1)}, bf16[1,16,256]{2,1,0:T(8,128)(2,1)S(1)}, u32[]{:S(2)}, u32[]{:S(2)}) %collective-permute-start.8) | collective-permute-done | bytes 8224 | tf_op jit(solution)/shard_map/ppermute | solution.py:16
  59.5 0.1 collective-permute-start.11
  59.6 0.5 collective-permute-start.10
  60.1 1.0 collective-permute-done.11
  61.0 3.6 %collective-permute-done.10 = bf16[18,1,256]{2,1,0:T(2,128)(2,1)S(1)} collective-permute-done((bf16[18,1,256]{2,1,0:T(2,128)(2,1)S(1)}, bf16[18,1,256]{2,1,0:T(2,128)(2,1)S(1)}, u32[]{:S(2)}, u32[]{:S(2)}) %collective-permute-start.10) | collective-permute-done | bytes 9248 | tf_op jit(solution)/shard_map/ppermute | solution.py:16
  64.6 0.1 maximum_convert_fusion.2
  64.7 0.1 fusion.22
  64.9 1.2 %convolution_convert_fusion.2 = bf16[512,256]{1,0:T(8,128)(2,1)} fusion(bf16[512,1024]{1,0:T(8,128)(2,1)S(1)} %copy-done.4, bf16[1,256,1024]{2,1,0:T(8,128)(2,1)S(1)} %copy-done.9), kind=kOutput, calls=%fused_computation.10 | convolution fusion | flops 268566528 | bytes 1835008 | tf_op jit(solution)/shard_map/dot_general | solution.py:75
  66.1 3.4 %all-to-all-start.1 = ((bf16[4,128,256]{2,1,0:T(8,128)(2,1)}), bf16[4,128,256]{2,1,0:T(8,128)(2,1)S(1)}, u32[]{:S(2)}, u32[]{:S(2)}) async-start(bf16[4,128,256]{2,1,0:T(8,128)(2,1)} %bitcast.9), calls=%async_computation.1 | async-start | bytes 524288 | tf_op jit(solution)/shard_map/all_to_all | solution.py:85
  69.5 0.1 collective-permute-start.13
  69.5 2.0 %collective-permute-start.12 = (bf16[1,16,256]{2,1,0:T(8,128)(2,1)S(1)}, bf16[1,16,256]{2,1,0:T(8,128)(2,1)S(1)}, u32[]{:S(2)}, u32[]{:S(2)}) collective-permute-start(bf16[1,16,256]{2,1,0:T(8,128)(2,1)S(1)} %get-tuple-element.20), channel_id=1, source_target_pairs={{0,8},{8,16},{16,24},{24,0},{1,9},{9,17},{17,25},{25,1},{2,10},{10... | collective-permute-start | bytes 24584 | tf_op jit(solution)/shard_map/ppermute | solution.py:16
  71.6 1.2 %convolution_convert_fusion = bf16[512,256]{1,0:T(8,128)(2,1)} fusion(bf16[512,1024]{1,0:T(8,128)(2,1)S(1)} %copy-done.2, bf16[1,256,1024]{2,1,0:T(8,128)(2,1)S(1)} %copy-done), kind=kOutput, calls=%fused_computation.8 | convolution fusion | flops 268566528 | bytes 1835008 | tf_op jit(solution)/shard_map/dot_general | solution.py:81
  72.7 3.5 %all-to-all-done.1 = bf16[4,128,256]{2,1,0:T(8,128)(2,1)S(1)} async-done(((bf16[4,128,256]{2,1,0:T(8,128)(2,1)}), bf16[4,128,256]{2,1,0:T(8,128)(2,1)S(1)}, u32[]{:S(2)}, u32[]{:S(2)}) %all-to-all-start.1) | async-done | bytes 262176 | tf_op jit(solution)/shard_map/all_to_all | solution.py:85
  76.2 3.4 %all-to-all-start.3 = ((bf16[4,128,256]{2,1,0:T(8,128)(2,1)}), bf16[4,128,256]{2,1,0:T(8,128)(2,1)S(1)}, u32[]{:S(2)}, u32[]{:S(2)}) async-start(bf16[4,128,256]{2,1,0:T(8,128)(2,1)} %bitcast.15), calls=%async_computation.3 | async-start | bytes 524288 | tf_op jit(solution)/shard_map/all_to_all | solution.py:88
  79.7 0.1 collective-permute-start.15
  79.8 0.5 collective-permute-start.14
  80.3 3.2 %collective-permute-done.15 = bf16[18,1,256]{2,1,0:T(2,128)(2,1)S(1)} collective-permute-done((bf16[18,1,256]{2,1,0:T(2,128)(2,1)S(1)}, bf16[18,1,256]{2,1,0:T(2,128)(2,1)S(1)}, u32[]{:S(2)}, u32[]{:S(2)}) %collective-permute-start.15) | collective-permute-done | bytes 9248 | tf_op jit(solution)/shard_map/ppermute | solution.py:18
  83.4 1.8 %collective-permute-done.14 = bf16[18,1,256]{2,1,0:T(2,128)(2,1)S(1)} collective-permute-done((bf16[18,1,256]{2,1,0:T(2,128)(2,1)S(1)}, bf16[18,1,256]{2,1,0:T(2,128)(2,1)S(1)}, u32[]{:S(2)}, u32[]{:S(2)}) %collective-permute-start.14) | collective-permute-done | bytes 9248 | tf_op jit(solution)/shard_map/ppermute | solution.py:16
  85.2 0.1 maximum_convert_fusion.3
  85.3 1.2 %gather_fusion = bf16[256,256]{1,0:T(8,128)(2,1)S(1)} fusion(bf16[512,256]{1,0:T(8,128)(2,1)S(1)} %bitcast.56, s32[1024]{0:T(1024)S(1)} %pad_clamp_fusion), kind=kCustom, calls=%fused_computation.clone | custom fusion | bytes 263168 | tf_op jit(solution)/shard_map/jit(_take)/gather | solution.py:100
  86.5 0.1 all-to-all-done.3
  86.6 1.2 %gather_fusion.1 = bf16[256,256]{1,0:T(8,128)(2,1)S(1)} fusion(bf16[512,256]{1,0:T(8,128)(2,1)S(1)} %bitcast.57, s32[1024]{0:T(1024)S(1)} %pad_clamp_fusion), kind=kCustom, calls=%fused_computation.1.clone | custom fusion | bytes 263168 | tf_op jit(solution)/shard_map/jit(_take)/gather | solution.py:101
  87.8 0.8 broadcast_select_fusion
  88.5 0.1 convert_multiply_fusion
  88.6 0.8 fusion.8
  89.5 3.4 %reduce-scatter.2.cloned.1.call-done = f32[512,128]{1,0:T(8,128)} async-done(((f32[4096,128]{1,0:T(8,128)}), f32[512,128]{1,0:T(8,128)}) %reduce-scatter.2.cloned.1.call-update) | async-done | bytes 262160 | tf_op jit(solution)/shard_map/reduce_scatter | solution.py:99
  (45 shorter events, 0.3 us)
Async XLA Ops:
  7.2 32.8 %copy-start = (bf16[1,256,1024]{2,1,0:T(8,128)(2,1)S(1)}, bf16[1,256,1024]{2,1,0:T(8,128)(2,1)}, u32[]{:S(2)}) copy-start(bf16[1,256,1024]{2,1,0:T(8,128)(2,1)} %param.12) | copy-start | bytes 1572868
  7.2 16.7 %copy-start.5 = (f32[16,16,256]{2,1,0:T(8,128)S(1)}, f32[16,16,256]{2,1,0:T(8,128)}, u32[]{:S(2)}) copy-start(f32[16,16,256]{2,1,0:T(8,128)} %param.8) | copy-start | bytes 786436
  7.2 16.7 %copy-start.6 = (f32[16,16]{1,0:T(8,128)S(1)}, f32[16,16]{1,0:T(8,128)}, u32[]{:S(2)}) copy-start(f32[16,16]{1,0:T(8,128)} %param.9) | copy-start | bytes 3076
  7.2 19.5 %copy-start.7 = (bf16[16,16,256]{2,1,0:T(8,128)(2,1)S(1)}, bf16[16,16,256]{2,1,0:T(8,128)(2,1)}, u32[]{:S(2)}) copy-start(bf16[16,16,256]{2,1,0:T(8,128)(2,1)} %param.10) | copy-start | bytes 393220
  8.3 7.6 %collective-permute-start.1 = (bf16[1,16,256]{2,1,0:T(8,128)(2,1)S(1)}, bf16[1,16,256]{2,1,0:T(8,128)(2,1)S(1)}, u32[]{:S(2)}, u32[]{:S(2)}) collective-permute-start(bf16[1,16,256]{2,1,0:T(8,128)(2,1)S(1)} %get-tuple-element.27), channel_id=1, source_target_pairs={{8,0},{16,8},{24,16},{0,24},{9,1},{17,9},{25,17},{1,25},{10,2},{18... | collective-permute-start | bytes 24584 | tf_op jit(solution)/shard_map/ppermute | solution.py:18
  12.2 4.5 %collective-permute-start = (bf16[1,16,256]{2,1,0:T(8,128)(2,1)S(1)}, bf16[1,16,256]{2,1,0:T(8,128)(2,1)S(1)}, u32[]{:S(2)}, u32[]{:S(2)}) collective-permute-start(bf16[1,16,256]{2,1,0:T(8,128)(2,1)S(1)} %get-tuple-element.26), channel_id=1, source_target_pairs={{0,8},{8,16},{16,24},{24,0},{1,9},{9,17},{17,25},{25,1},{2,10},{10... | collective-permute-start | bytes 24584 | tf_op jit(solution)/shard_map/ppermute | solution.py:16
  16.8 6.4 %collective-permute-start.3 = (bf16[18,1,256]{2,1,0:T(2,128)(2,1)S(1)}, bf16[18,1,256]{2,1,0:T(2,128)(2,1)S(1)}, u32[]{:S(2)}, u32[]{:S(2)}) collective-permute-start(bf16[18,1,256]{2,1,0:T(2,128)(2,1)S(1)} %get-tuple-element.19), channel_id=1, source_target_pairs={{1,0},{2,1},{3,2},{4,3},{5,4},{6,5},{7,6},{0,7},{9,8},{10,9},{11,1... | collective-permute-start | bytes 27656 | tf_op jit(solution)/shard_map/ppermute | solution.py:18
  18.8 5.0 %collective-permute-start.2 = (bf16[18,1,256]{2,1,0:T(2,128)(2,1)S(1)}, bf16[18,1,256]{2,1,0:T(2,128)(2,1)S(1)}, u32[]{:S(2)}, u32[]{:S(2)}) collective-permute-start(bf16[18,1,256]{2,1,0:T(2,128)(2,1)S(1)} %get-tuple-element.18), channel_id=1, source_target_pairs={{0,1},{1,2},{2,3},{3,4},{4,5},{5,6},{6,7},{7,0},{8,9},{9,10},{10,1... | collective-permute-start | bytes 27656 | tf_op jit(solution)/shard_map/ppermute | solution.py:16
  19.7 12.4 %all-to-all-start = ((bf16[4,128,256]{2,1,0:T(8,128)(2,1)}), bf16[4,128,256]{2,1,0:T(8,128)(2,1)S(1)}, u32[]{:S(2)}, u32[]{:S(2)}) async-start(bf16[4,128,256]{2,1,0:T(8,128)(2,1)} %bitcast.5), calls=%async_computation | async-start | bytes 524288 | tf_op jit(solution)/shard_map/all_to_all | solution.py:47
  24.0 11.9 %collective-permute-start.5 = (bf16[1,16,256]{2,1,0:T(8,128)(2,1)S(1)}, bf16[1,16,256]{2,1,0:T(8,128)(2,1)S(1)}, u32[]{:S(2)}, u32[]{:S(2)}) collective-permute-start(bf16[1,16,256]{2,1,0:T(8,128)(2,1)S(1)} %get-tuple-element.25), channel_id=1, source_target_pairs={{8,0},{16,8},{24,16},{0,24},{9,1},{17,9},{25,17},{1,25},{10,2},{18... | collective-permute-start | bytes 24584 | tf_op jit(solution)/shard_map/ppermute | solution.py:18
  26.7 9.2 %collective-permute-start.4 = (bf16[1,16,256]{2,1,0:T(8,128)(2,1)S(1)}, bf16[1,16,256]{2,1,0:T(8,128)(2,1)S(1)}, u32[]{:S(2)}, u32[]{:S(2)}) collective-permute-start(bf16[1,16,256]{2,1,0:T(8,128)(2,1)S(1)} %get-tuple-element.24), channel_id=1, source_target_pairs={{0,8},{8,16},{16,24},{24,0},{1,9},{9,17},{17,25},{25,1},{2,10},{10... | collective-permute-start | bytes 24584 | tf_op jit(solution)/shard_map/ppermute | solution.py:16
  32.1 14.1 %all-to-all-start.2 = ((bf16[4,128,256]{2,1,0:T(8,128)(2,1)}), bf16[4,128,256]{2,1,0:T(8,128)(2,1)S(1)}, u32[]{:S(2)}, u32[]{:S(2)}) async-start(bf16[4,128,256]{2,1,0:T(8,128)(2,1)} %bitcast.13), calls=%async_computation.2 | async-start | bytes 524288 | tf_op jit(solution)/shard_map/all_to_all | solution.py:54
  35.9 56.9 %reduce-scatter.2.cloned.1.call-start = ((), (), s32[]{:S(2)}) async-start(), calls=%async_computation.5 | async-start | bytes 2359296 | tf_op jit(solution)/shard_map/reduce_scatter | solution.py:99
  36.0 16.1 %collective-permute-start.7 = (bf16[18,1,256]{2,1,0:T(2,128)(2,1)S(1)}, bf16[18,1,256]{2,1,0:T(2,128)(2,1)S(1)}, u32[]{:S(2)}, u32[]{:S(2)}) collective-permute-start(bf16[18,1,256]{2,1,0:T(2,128)(2,1)S(1)} %get-tuple-element.17), channel_id=1, source_target_pairs={{1,0},{2,1},{3,2},{4,3},{5,4},{6,5},{7,6},{0,7},{9,8},{10,9},{11,1... | collective-permute-start | bytes 27656 | tf_op jit(solution)/shard_map/ppermute | solution.py:18
  39.9 12.2 %collective-permute-start.6 = (bf16[18,1,256]{2,1,0:T(2,128)(2,1)S(1)}, bf16[18,1,256]{2,1,0:T(2,128)(2,1)S(1)}, u32[]{:S(2)}, u32[]{:S(2)}) collective-permute-start(bf16[18,1,256]{2,1,0:T(2,128)(2,1)S(1)} %get-tuple-element.16), channel_id=1, source_target_pairs={{0,1},{1,2},{2,3},{3,4},{4,5},{5,6},{6,7},{7,0},{8,9},{9,10},{10,1... | collective-permute-start | bytes 27656 | tf_op jit(solution)/shard_map/ppermute | solution.py:16
  41.9 4.8 %copy-start.3 = (bf16[512,1024]{1,0:T(8,128)(2,1)}, bf16[512,1024]{1,0:T(8,128)(2,1)S(1)}, u32[]{:S(2)}) copy-start(bf16[512,1024]{1,0:T(8,128)(2,1)S(1)} %get-tuple-element.28) | copy-start | bytes 3145732
  46.2 1.0 %copy-start.8 = (bf16[1,256,1024]{2,1,0:T(8,128)(2,1)S(1)}, bf16[1,256,1024]{2,1,0:T(8,128)(2,1)}, u32[]{:S(2)}) copy-start(bf16[1,256,1024]{2,1,0:T(8,128)(2,1)} %param.13) | copy-start | bytes 1572868
  46.2 1.8 %copy-start.10 = (f32[512,1024]{1,0:T(8,128)S(1)}, f32[512,1024]{1,0:T(8,128)}, u32[]{:S(2)}) copy-start(f32[512,1024]{1,0:T(8,128)} %get-tuple-element.29) | copy-start | bytes 6291460
  48.8 1.0 copy-start.1
  52.2 12.7 %copy-start.4 = (bf16[512,1024]{1,0:T(8,128)(2,1)S(1)}, bf16[512,1024]{1,0:T(8,128)(2,1)}, u32[]{:S(2)}) copy-start(bf16[512,1024]{1,0:T(8,128)(2,1)} %copy-done.3) | copy-start | bytes 3145732
  52.2 12.7 %copy-start.9 = (bf16[1,256,1024]{2,1,0:T(8,128)(2,1)S(1)}, bf16[1,256,1024]{2,1,0:T(8,128)(2,1)}, u32[]{:S(2)}) copy-start(bf16[1,256,1024]{2,1,0:T(8,128)(2,1)} %param.13) | copy-start | bytes 1572868
  52.3 4.0 %collective-permute-start.9 = (bf16[1,16,256]{2,1,0:T(8,128)(2,1)S(1)}, bf16[1,16,256]{2,1,0:T(8,128)(2,1)S(1)}, u32[]{:S(2)}, u32[]{:S(2)}) collective-permute-start(bf16[1,16,256]{2,1,0:T(8,128)(2,1)S(1)} %get-tuple-element.23), channel_id=1, source_target_pairs={{8,0},{16,8},{24,16},{0,24},{9,1},{17,9},{25,17},{1,25},{10,2},{18... | collective-permute-start | bytes 24584 | tf_op jit(solution)/shard_map/ppermute | solution.py:18
  54.9 4.5 %collective-permute-start.8 = (bf16[1,16,256]{2,1,0:T(8,128)(2,1)S(1)}, bf16[1,16,256]{2,1,0:T(8,128)(2,1)S(1)}, u32[]{:S(2)}, u32[]{:S(2)}) collective-permute-start(bf16[1,16,256]{2,1,0:T(8,128)(2,1)S(1)} %get-tuple-element.22), channel_id=1, source_target_pairs={{0,8},{8,16},{16,24},{24,0},{1,9},{9,17},{17,25},{25,1},{2,10},{10... | collective-permute-start | bytes 24584 | tf_op jit(solution)/shard_map/ppermute | solution.py:16
  59.5 1.5 %collective-permute-start.11 = (bf16[18,1,256]{2,1,0:T(2,128)(2,1)S(1)}, bf16[18,1,256]{2,1,0:T(2,128)(2,1)S(1)}, u32[]{:S(2)}, u32[]{:S(2)}) collective-permute-start(bf16[18,1,256]{2,1,0:T(2,128)(2,1)S(1)} %get-tuple-element.15), channel_id=1, source_target_pairs={{1,0},{2,1},{3,2},{4,3},{5,4},{6,5},{7,6},{0,7},{9,8},{10,9},{11,1... | collective-permute-start | bytes 27656 | tf_op jit(solution)/shard_map/ppermute | solution.py:18
  59.6 5.0 %collective-permute-start.10 = (bf16[18,1,256]{2,1,0:T(2,128)(2,1)S(1)}, bf16[18,1,256]{2,1,0:T(2,128)(2,1)S(1)}, u32[]{:S(2)}, u32[]{:S(2)}) collective-permute-start(bf16[18,1,256]{2,1,0:T(2,128)(2,1)S(1)} %get-tuple-element.14), channel_id=1, source_target_pairs={{0,1},{1,2},{2,3},{3,4},{4,5},{5,6},{6,7},{7,0},{8,9},{9,10},{10,1... | collective-permute-start | bytes 27656 | tf_op jit(solution)/shard_map/ppermute | solution.py:16
  64.7 6.8 %copy-start.2 = (bf16[512,1024]{1,0:T(8,128)(2,1)S(1)}, bf16[512,1024]{1,0:T(8,128)(2,1)}, u32[]{:S(2)}) copy-start(bf16[512,1024]{1,0:T(8,128)(2,1)} %copy-done.1) | copy-start | bytes 3145732
  66.1 10.2 %all-to-all-start.1 = ((bf16[4,128,256]{2,1,0:T(8,128)(2,1)}), bf16[4,128,256]{2,1,0:T(8,128)(2,1)S(1)}, u32[]{:S(2)}, u32[]{:S(2)}) async-start(bf16[4,128,256]{2,1,0:T(8,128)(2,1)} %bitcast.9), calls=%async_computation.1 | async-start | bytes 524288 | tf_op jit(solution)/shard_map/all_to_all | solution.py:85
  69.5 10.2 %collective-permute-start.13 = (bf16[1,16,256]{2,1,0:T(8,128)(2,1)S(1)}, bf16[1,16,256]{2,1,0:T(8,128)(2,1)S(1)}, u32[]{:S(2)}, u32[]{:S(2)}) collective-permute-start(bf16[1,16,256]{2,1,0:T(8,128)(2,1)S(1)} %get-tuple-element.21), channel_id=1, source_target_pairs={{8,0},{16,8},{24,16},{0,24},{9,1},{17,9},{25,17},{1,25},{10,2},{18... | collective-permute-start | bytes 24584 | tf_op jit(solution)/shard_map/ppermute | solution.py:18
  69.5 10.1 %collective-permute-start.12 = (bf16[1,16,256]{2,1,0:T(8,128)(2,1)S(1)}, bf16[1,16,256]{2,1,0:T(8,128)(2,1)S(1)}, u32[]{:S(2)}, u32[]{:S(2)}) collective-permute-start(bf16[1,16,256]{2,1,0:T(8,128)(2,1)S(1)} %get-tuple-element.20), channel_id=1, source_target_pairs={{0,8},{8,16},{16,24},{24,0},{1,9},{9,17},{17,25},{25,1},{2,10},{10... | collective-permute-start | bytes 24584 | tf_op jit(solution)/shard_map/ppermute | solution.py:16
  76.2 10.4 %all-to-all-start.3 = ((bf16[4,128,256]{2,1,0:T(8,128)(2,1)}), bf16[4,128,256]{2,1,0:T(8,128)(2,1)S(1)}, u32[]{:S(2)}, u32[]{:S(2)}) async-start(bf16[4,128,256]{2,1,0:T(8,128)(2,1)} %bitcast.15), calls=%async_computation.3 | async-start | bytes 524288 | tf_op jit(solution)/shard_map/all_to_all | solution.py:88
  79.7 3.7 %collective-permute-start.15 = (bf16[18,1,256]{2,1,0:T(2,128)(2,1)S(1)}, bf16[18,1,256]{2,1,0:T(2,128)(2,1)S(1)}, u32[]{:S(2)}, u32[]{:S(2)}) collective-permute-start(bf16[18,1,256]{2,1,0:T(2,128)(2,1)S(1)} %get-tuple-element.13), channel_id=1, source_target_pairs={{1,0},{2,1},{3,2},{4,3},{5,4},{6,5},{7,6},{0,7},{9,8},{10,9},{11,1... | collective-permute-start | bytes 27656 | tf_op jit(solution)/shard_map/ppermute | solution.py:18
  79.8 5.5 %collective-permute-start.14 = (bf16[18,1,256]{2,1,0:T(2,128)(2,1)S(1)}, bf16[18,1,256]{2,1,0:T(2,128)(2,1)S(1)}, u32[]{:S(2)}, u32[]{:S(2)}) collective-permute-start(bf16[18,1,256]{2,1,0:T(2,128)(2,1)S(1)} %get-tuple-element.12), channel_id=1, source_target_pairs={{0,1},{1,2},{2,3},{3,4},{4,5},{5,6},{6,7},{7,0},{8,9},{9,10},{10,1... | collective-permute-start | bytes 27656 | tf_op jit(solution)/shard_map/ppermute | solution.py:16
Sparse Core Ops, SparseCore 0:
  52.2 40.6 reduce-scatter.1
where the time goes:
time: 100 us; the launch traced here: 99.7 us
  starting transfers between devices  32.5 us (32%)
  waiting for transfers between devices  31.2 us (31%)
  between operations  14.3 us (14%)
  matrix products  8.01 us (8%)
  other arithmetic  7.25 us (7%)
  local copies, waits for them, and re-layouts  6.41 us (6%)
    ppermute x8, starting transfers between devices, padded_2(): lax.ppermute(head, axis, [((i + 1) % count, i) for i in range(count)])  15.3 us
    ppermute x8, waiting for transfers between devices, padded_2(): lax.ppermute(tail, axis, [(i, (i + 1) % count) for i in range(count)])  9.99 us
    ppermute x8, waiting for transfers between devices, padded_2(): lax.ppermute(head, axis, [((i + 1) % count, i) for i in range(count)])  5.5 us
    all_to_all x1, waiting for transfers between devices, local(): lax.all_to_all(packed_cols.reshape(owners, capacity, feats), 'grp', split...  4.44 us
    all_to_all x1, waiting for transfers between devices, local(): lax.all_to_all(packed_cots.reshape(owners, capacity, feats), 'grp', split...  4.25 us
    all_to_all x1, starting transfers between devices, local(): lax.all_to_all(packed_cots.reshape(owners, capacity, feats), 'grp', split...  3.83 us
    all_to_all x1, starting transfers between devices, local(): lax.all_to_all(packed_cols.reshape(owners, capacity, feats), 'grp', split...  3.47 us
    all_to_all x1, waiting for transfers between devices, local(): lax.all_to_all(tend.reshape(owners, capacity, feats), 'grp', split_axis=0...  3.47 us
  transfers between devices with their start and end apart: 21, of which 13 were waited for; matrix products, arithmetic and copies ran while one was open for 18% of the time, Pallas kernels for 0%

commit v1 on v0

v1 whole, which is shorter than its diff:
```python
import functools

import jax
import jax.numpy as jnp
from jax import lax
from jax.experimental import pallas as pl
from jax.experimental.pallas import tpu as pltpu
from jax.sharding import PartitionSpec as P

STEPS = 4
BF16 = jnp.bfloat16
F32 = jnp.float32
VMEM = pl.BlockSpec(memory_space=pltpu.VMEM)
SMEM = pl.BlockSpec(memory_space=pltpu.SMEM)


def call(kernel, ins, outs, scratch=(), flops=0, vmem=24 << 20):
    moved = sum(x.size * x.dtype.itemsize for x in ins) + sum(
        o.size * o.dtype.itemsize for o in outs
    )
    specs = [SMEM if x.ndim == 1 else VMEM for x in ins]
    return pl.pallas_call(
        kernel,
        out_shape=list(outs),
        in_specs=specs,
        out_specs=[VMEM] * len(outs),
        scratch_shapes=list(scratch),
        compiler_params=pltpu.CompilerParams(vmem_limit_bytes=vmem),
        cost_estimate=pl.CostEstimate(flops=flops, bytes_accessed=moved, transcendentals=0),
    )(*ins)


def shape(dims, dtype):
    return jax.ShapeDtypeStruct(dims, dtype)


def nt(a, b):
    return lax.dot_general(a, b, (((1,), (1,)), ((), ())), preferred_element_type=F32)


def nn(a, b):
    return jnp.dot(a, b, preferred_element_type=F32)


def pack_kernel(owners, cap, wide, high, where, state, cot, dest, rate, *outs):
    chunks, up, down = outs[:owners], outs[owners], outs[owners + 1]
    count, feats = state.shape
    named = lax.broadcasted_iota(jnp.int32, (max(8, owners), count), 0) == dest[...]
    earlier = lax.broadcasted_iota(jnp.int32, (count, count), 0) < lax.broadcasted_iota(
        jnp.int32, (count, count), 1
    )
    ranks = nn(named.astype(F32).astype(BF16), earlier.astype(F32).astype(BF16))
    slot = jnp.sum(jnp.where(named, ranks, 0.0), axis=0, keepdims=True).astype(jnp.int32)
    place = (dest[...] ^ where[0]) * cap + slot
    cols = state[...].astype(BF16)
    cots = cot[...]
    for k in range(owners):
        rows = lax.broadcasted_iota(jnp.int32, (cap, count), 0) + k * cap
        placing = (rows == place).astype(F32).astype(BF16)
        chunks[k][:, :feats] = nn(placing, cols).astype(BF16)
        chunks[k][:, feats:] = nn(placing, cots).astype(BF16)
    strip = STEPS * wide
    for out, start in ((up, 0), (down, count - strip)):
        out[:, :feats] = state[start : start + strip].astype(BF16)
        out[:, feats:] = jnp.broadcast_to(rate[start : start + strip], (strip, 128)).astype(BF16)


def edge_kernel(wide, high, state, rate, above, below, dest, where, left, right, places):
    feats = state.shape[1]
    span = high + 2 * STEPS
    half = span // 2
    low = lax.broadcasted_iota(jnp.int32, (8, feats + 128), 0) < STEPS
    tiles = []
    for r in range(span):
        if r < high:
            first = [
                jnp.concatenate(
                    [
                        state[r * wide + c : r * wide + c + 8],
                        jnp.broadcast_to(rate[r * wide + c : r * wide + c + 8], (8, 128)),
                    ],
                    axis=1,
                )
                for c in (0, wide - 8)
            ]
        else:
            ref, at = (below, r - high) if r < high + STEPS else (above, r - high - STEPS)
            both = ref[at * wide : (at + 1) * wide].astype(F32)
            first = [both[:8], both[wide - 8 :]]
        tiles.append(jnp.where(low, first[0], first[1]))
    lefts, rights = [], []
    for i in range(half):
        turned = pltpu.roll(tiles[i + half], STEPS, 0)
        lefts.append(jnp.where(low, tiles[i], turned))
        rights.append(jnp.where(low, turned, tiles[i]))
    for i in range(0, half, 2):
        left[i * 8 : i * 8 + 16] = jnp.concatenate(lefts[i : i + 2], axis=0).astype(BF16)
        right[i * 8 : i * 8 + 16] = jnp.concatenate(rights[i : i + 2], axis=0).astype(BF16)
    count = state.shape[0]
    lanes = 128
    named = lax.broadcasted_iota(jnp.int32, (count, lanes), 1) == dest[...]
    earlier = lax.broadcasted_iota(jnp.int32, (count, count), 1) < lax.broadcasted_iota(
        jnp.int32, (count, count), 0
    )
    ranks = nn(earlier.astype(F32).astype(BF16), named.astype(F32).astype(BF16))
    slot = jnp.sum(jnp.where(named, ranks, 0.0), axis=1, keepdims=True).astype(jnp.int32)
    owners_cap = places.shape[1]
    place = (dest[...] ^ where[0]) * where[1] + slot
    hits = lax.broadcasted_iota(jnp.int32, (count, owners_cap), 1) == place
    places[...] = hits.astype(F32).astype(BF16)


def flow_kernel(wide, high, state, rate, above, below, lefts, rights, out, grid, rates):
    feats = state.shape[1]
    span, across = high + 2 * STEPS, wide + 2 * STEPS
    half = span // 2
    low = lax.broadcasted_iota(jnp.int32, (8, feats + 128), 0) < STEPS
    for i in range(half):
        from_right = rights[i * 8 : i * 8 + 8].astype(F32)
        from_left = lefts[i * 8 : i * 8 + 8].astype(F32)
        near = jnp.where(low, from_right, from_left)
        far = pltpu.roll(jnp.where(low, from_left, from_right), STEPS, 0)
        for r, tile in ((i, near), (i + half, far)):
            grid[0, r, wide:] = tile[:, :feats]
            rates[r, wide:] = tile[:, feats:]
    for r in range(high):
        grid[0, r, :wide] = state[r * wide : (r + 1) * wide]
        rates[r, :wide] = jnp.broadcast_to(rate[r * wide : (r + 1) * wide], (wide, 128))
    for at in range(STEPS):
        for ref, start in ((below, high), (above, high + STEPS)):
            strip = ref[at * wide : (at + 1) * wide].astype(F32)
            grid[0, start + at, :wide] = strip[:, :feats]
            rates[start + at, :wide] = strip[:, feats:]
    for step in range(STEPS):
        now, later = step % 2, (step + 1) % 2
        margin = STEPS - 1 - step
        for r in [r % span for r in range(-margin, high + margin)]:
            here = grid[now, r]
            beside = (
                grid[now, (r - 1) % span]
                + grid[now, (r + 1) % span]
                + pltpu.roll(here, 1, 0)
                + pltpu.roll(here, across - 1, 0)
            )
            amount = rates[r]
            amount = jnp.concatenate([amount] * (feats // 128), axis=1)
            here = here + amount * (beside - 4.0 * here)
            if step == STEPS - 1:
                out[r * wide : (r + 1) * wide] = here[:wide]
            else:
                grid[later, r] = here


def physics_kernel(chunk, w_in, w_out, back, act_out, dpre_out):
    feats, hidden = w_in.shape
    cols = chunk[:, :feats]
    dtend = (0.5 * chunk[:, feats:].astype(F32)).astype(BF16)
    tend = adjoint = None
    piece = 256
    for h in range(0, hidden, piece):
        win, wout = w_in[:, h : h + piece], w_out[:, h : h + piece]
        pre = nn(cols, win)
        dact = nn(dtend, wout)
        sigma = 1.0 / (1.0 + jnp.exp(-pre))
        act = (pre * sigma).astype(BF16)
        dpre = (dact * (sigma * (1.0 + pre * (1.0 - sigma)))).astype(BF16)
        act_out[:, h : h + piece] = act
        dpre_out[:, h : h + piece] = dpre
        tend_h, adj_h = nt(act, wout), nt(dpre, win)
        tend = tend_h if tend is None else tend + tend_h
        adjoint = adj_h if adjoint is None else adjoint + adj_h
    back[:, :feats] = tend.astype(BF16)
    back[:, feats:] = adjoint.astype(BF16)


def grads_of(chunks, acts, dpres, h, piece, feats):
    dpre = jnp.concatenate([d[:, h : h + piece] for d in dpres], axis=0)
    act = jnp.concatenate([a[:, h : h + piece] for a in acts], axis=0)
    return dpre, act


def grads_kernel(owners, where, *refs):
    chunks, acts, dpres = refs[:owners], refs[owners : 2 * owners], refs[2 * owners : 3 * owners]
    keep, send = refs[3 * owners :]
    feats = chunks[0].shape[1] // 2
    hidden = acts[0].shape[1]
    block = keep.shape[2]
    cols = jnp.concatenate([c[:, :feats] for c in chunks], axis=0).T
    cots = jnp.concatenate([c[:, feats:] for c in chunks], axis=0)
    dtend = (0.5 * cots.astype(F32)).astype(BF16).T
    core = where[2]
    piece = 256
    for h in range(0, hidden, piece):
        dpre, act = grads_of(chunks, acts, dpres, h, piece, feats)
        for which, total in ((0, nn(cols, dpre)), (1, nn(dtend, act))):
            for x in range(2):
                one = total[2 * x * block : (2 * x + 1) * block]
                two = total[(2 * x + 1) * block : (2 * x + 2) * block]
                keep[which, x, :, h : h + piece] = jnp.where(core == 0, one, two)
                send[which, x, :, h : h + piece] = jnp.where(core == 0, two, one).astype(BF16)


def whole_grads_kernel(owners, *refs):
    chunks, acts, dpres = refs[:owners], refs[owners : 2 * owners], refs[2 * owners : 3 * owners]
    out = refs[3 * owners]
    feats = chunks[0].shape[1] // 2
    cols = jnp.concatenate([c[:, :feats] for c in chunks], axis=0).T
    cots = jnp.concatenate([c[:, feats:] for c in chunks], axis=0)
    dtend = (0.5 * cots.astype(F32)).astype(BF16).T
    piece = 256
    for h in range(0, acts[0].shape[1], piece):
        dpre, act = grads_of(chunks, acts, dpres, h, piece, feats)
        out[:feats, h : h + piece] = nn(cols, dpre)
        out[feats:, h : h + piece] = nn(dtend, act)


def share_kernel(where, keep, got, mine, *sends):
    y, x = where[3], where[4]
    mine[...] = keep[y, x] + got[y, x].astype(F32)
    for send, (dy, dx) in zip(sends, ((0, 1), (1, 0), (1, 1))):
        send[...] = (keep[y ^ dy, x ^ dx] + got[y ^ dy, x ^ dx].astype(F32)).astype(BF16)


def gather_kernel(mine, one, two, three, out):
    rows, hidden = mine.shape
    for j in range(hidden // 128):
        at = slice(j * 128, (j + 1) * 128)
        total = mine[:, at] + one[:, at].astype(F32) + (two[:, at].astype(F32) + three[:, at].astype(F32))
        out[pl.ds(j, rows, stride=hidden // 128), :] = total


def finish_kernel(owners, field, places, *refs):
    backs, new_state, column_adjoint = refs[:owners], refs[owners], refs[owners + 1]
    feats = field.shape[1]
    cap = backs[0].shape[0]
    rows = nn(places[...], jnp.concatenate([b[...] for b in backs], axis=0))
    new_state[...] = field[...] + 0.5 * rows[:, :feats]
    column_adjoint[...] = rows[:, feats:].astype(BF16)


def ring(axis, step):
    count = lax.axis_size(axis)
    return [(i, (i + step) % count) for i in range(count)]


def swap(axis, bit):
    return [(i, i ^ bit) for i in range(lax.axis_size(axis))]


def local(state, rate, cotangent, dest, w_in, w_out):
    high, wide, feats = state.shape
    count = high * wide
    owners = lax.axis_size("grp")
    cap = 2 * count // owners
    hidden = w_in.shape[2]
    grp, row, core = lax.axis_index("grp"), lax.axis_index("row"), lax.axis_index("col")
    where = jnp.stack([grp, jnp.int32(cap), core, row // 2, row % 2]).astype(jnp.int32)
    flat_state = state.reshape(count, feats)
    flat_cot = cotangent.reshape(count, feats)
    rate_col = rate.reshape(count, 1)
    dest_col = dest.reshape(count, 1)
    weight_in, weight_out = w_in[0], w_out[0]

    strip = shape((STEPS * wide, feats + 128), BF16)
    *chunks, up, down = call(
        functools.partial(pack_kernel, owners, cap, wide, high),
        [where, flat_state, flat_cot, dest.reshape(1, count), rate_col],
        [shape((cap, 2 * feats), BF16)] * owners + [strip, strip],
        flops=2 * owners * cap * count * 2 * feats,
    )
    got = [chunks[0]] + [None] * (owners - 1)
    for k in range(owners - 1, 0, -1):
        got[k] = lax.ppermute(chunks[k], "grp", swap("grp", k))
    above = lax.ppermute(down, "row", ring("row", 1))
    below = lax.ppermute(up, "row", ring("row", -1))

    backs, acts, dpres = [None] * owners, [None] * owners, [None] * owners

    def physics(k):
        backs[k], acts[k], dpres[k] = call(
            physics_kernel,
            [got[k], weight_in, weight_out],
            [
                shape((cap, 2 * feats), BF16),
                shape((cap, hidden), BF16),
                shape((cap, hidden), BF16),
            ],
            flops=8 * cap * feats * hidden,
        )
        if k > 0:
            backs[k] = lax.ppermute(backs[k], "grp", swap("grp", k))

    physics(0)
    side = shape(((high + 2 * STEPS) * STEPS, feats + 128), BF16)
    to_left, to_right, places = call(
        functools.partial(edge_kernel, wide, high),
        [flat_state, rate_col, above, below, dest_col, where],
        [side, side, shape((count, owners * cap), BF16)],
        flops=2 * count * count * 128,
    )
    from_left = lax.ppermute(to_right, ("grp", "col"), ring(("grp", "col"), 1))
    from_right = lax.ppermute(to_left, ("grp", "col"), ring(("grp", "col"), -1))
    for k in range(1, owners):
        physics(k)
    (field,) = call(
        functools.partial(flow_kernel, wide, high),
        [flat_state, rate_col, above, below, from_left, from_right],
        [shape((count, feats), F32)],
        [
            pltpu.VMEM((2, high + 2 * STEPS, wide + 2 * STEPS, feats), F32),
            pltpu.VMEM((high + 2 * STEPS, wide + 2 * STEPS, 128), F32),
        ],
        flops=40 * count * feats,
    )

    parts = lax.axis_size("row") * lax.axis_size("col")
    block = 2 * feats // parts
    grad_flops = 4 * owners * cap * feats * hidden
    if lax.axis_size("row") == 4 and lax.axis_size("col") == 2:
        keep, send = call(
            functools.partial(grads_kernel, owners),
            [where, *got, *acts, *dpres],
            [shape((2, 2, block, hidden), F32), shape((2, 2, block, hidden), BF16)],
            flops=grad_flops,
        )
        arrived = lax.ppermute(send, "col", swap("col", 1))
        mine, *shares = call(
            share_kernel,
            [where, keep, arrived],
            [shape((block, hidden), F32)] + [shape((block, hidden), BF16)] * 3,
        )
        shares = [lax.ppermute(s, "row", swap("row", bit + 1)) for bit, s in enumerate(shares)]
        (summed,) = call(
            gather_kernel, [mine, *shares], [shape((block * hidden // 128, 128), F32)]
        )
    else:
        (flat,) = call(
            functools.partial(whole_grads_kernel, owners),
            [*got, *acts, *dpres],
            [shape((2 * feats, hidden), F32)],
            flops=grad_flops,
        )
        summed = lax.psum_scatter(
            flat.reshape(-1, 128), ("row", "col"), scatter_dimension=0, tiled=True
        )
    new_state, column_adjoint = call(
        functools.partial(finish_kernel, owners),
        [field, places, *backs],
        [shape((count, feats), F32), shape((count, feats), BF16)],
        flops=4 * count * owners * cap * feats,
    )
    return (
        new_state.reshape(state.shape),
        column_adjoint.reshape(state.shape),
        summed[None],
    )


def solution(mesh):
    in_specs = (
        P("row", ("grp", "col"), None),
        P("row", ("grp", "col")),
        P("row", ("grp", "col"), None),
        P("row", ("grp", "col"), None, None),
        P("grp", None, None),
        P("grp", None, None),
    )
    out_specs = (
        P("row", ("grp", "col"), None),
        P("row", ("grp", "col"), None),
        P("grp", ("row", "col"), None),
    )
    return jax.shard_map(local, mesh=mesh, in_specs=in_specs, out_specs=out_specs, check_vma=False)
```

time: 100 us -> 50.9 us (0.51)
  waiting for transfers between devices: 31.2 us -> 15.7 us
  starting transfers between devices: 32.5 us -> 18.9 us
  between operations: 14.3 us -> 0.79 us
  Pallas kernels: 0 us -> 10.5 us
  matrix products: 8.01 us -> 0 us
  other arithmetic: 7.25 us -> 0 us
  local copies, waits for them, and re-layouts: 6.41 us -> 4.65 us
    all_to_all x4 -> x0, starting transfers between devices: 14.1 us -> none  [the longest x1 3.83 us: local(): lax.all_to_all(packed_cots.reshape(owners, capacity, feats), 'grp', split...]
    all_to_all x4 -> x0, waiting for transfers between devices: 12.3 us -> none  [the longest x1 4.44 us: local(): lax.all_to_all(packed_cols.reshape(owners, capacity, feats), 'grp', split...]
    pallas_call x0 -> x11, Pallas kernels: none -> 10.5 us  [call(): pl.pallas_call(kernel, out_shape=list(outs), in_specs=specs, out_specs=[V...]
    dot_general x8 -> x0, matrix products: 8.01 us -> none  [the longest x1 2 us: local(): pre = jnp.dot(owner_cols, weight_in, preferred_element_type=jnp.float32)]
    reduce_scatter x1 -> x0, waiting for transfers between devices: 3.38 us -> none  [local(): lax.psum_scatter(flat, ('row', 'col'), scatter_dimension=0, tiled=True)]
    convert_element_type x10 -> x0, other arithmetic: 2.47 us -> none  [the longest x4 1.42 us: local(): field.astype(jnp.bfloat16)]
    gather x2 -> x0, local copies, waits for them, and re-layouts: 2.3 us -> none  [the longest x1 1.15 us: local(): jnp.take(back_tend.reshape(owners * capacity, feats), places, axis=0)]
    another operation x3 -> x0, other arithmetic: 1.48 us -> none
  transfers between devices with their start and end apart: 21 -> 14, of which waited for: 13 -> 6; matrix products, arithmetic and copies ran while one was open for 18% -> 0% of each run, Pallas kernels for 0% -> 12%
where the time goes in v1:
time: 50.9 us; the launch traced here: 50.6 us
  starting transfers between devices  18.9 us (37%)
  waiting for transfers between devices  15.7 us (31%)
  Pallas kernels  10.5 us (21%)
  local copies, waits for them, and re-layouts  4.65 us (9%)
  between operations  0.79 us (2%)
    pallas_call x11, Pallas kernels, call(): pl.pallas_call(kernel, out_shape=list(outs), in_specs=specs, out_specs=[V...  10.5 us
    ppermute x3, waiting for transfers between devices, local(): got[k] = lax.ppermute(chunks[k], 'grp', swap('grp', k))  7.5 us
    ppermute x3, starting transfers between devices, local(): got[k] = lax.ppermute(chunks[k], 'grp', swap('grp', k))  5.62 us
    ppermute x3, waiting for transfers between devices, physics(): backs[k] = lax.ppermute(backs[k], 'grp', swap('grp', k))  5.19 us
    ppermute x3, starting transfers between devices, local(): lax.ppermute(s, 'row', swap('row', bit + 1))  4.08 us
    unnamed x14, local copies, waits for them, and re-layouts  3.59 us
    ppermute x1, starting transfers between devices, local(): from_right = lax.ppermute(to_left, ('grp', 'col'), ring(('grp', 'col'), -1))  3.53 us
    ppermute x3, starting transfers between devices, physics(): backs[k] = lax.ppermute(backs[k], 'grp', swap('grp', k))  2.66 us
  transfers between devices with their start and end apart: 14, of which 6 were waited for; matrix products, arithmetic and copies ran while one was open for 0% of the time, Pallas kernels for 12%

profile of v1, /device:TPU:0, one launch (start us, length us, event | category | flops | bytes accessed | tf_op | source)
XLA Modules:
  0.0 50.6 jit_solution(10910392809044480558)
XLA Ops:
  0.6 0.0 copy-start
  0.7 0.8 %reshape.34.rate = f32[256,1]{1,0:T(8,128)S(1)} reshape(f32[16,16]{1,0:T(8,128)} %param.7) | data formatting | bytes 2048 | tf_op jit(solution)/shard_map/reshape | solution.py:260
  1.5 0.1 stack.19.where
  1.6 0.0 copy-start.2
  1.6 0.9 %copy-done.2 = f32[16,16,256]{2,1,0:T(8,128)S(1)} copy-done((f32[16,16,256]{2,1,0:T(8,128)S(1)}, f32[16,16,256]{2,1,0:T(8,128)}, u32[]{:S(2)}) %copy-start.2) | copy-done | bytes 262168
  2.6 0.0 copy-start.4
  2.6 0.9 %copy-done.4 = bf16[16,16,256]{2,1,0:T(8,128)(2,1)S(1)} copy-done((bf16[16,16,256]{2,1,0:T(8,128)(2,1)S(1)}, bf16[16,16,256]{2,1,0:T(8,128)(2,1)}, u32[]{:S(2)}) %copy-start.4) | copy-done | bytes 131096
  3.5 0.0 copy-start.5
  3.5 0.7 %copy-done.5 = s32[1,1,256,1]{2,3,1,0:T(1,128)S(1)} copy-done((s32[1,1,256,1]{2,3,1,0:T(1,128)S(1)}, s32[1,1,256,1]{2,3,1,0:T(1,128)}, u32[]{:S(2)}) %copy-start.5) | copy-done | bytes 1048
  4.2 1.6 %shard_map.85 = (bf16[128,512]{1,0:T(8,128)(2,1)S(1)}, bf16[128,512]{1,0:T(8,128)(2,1)S(1)}, bf16[128,512]{1,0:T(8,128)(2,1)S(1)}, bf16[128,512]{1,0:T(8,128)(2,...) custom-call(s32[5]{0:T(128)S(1)} %stack.19.where, f32[256,256]{1,0:T(8,128)S(1)} %bitcast.21, ...), custom_call_target="tpu_custom_call" | custom-call | flops 134217728 | bytes 1017876 | tf_op jit(solution)/shard_map/pallas_call | solution.py:22
  5.7 3.0 %collective-permute-start.4 = (bf16[128,512]{1,0:T(8,128)(2,1)S(1)}, bf16[128,512]{1,0:T(8,128)(2,1)S(1)}, u32[]{:S(2)}, u32[]{:S(2)}) collective-permute-start(bf16[128,512]{1,0:T(8,128)(2,1)S(1)} %get-tuple-element.39), channel_id=1, source_target_pairs={{0,2},{2,0},{4,6},{6,4},{1,3},{3,1},{5,7},{7,5},{8,10},{10,8},{12,... | collective-permute-start | bytes 393224 | tf_op jit(solution)/shard_map/ppermute | solution.py:273
  8.7 2.6 %collective-permute-start.6 = (bf16[128,512]{1,0:T(8,128)(2,1)S(1)}, bf16[128,512]{1,0:T(8,128)(2,1)S(1)}, u32[]{:S(2)}, u32[]{:S(2)}) collective-permute-start(bf16[128,512]{1,0:T(8,128)(2,1)S(1)} %get-tuple-element.41), channel_id=1, source_target_pairs={{0,4},{2,6},{4,0},{6,2},{1,5},{3,7},{5,1},{7,3},{8,12},{10,14},{12... | collective-permute-start | bytes 393224 | tf_op jit(solution)/shard_map/ppermute | solution.py:273
  11.3 0.0 collective-permute-start.8
  11.3 0.0 copy-done
  11.3 0.0 copy-start.1
  11.3 1.0 %copy-done.1 = bf16[1,256,1024]{2,1,0:T(8,128)(2,1)S(1)} copy-done((bf16[1,256,1024]{2,1,0:T(8,128)(2,1)S(1)}, bf16[1,256,1024]{2,1,0:T(8,128)(2,1)}, u32[]{:S(2)}) %copy-start.1) | copy-done | bytes 524312
  12.4 0.9 %shard_map.88 = (bf16[128,512]{1,0:T(8,128)(2,1)S(1)}, bf16[128,1024]{1,0:T(8,128)(2,1)S(1)}, bf16[128,1024]{1,0:T(8,128)(2,1)S(1)}) custom-call(bf16[128,512]{1,0:T(8,128)(2,1)S(1)} %get-tuple-element.37.chunk.refs_0_, bf16[256,1024]{1,0:T(8,128)(2,1)S(1)} %bitcast.13, bf16[256,1024]{1,0:T(8,128)(2,1)S(1)} %bitcast.17), custom_call_target="tpu_custom_call" | custom-call | flops 268435456 | bytes 1835008 | tf_op jit(solution)/shard_map/pallas_call | solution.py:22
  13.3 0.5 collective-permute-done.4.chunk.refs_1_
  13.8 0.9 %shard_map.89 = (bf16[128,512]{1,0:T(8,128)(2,1)S(1)}, bf16[128,1024]{1,0:T(8,128)(2,1)S(1)}, bf16[128,1024]{1,0:T(8,128)(2,1)S(1)}) custom-call(bf16[128,512]{1,0:T(8,128)(2,1)S(1)} %collective-permute-done.4.chunk.refs_1_, bf16[256,1024]{1,0:T(8,128)(2,1)S(1)} %bitcast.14, bf16[256,1024]{1,0:T(8,128)(2,1)S(1)} %bitcast.18), custom_call_target="tpu_custom_call" | custom-call | flops 268435456 | bytes 1835008 | tf_op jit(solution)/shard_map/pallas_call | solution.py:22
  14.7 7.0 %collective-permute-done.6.chunk.refs_2_ = bf16[128,512]{1,0:T(8,128)(2,1)S(1)} collective-permute-done((bf16[128,512]{1,0:T(8,128)(2,1)S(1)}, bf16[128,512]{1,0:T(8,128)(2,1)S(1)}, u32[]{:S(2)}, u32[]{:S(2)}) %collective-permute-start.6) | collective-permute-done | bytes 131104 | tf_op jit(solution)/shard_map/ppermute | solution.py:273
  21.7 0.9 %shard_map.90 = (bf16[128,512]{1,0:T(8,128)(2,1)S(1)}, bf16[128,1024]{1,0:T(8,128)(2,1)S(1)}, bf16[128,1024]{1,0:T(8,128)(2,1)S(1)}) custom-call(bf16[128,512]{1,0:T(8,128)(2,1)S(1)} %collective-permute-done.6.chunk.refs_2_, bf16[256,1024]{1,0:T(8,128)(2,1)S(1)} %bitcast.15, bf16[256,1024]{1,0:T(8,128)(2,1)S(1)} %bitcast.19), custom_call_target="tpu_custom_call" | custom-call | flops 268435456 | bytes 1835008 | tf_op jit(solution)/shard_map/pallas_call | solution.py:22
  22.6 0.0 collective-permute-done.8.chunk.refs_3_
  22.6 0.9 %shard_map.91 = (bf16[128,512]{1,0:T(8,128)(2,1)S(1)}, bf16[128,1024]{1,0:T(8,128)(2,1)S(1)}, bf16[128,1024]{1,0:T(8,128)(2,1)S(1)}) custom-call(bf16[128,512]{1,0:T(8,128)(2,1)S(1)} %collective-permute-done.8.chunk.refs_3_, bf16[256,1024]{1,0:T(8,128)(2,1)S(1)} %bitcast.16, bf16[256,1024]{1,0:T(8,128)(2,1)S(1)} %bitcast.20), custom_call_target="tpu_custom_call" | custom-call | flops 268435456 | bytes 1835008 | tf_op jit(solution)/shard_map/pallas_call | solution.py:22
  23.5 0.0 copy-start.3
  23.5 1.3 %shard_map.93 = (f32[2,2,64,1024]{3,2,1,0:T(8,128)S(1)}, bf16[2,2,64,1024]{3,2,1,0:T(8,128)(2,1)S(1)}) custom-call(s32[5]{0:T(128)S(1)} %stack.19.where, bf16[128,512]{1,0:T(8,128)(2,1)S(1)} %get-tuple-element.37.chunk.refs_0_, bf16[128,512]{1,0:T(8,128)(2,1)S(1)} %collective-permute-done.4.chunk.refs_1_, ...), custom_call_target="tpu_custom_call" | custom-call | flops 536870912 | bytes 4194324 | tf_op jit(solution)/shard_map/pallas_call | solution.py:22
  24.8 0.1 collective-permute-start.10
  24.9 1.1 %collective-permute-start.5 = (bf16[128,512]{1,0:T(8,128)(2,1)S(1)}, bf16[128,512]{1,0:T(8,128)(2,1)S(1)}, u32[]{:S(2)}, u32[]{:S(2)}) collective-permute-start(bf16[128,512]{1,0:T(8,128)(2,1)S(1)} %get-tuple-element.40), channel_id=1, source_target_pairs={{0,2},{2,0},{4,6},{6,4},{1,3},{3,1},{5,7},{7,5},{8,10},{10,8},{12,... | collective-permute-start | bytes 393224 | tf_op jit(solution)/shard_map/ppermute | solution.py:291
  26.0 1.5 %collective-permute-start = (bf16[64,384]{1,0:T(8,128)(2,1)}, bf16[64,384]{1,0:T(8,128)(2,1)S(1)}, u32[]{:S(2)}, u32[]{:S(2)}) collective-permute-start(bf16[64,384]{1,0:T(8,128)(2,1)} %get-tuple-element.32), channel_id=1, source_target_pairs={{0,8},{8,16},{16,24},{24,0},{1,9},{9,17},{17,25},{25,1},{2,10},{10... | collective-permute-start | bytes 147464 | tf_op jit(solution)/shard_map/ppermute | solution.py:274
  27.5 0.0 copy-start.6
  27.5 1.4 %collective-permute-start.1 = (bf16[64,384]{1,0:T(8,128)(2,1)}, bf16[64,384]{1,0:T(8,128)(2,1)S(1)}, u32[]{:S(2)}, u32[]{:S(2)}) collective-permute-start(bf16[64,384]{1,0:T(8,128)(2,1)} %get-tuple-element.33), channel_id=1, source_target_pairs={{0,24},{8,0},{16,8},{24,16},{1,25},{9,1},{17,9},{25,17},{2,26},{10... | collective-permute-start | bytes 147464 | tf_op jit(solution)/shard_map/ppermute | solution.py:275
  28.9 0.0 copy-done.6
  29.0 0.1 copy.11.dest
  29.1 2.3 %collective-permute-done.above = bf16[64,384]{1,0:T(8,128)(2,1)S(1)} collective-permute-done((bf16[64,384]{1,0:T(8,128)(2,1)}, bf16[64,384]{1,0:T(8,128)(2,1)S(1)}, u32[]{:S(2)}, u32[]{:S(2)}) %collective-permute-start) | collective-permute-done | bytes 49184 | tf_op jit(solution)/shard_map/ppermute | solution.py:274
  31.4 0.7 %collective-permute-done.1.below = bf16[64,384]{1,0:T(8,128)(2,1)S(1)} collective-permute-done((bf16[64,384]{1,0:T(8,128)(2,1)}, bf16[64,384]{1,0:T(8,128)(2,1)S(1)}, u32[]{:S(2)}, u32[]{:S(2)}) %collective-permute-start.1) | collective-permute-done | bytes 49184 | tf_op jit(solution)/shard_map/ppermute | solution.py:275
  32.1 0.0 copy-done.3
  32.1 1.0 %shard_map.86 = (bf16[96,384]{1,0:T(8,128)(2,1)S(1)}, bf16[96,384]{1,0:T(8,128)(2,1)S(1)}, bf16[256,512]{1,0:T(8,128)(2,1)S(1)}) custom-call(f32[256,256]{1,0:T(8,128)S(1)} %bitcast.22, f32[256,1]{1,0:T(8,128)S(1)} %reshape.34.rate, bf16[64,384]{1,0:T(8,128)(2,1)S(1)} %collective-permute-done.above, bf16[64,384]{1,0:T(8,128)(2,1)S(1)} %collective-permute-done.1.below, ...), custom_call_target="tpu_custom_call" | custom-call | flops 16777216 | bytes 772116 | tf_op jit(solution)/shard_map/pallas_call | solution.py:22
  33.0 0.1 collective-permute-start.2
  33.1 3.5 %collective-permute-start.3 = (bf16[96,384]{1,0:T(8,128)(2,1)S(1)}, bf16[96,384]{1,0:T(8,128)(2,1)S(1)}, u32[]{:S(2)}, u32[]{:S(2)}) collective-permute-start(bf16[96,384]{1,0:T(8,128)(2,1)S(1)} %get-tuple-element.35), channel_id=1, source_target_pairs={{0,7},{1,0},{2,1},{3,2},{4,3},{5,4},{6,5},{7,6},{8,15},{9,8},{10,9... | collective-permute-start | bytes 221192 | tf_op jit(solution)/shard_map/ppermute | solution.py:302
  36.6 0.0 collective-permute-start.7
  36.6 0.0 collective-permute-done.10.got
  36.6 1.5 %collective-permute-start.9 = (bf16[128,512]{1,0:T(8,128)(2,1)S(1)}, bf16[128,512]{1,0:T(8,128)(2,1)S(1)}, u32[]{:S(2)}, u32[]{:S(2)}) collective-permute-start(bf16[128,512]{1,0:T(8,128)(2,1)S(1)} %get-tuple-element.44), channel_id=1, source_target_pairs={{0,6},{2,4},{4,2},{6,0},{1,7},{3,5},{5,3},{7,1},{8,14},{10,12},{12... | collective-permute-start | bytes 393224 | tf_op jit(solution)/shard_map/ppermute | solution.py:291
  38.2 0.6 %shard_map.94 = (f32[64,1024]{1,0:T(8,128)S(1)}, bf16[64,1024]{1,0:T(8,128)(2,1)S(1)}, bf16[64,1024]{1,0:T(8,128)(2,1)S(1)}, bf16[64,1024]{1,0:T(8,128)(2,1)S(1)}) custom-call(s32[5]{0:T(128)S(1)} %stack.19.where, f32[2,2,64,1024]{3,2,1,0:T(8,128)S(1)} %get-tuple-element.55.keep, bf16[2,2,64,1024]{3,2,1,0:T(8,128)(2,1)S(1)} %collective-permute-done.10.got), custom_call_target="tpu_custom_call" | custom-call | bytes 2228244 | tf_op jit(solution)/shard_map/pallas_call | solution.py:22
  38.8 0.1 collective-permute-done.2.lefts
  38.9 2.2 %collective-permute-start.11 = (bf16[64,1024]{1,0:T(8,128)(2,1)S(1)}, bf16[64,1024]{1,0:T(8,128)(2,1)S(1)}, u32[]{:S(2)}, u32[]{:S(2)}) collective-permute-start(bf16[64,1024]{1,0:T(8,128)(2,1)S(1)} %get-tuple-element.58), channel_id=1, source_target_pairs={{0,8},{8,0},{16,24},{24,16},{1,9},{9,1},{17,25},{25,17},{2,10},{10... | collective-permute-start | bytes 393224 | tf_op jit(solution)/shard_map/ppermute | solution.py:332
  41.0 0.0 collective-permute-done.3.rights
  41.0 0.5 collective-permute-start.12
  41.5 0.0 collective-permute-done.5.refs_1_
  41.5 1.4 %collective-permute-start.13 = (bf16[64,1024]{1,0:T(8,128)(2,1)S(1)}, bf16[64,1024]{1,0:T(8,128)(2,1)S(1)}, u32[]{:S(2)}, u32[]{:S(2)}) collective-permute-start(bf16[64,1024]{1,0:T(8,128)(2,1)S(1)} %get-tuple-element.60), channel_id=1, source_target_pairs={{0,24},{8,16},{16,8},{24,0},{1,25},{9,17},{17,9},{25,1},{2,26},{10... | collective-permute-start | bytes 393224 | tf_op jit(solution)/shard_map/ppermute | solution.py:332
  42.9 0.7 %shard_map.87.field = f32[256,256]{1,0:T(8,128)S(1)} custom-call(f32[256,256]{1,0:T(8,128)S(1)} %bitcast.23, f32[256,1]{1,0:T(8,128)S(1)} %reshape.34.rate, bf16[64,384]{1,0:T(8,128)(2,1)S(1)} %collective-permute-done.above, bf16[64,384]{1,0:T(8,128)(2,1)S(1)} %collective-permute-done.1.below, bf16[96,384]{1,0:T(8,128)(2,1)S(1)} %collective-permute-done.2.lefts, ...), custom_call_target="tpu_custom_call" | custom-call | flops 2621440 | bytes 771072 | tf_op jit(solution)/shard_map/pallas_call | solution.py:22
  43.6 5.2 %collective-permute-done.7.refs_2_ = bf16[128,512]{1,0:T(8,128)(2,1)S(1)} collective-permute-done((bf16[128,512]{1,0:T(8,128)(2,1)S(1)}, bf16[128,512]{1,0:T(8,128)(2,1)S(1)}, u32[]{:S(2)}, u32[]{:S(2)}) %collective-permute-start.7) | collective-permute-done | bytes 131104 | tf_op jit(solution)/shard_map/ppermute | solution.py:291
  48.8 0.0 collective-permute-done.9.refs_3_
  48.8 1.1 %shard_map.92 = (f32[256,256]{1,0:T(8,128)}, bf16[256,256]{1,0:T(8,128)(2,1)}) custom-call(f32[256,256]{1,0:T(8,128)S(1)} %shard_map.87.field, bf16[256,512]{1,0:T(8,128)(2,1)S(1)} %get-tuple-element.36.places, bf16[128,512]{1,0:T(8,128)(2,1)S(1)} %get-tuple-element.38.refs_0_, bf16[128,512]{1,0:T(8,128)(2,1)S(1)} %collective-permute-done.5.refs_1_, ...), custom_call_target="tpu_custom_call" | custom-call | flops 134217728 | bytes 1441792 | tf_op jit(solution)/shard_map/pallas_call | solution.py:22
  49.9 0.0 collective-permute-done.11.one
  49.9 0.0 collective-permute-done.12.two
  49.9 0.0 collective-permute-done.13.three
  49.9 0.8 %shard_map.95 = f32[512,128]{1,0:T(8,128)} custom-call(f32[64,1024]{1,0:T(8,128)S(1)} %get-tuple-element.57.mine, bf16[64,1024]{1,0:T(8,128)(2,1)S(1)} %collective-permute-done.11.one, bf16[64,1024]{1,0:T(8,128)(2,1)S(1)} %collective-permute-done.12.two, bf16[64,1024]{1,0:T(8,128)(2,1)S(1)} %collective-permute-done.13.three), custom_call_target="tpu_custom_call" | custom-call | bytes 917504 | tf_op jit(solution)/shard_map/pallas_call | solution.py:22
Async XLA Ops:
  0.6 10.7 %copy-start = (bf16[1,256,1024]{2,1,0:T(8,128)(2,1)S(1)}, bf16[1,256,1024]{2,1,0:T(8,128)(2,1)}, u32[]{:S(2)}) copy-start(bf16[1,256,1024]{2,1,0:T(8,128)(2,1)} %param.10) | copy-start | bytes 1572868
  1.6 1.0 %copy-start.2 = (f32[16,16,256]{2,1,0:T(8,128)S(1)}, f32[16,16,256]{2,1,0:T(8,128)}, u32[]{:S(2)}) copy-start(f32[16,16,256]{2,1,0:T(8,128)} %param.6) | copy-start | bytes 786436
  2.6 0.9 %copy-start.4 = (bf16[16,16,256]{2,1,0:T(8,128)(2,1)S(1)}, bf16[16,16,256]{2,1,0:T(8,128)(2,1)}, u32[]{:S(2)}) copy-start(bf16[16,16,256]{2,1,0:T(8,128)(2,1)} %param.8) | copy-start | bytes 393220
  3.5 0.7 %copy-start.5 = (s32[1,1,256,1]{2,3,1,0:T(1,128)S(1)}, s32[1,1,256,1]{2,3,1,0:T(1,128)}, u32[]{:S(2)}) copy-start(s32[1,1,256,1]{2,3,1,0:T(1,128)} %param.9) | copy-start | bytes 3076
  5.7 8.1 %collective-permute-start.4 = (bf16[128,512]{1,0:T(8,128)(2,1)S(1)}, bf16[128,512]{1,0:T(8,128)(2,1)S(1)}, u32[]{:S(2)}, u32[]{:S(2)}) collective-permute-start(bf16[128,512]{1,0:T(8,128)(2,1)S(1)} %get-tuple-element.39), channel_id=1, source_target_pairs={{0,2},{2,0},{4,6},{6,4},{1,3},{3,1},{5,7},{7,5},{8,10},{10,8},{12,... | collective-permute-start | bytes 393224 | tf_op jit(solution)/shard_map/ppermute | solution.py:273
  8.7 12.9 %collective-permute-start.6 = (bf16[128,512]{1,0:T(8,128)(2,1)S(1)}, bf16[128,512]{1,0:T(8,128)(2,1)S(1)}, u32[]{:S(2)}, u32[]{:S(2)}) collective-permute-start(bf16[128,512]{1,0:T(8,128)(2,1)S(1)} %get-tuple-element.41), channel_id=1, source_target_pairs={{0,4},{2,6},{4,0},{6,2},{1,5},{3,7},{5,1},{7,3},{8,12},{10,14},{12... | collective-permute-start | bytes 393224 | tf_op jit(solution)/shard_map/ppermute | solution.py:273
  11.3 11.2 %collective-permute-start.8 = (bf16[128,512]{1,0:T(8,128)(2,1)S(1)}, bf16[128,512]{1,0:T(8,128)(2,1)S(1)}, u32[]{:S(2)}, u32[]{:S(2)}) collective-permute-start(bf16[128,512]{1,0:T(8,128)(2,1)S(1)} %get-tuple-element.43), channel_id=1, source_target_pairs={{0,6},{2,4},{4,2},{6,0},{1,7},{3,5},{5,3},{7,1},{8,14},{10,12},{12... | collective-permute-start | bytes 393224 | tf_op jit(solution)/shard_map/ppermute | solution.py:273
  11.3 1.0 %copy-start.1 = (bf16[1,256,1024]{2,1,0:T(8,128)(2,1)S(1)}, bf16[1,256,1024]{2,1,0:T(8,128)(2,1)}, u32[]{:S(2)}) copy-start(bf16[1,256,1024]{2,1,0:T(8,128)(2,1)} %param.11) | copy-start | bytes 1572868
  23.5 8.6 %copy-start.3 = (f32[16,16,256]{2,1,0:T(8,128)S(1)}, f32[16,16,256]{2,1,0:T(8,128)}, u32[]{:S(2)}) copy-start(f32[16,16,256]{2,1,0:T(8,128)} %param.6) | copy-start | bytes 786436
  24.8 11.8 %collective-permute-start.10 = (bf16[2,2,64,1024]{3,2,1,0:T(8,128)(2,1)S(1)}, bf16[2,2,64,1024]{3,2,1,0:T(8,128)(2,1)S(1)}, u32[]{:S(2)}, u32[]{:S(2)}) collective-permute-start(bf16[2,2,64,1024]{3,2,1,0:T(8,128)(2,1)S(1)} %get-tuple-element.56), channel_id=1, source_target_pairs={{0,1},{1,0},{2,3},{3,2},{4,5},{5,4},{6,7},{7,6},{8,9},{9,8},{10,11... | collective-permute-start | bytes 1572872 | tf_op jit(solution)/shard_map/ppermute | solution.py:326
  24.9 16.6 %collective-permute-start.5 = (bf16[128,512]{1,0:T(8,128)(2,1)S(1)}, bf16[128,512]{1,0:T(8,128)(2,1)S(1)}, u32[]{:S(2)}, u32[]{:S(2)}) collective-permute-start(bf16[128,512]{1,0:T(8,128)(2,1)S(1)} %get-tuple-element.40), channel_id=1, source_target_pairs={{0,2},{2,0},{4,6},{6,4},{1,3},{3,1},{5,7},{7,5},{8,10},{10,8},{12,... | collective-permute-start | bytes 393224 | tf_op jit(solution)/shard_map/ppermute | solution.py:291
  26.0 5.3 %collective-permute-start = (bf16[64,384]{1,0:T(8,128)(2,1)}, bf16[64,384]{1,0:T(8,128)(2,1)S(1)}, u32[]{:S(2)}, u32[]{:S(2)}) collective-permute-start(bf16[64,384]{1,0:T(8,128)(2,1)} %get-tuple-element.32), channel_id=1, source_target_pairs={{0,8},{8,16},{16,24},{24,0},{1,9},{9,17},{17,25},{25,1},{2,10},{10... | collective-permute-start | bytes 147464 | tf_op jit(solution)/shard_map/ppermute | solution.py:274
  27.5 1.4 %copy-start.6 = (s32[1,1,256,1]{2,3,1,0:T(1,128)S(1)}, s32[1,1,256,1]{2,3,1,0:T(1,128)}, u32[]{:S(2)}) copy-start(s32[1,1,256,1]{2,3,1,0:T(1,128)} %param.9) | copy-start | bytes 3076
  27.5 4.5 %collective-permute-start.1 = (bf16[64,384]{1,0:T(8,128)(2,1)}, bf16[64,384]{1,0:T(8,128)(2,1)S(1)}, u32[]{:S(2)}, u32[]{:S(2)}) collective-permute-start(bf16[64,384]{1,0:T(8,128)(2,1)} %get-tuple-element.33), channel_id=1, source_target_pairs={{0,24},{8,0},{16,8},{24,16},{1,25},{9,1},{17,9},{25,17},{2,26},{10... | collective-permute-start | bytes 147464 | tf_op jit(solution)/shard_map/ppermute | solution.py:275
  33.0 5.8 %collective-permute-start.2 = (bf16[96,384]{1,0:T(8,128)(2,1)S(1)}, bf16[96,384]{1,0:T(8,128)(2,1)S(1)}, u32[]{:S(2)}, u32[]{:S(2)}) collective-permute-start(bf16[96,384]{1,0:T(8,128)(2,1)S(1)} %get-tuple-element.34), channel_id=1, source_target_pairs={{0,1},{1,2},{2,3},{3,4},{4,5},{5,6},{6,7},{7,0},{8,9},{9,10},{10,1... | collective-permute-start | bytes 221192 | tf_op jit(solution)/shard_map/ppermute | solution.py:301
  33.1 7.9 %collective-permute-start.3 = (bf16[96,384]{1,0:T(8,128)(2,1)S(1)}, bf16[96,384]{1,0:T(8,128)(2,1)S(1)}, u32[]{:S(2)}, u32[]{:S(2)}) collective-permute-start(bf16[96,384]{1,0:T(8,128)(2,1)S(1)} %get-tuple-element.35), channel_id=1, source_target_pairs={{0,7},{1,0},{2,1},{3,2},{4,3},{5,4},{6,5},{7,6},{8,15},{9,8},{10,9... | collective-permute-start | bytes 221192 | tf_op jit(solution)/shard_map/ppermute | solution.py:302
  36.6 12.2 %collective-permute-start.7 = (bf16[128,512]{1,0:T(8,128)(2,1)S(1)}, bf16[128,512]{1,0:T(8,128)(2,1)S(1)}, u32[]{:S(2)}, u32[]{:S(2)}) collective-permute-start(bf16[128,512]{1,0:T(8,128)(2,1)S(1)} %get-tuple-element.42), channel_id=1, source_target_pairs={{0,4},{2,6},{4,0},{6,2},{1,5},{3,7},{5,1},{7,3},{8,12},{10,14},{12... | collective-permute-start | bytes 393224 | tf_op jit(solution)/shard_map/ppermute | solution.py:291
  36.6 12.2 %collective-permute-start.9 = (bf16[128,512]{1,0:T(8,128)(2,1)S(1)}, bf16[128,512]{1,0:T(8,128)(2,1)S(1)}, u32[]{:S(2)}, u32[]{:S(2)}) collective-permute-start(bf16[128,512]{1,0:T(8,128)(2,1)S(1)} %get-tuple-element.44), channel_id=1, source_target_pairs={{0,6},{2,4},{4,2},{6,0},{1,7},{3,5},{5,3},{7,1},{8,14},{10,12},{12... | collective-permute-start | bytes 393224 | tf_op jit(solution)/shard_map/ppermute | solution.py:291
  38.9 11.0 %collective-permute-start.11 = (bf16[64,1024]{1,0:T(8,128)(2,1)S(1)}, bf16[64,1024]{1,0:T(8,128)(2,1)S(1)}, u32[]{:S(2)}, u32[]{:S(2)}) collective-permute-start(bf16[64,1024]{1,0:T(8,128)(2,1)S(1)} %get-tuple-element.58), channel_id=1, source_target_pairs={{0,8},{8,0},{16,24},{24,16},{1,9},{9,1},{17,25},{25,17},{2,10},{10... | collective-permute-start | bytes 393224 | tf_op jit(solution)/shard_map/ppermute | solution.py:332
  41.0 8.8 %collective-permute-start.12 = (bf16[64,1024]{1,0:T(8,128)(2,1)S(1)}, bf16[64,1024]{1,0:T(8,128)(2,1)S(1)}, u32[]{:S(2)}, u32[]{:S(2)}) collective-permute-start(bf16[64,1024]{1,0:T(8,128)(2,1)S(1)} %get-tuple-element.59), channel_id=1, source_target_pairs={{0,16},{8,24},{16,0},{24,8},{1,17},{9,25},{17,1},{25,9},{2,18},{10... | collective-permute-start | bytes 393224 | tf_op jit(solution)/shard_map/ppermute | solution.py:332
  41.5 8.3 %collective-permute-start.13 = (bf16[64,1024]{1,0:T(8,128)(2,1)S(1)}, bf16[64,1024]{1,0:T(8,128)(2,1)S(1)}, u32[]{:S(2)}, u32[]{:S(2)}) collective-permute-start(bf16[64,1024]{1,0:T(8,128)(2,1)S(1)} %get-tuple-element.60), channel_id=1, source_target_pairs={{0,24},{8,16},{16,8},{24,0},{1,25},{9,17},{17,9},{25,1},{2,26},{10... | collective-permute-start | bytes 393224 | tf_op jit(solution)/shard_map/ppermute | solution.py:332

commit v2 on v1

v2 whole, which is shorter than its diff:
```python
import functools

import jax
import jax.numpy as jnp
from jax import lax
from jax.experimental import pallas as pl
from jax.experimental.pallas import tpu as pltpu
from jax.sharding import PartitionSpec as P

STEPS = 4
BF16 = jnp.bfloat16
F32 = jnp.float32
VMEM = pl.BlockSpec(memory_space=pltpu.VMEM)
HBM = pl.BlockSpec(memory_space=pltpu.HBM)
ANY = pl.BlockSpec(memory_space=pl.ANY)


def call(kernel, ins, outs, scratch=(), after=(), far=(), vmem=24 << 20):
    specs = [HBM if n in far else VMEM for n in range(len(ins))]
    count = len(ins)

    def body(*refs):
        kernel(*refs[:count], *refs[count + len(after) :])

    return pl.pallas_call(
        body,
        out_shape=list(outs),
        in_specs=specs + [ANY] * len(after),
        out_specs=[VMEM] * len(outs),
        scratch_shapes=list(scratch),
        compiler_params=pltpu.CompilerParams(vmem_limit_bytes=vmem),
    )(*ins, *after)


def shape(dims, dtype):
    return jax.ShapeDtypeStruct(dims, dtype)


def nt(a, b):
    return lax.dot_general(a, b, (((1,), (1,)), ((), ())), preferred_element_type=F32)


def nn(a, b):
    return jnp.dot(a, b, preferred_element_type=F32)


def pack_kernel(owners, cap, wide, high, *refs):
    far, near, sems = refs[:4], refs[-5:-1], refs[-1]
    chunks, inner, outer, rate_cols, places = refs[4 : owners + 4], *refs[owners + 4 : -5]
    copies = [pltpu.make_async_copy(a, b, sems.at[n]) for n, (a, b) in enumerate(zip(far, near))]
    for copy in copies:
        copy.start()
    dest, rate, state, cot = near
    count, feats = state.shape
    copies[0].wait()
    named = lax.broadcasted_iota(jnp.int32, (max(8, owners), count), 0) == dest[...]
    earlier = lax.broadcasted_iota(jnp.int32, (count, count), 0) < lax.broadcasted_iota(
        jnp.int32, (count, count), 1
    )
    ranks = nn(named.astype(F32).astype(BF16), earlier.astype(F32).astype(BF16))
    slot = jnp.sum(jnp.where(named, ranks, 0.0), axis=0, keepdims=True).astype(jnp.int32)
    apart = dest[...] ^ lax.axis_index("grp")
    place = jnp.where(lax.axis_index("col") == 0, apart, (owners - apart) & (owners - 1)) * cap + slot
    places[...] = place
    for copy in copies[1:]:
        copy.wait()
    turned = rate[...].T
    for r in range(high):
        rate_cols[r * wide : (r + 1) * wide] = turned[:, r : r + 1]
    cols = state[...].astype(BF16)
    cots = cot[...]
    for k in range(owners):
        rows = lax.broadcasted_iota(jnp.int32, (cap, count), 0) + k * cap
        placing = (rows == place).astype(F32).astype(BF16)
        chunks[k][:, :feats] = nn(placing, cols).astype(BF16)
        chunks[k][:, feats:] = nn(placing, cots).astype(BF16)
    strip = STEPS * wide
    odd = lax.rem(lax.axis_index("row"), 2)
    for out, top in ((inner, odd), (outer, 1 - odd)):
        start = pl.multiple_of((1 - top) * (count - strip), strip)
        out[:, :feats] = state[pl.ds(start, strip)].astype(BF16)
        out[:, feats:] = jnp.broadcast_to(rate_cols[pl.ds(start, strip)], (strip, 128)).astype(BF16)


def edge_kernel(wide, high, state, rate, near, far, place_row, inner, outer, places):
    feats = state.shape[1]
    span = high + 2 * STEPS
    half = span // 2
    odd, core = lax.rem(lax.axis_index("row"), 2), lax.axis_index("col")
    low = lax.broadcasted_iota(jnp.int32, (8, feats + 128), 0) < STEPS
    tiles = []
    for r in range(span):
        if r < high:
            first = [
                jnp.concatenate(
                    [
                        state[r * wide + c : r * wide + c + 8],
                        jnp.broadcast_to(rate[r * wide + c : r * wide + c + 8], (8, 128)),
                    ],
                    axis=1,
                )
                for c in (0, wide - 8)
            ]
        else:
            at = slice((r - high) % STEPS * wide, ((r - high) % STEPS + 1) * wide)
            is_near = (odd == 0) if r < high + STEPS else (odd == 1)
            both = jnp.where(is_near, near[at].astype(F32), far[at].astype(F32))
            first = [both[:8], both[wide - 8 :]]
        tiles.append(jnp.where(low, first[0], first[1]))
    lefts, rights = [], []
    for i in range(half):
        turned = pltpu.roll(tiles[i + half], STEPS, 0)
        lefts.append(jnp.where(low, tiles[i], turned))
        rights.append(jnp.where(low, turned, tiles[i]))
    for i in range(0, half, 2):
        one = jnp.concatenate(lefts[i : i + 2], axis=0)
        two = jnp.concatenate(rights[i : i + 2], axis=0)
        inner[i * 8 : i * 8 + 16] = jnp.where(core == 0, two, one).astype(BF16)
        outer[i * 8 : i * 8 + 16] = jnp.where(core == 0, one, two).astype(BF16)
    count = state.shape[0]
    same = lax.broadcasted_iota(jnp.int32, (count, count), 0) == lax.broadcasted_iota(
        jnp.int32, (count, count), 1
    )
    place = jnp.sum(jnp.where(same, place_row[...], 0).astype(F32), axis=1, keepdims=True)
    hits = lax.broadcasted_iota(jnp.int32, places.shape, 1) == place.astype(jnp.int32)
    places[...] = hits.astype(F32).astype(BF16)


def flow_kernel(wide, high, state, rate, near, far, inner, outer, out, grid, rates):
    feats = state.shape[1]
    span, across = high + 2 * STEPS, wide + 2 * STEPS
    half = span // 2
    odd, core = lax.rem(lax.axis_index("row"), 2), lax.axis_index("col")
    at = lax.broadcasted_iota(jnp.int32, (8, feats + 128), 0)
    low = jnp.where(core == 0, at, 7 - at) < STEPS
    for i in range(half):
        one = inner[i * 8 : i * 8 + 8].astype(F32)
        two = outer[i * 8 : i * 8 + 8].astype(F32)
        this = jnp.where(low, one, two)
        that = pltpu.roll(jnp.where(low, two, one), STEPS, 0)
        for r, tile in ((i, this), (i + half, that)):
            grid[0, r, wide:] = tile[:, :feats]
            rates[r, wide:] = tile[:, feats:]
    for r in range(high):
        grid[0, r, :wide] = state[r * wide : (r + 1) * wide]
        rates[r, :wide] = jnp.broadcast_to(rate[r * wide : (r + 1) * wide], (wide, 128))
    for at in range(STEPS):
        for ref, start in ((near, high + STEPS * odd), (far, high + STEPS * (1 - odd))):
            strip = ref[at * wide : (at + 1) * wide].astype(F32)
            grid[0, start + at, :wide] = strip[:, :feats]
            rates[start + at, :wide] = strip[:, feats:]
    for step in range(STEPS):
        now, later = step % 2, (step + 1) % 2
        margin = STEPS - 1 - step
        for r in [r % span for r in range(-margin, high + margin)]:
            here = grid[now, r]
            beside = (
                grid[now, (r - 1) % span]
                + grid[now, (r + 1) % span]
                + pltpu.roll(here, 1, 0)
                + pltpu.roll(here, across - 1, 0)
            )
            amount = rates[r]
            amount = jnp.concatenate([amount] * (feats // 128), axis=1)
            here = here + amount * (beside - 4.0 * here)
            if step == STEPS - 1:
                out[r * wide : (r + 1) * wide] = here[:wide]
            else:
                grid[later, r] = here


def physics_kernel(chunk, w_in, w_out, back, act_out, dpre_out):
    feats, hidden = w_in.shape
    cols = chunk[:, :feats]
    dtend = (0.5 * chunk[:, feats:].astype(F32)).astype(BF16)
    tend = adjoint = None
    piece = 256
    for h in range(0, hidden, piece):
        win, wout = w_in[:, h : h + piece], w_out[:, h : h + piece]
        pre = nn(cols, win)
        dact = nn(dtend, wout)
        sigma = 1.0 / (1.0 + jnp.exp(-pre))
        act = (pre * sigma).astype(BF16)
        dpre = (dact * (sigma * (1.0 + pre * (1.0 - sigma)))).astype(BF16)
        act_out[:, h : h + piece] = act
        dpre_out[:, h : h + piece] = dpre
        tend_h, adj_h = nt(act, wout), nt(dpre, win)
        tend = tend_h if tend is None else tend + tend_h
        adjoint = adj_h if adjoint is None else adjoint + adj_h
    back[:, :feats] = tend.astype(BF16)
    back[:, feats:] = adjoint.astype(BF16)


def first_physics_kernel(chunk, w_in_far, w_out_far, back, act_out, dpre_out, w_in, w_out, sems):
    copies = [
        pltpu.make_async_copy(w_in_far, w_in, sems.at[0]),
        pltpu.make_async_copy(w_out_far, w_out, sems.at[1]),
    ]
    for copy in copies:
        copy.start()
    for copy in copies:
        copy.wait()
    physics_kernel(chunk, w_in, w_out, back, act_out, dpre_out)


def grads_of(chunks, acts, dpres, h, piece, feats):
    dpre = jnp.concatenate([d[:, h : h + piece] for d in dpres], axis=0)
    act = jnp.concatenate([a[:, h : h + piece] for a in acts], axis=0)
    return dpre, act


def grads_kernel(owners, *refs):
    chunks, acts, dpres = refs[:owners], refs[owners : 2 * owners], refs[2 * owners : 3 * owners]
    keep, send = refs[3 * owners :]
    feats = chunks[0].shape[1] // 2
    hidden = acts[0].shape[1]
    block = keep.shape[2]
    cols = jnp.concatenate([c[:, :feats] for c in chunks], axis=0).T
    cots = jnp.concatenate([c[:, feats:] for c in chunks], axis=0)
    dtend = (0.5 * cots.astype(F32)).astype(BF16).T
    core = lax.axis_index("col")
    piece = 256
    for h in range(0, hidden, piece):
        dpre, act = grads_of(chunks, acts, dpres, h, piece, feats)
        for which, total in ((0, nn(cols, dpre)), (1, nn(dtend, act))):
            for x in range(2):
                one = total[2 * x * block : (2 * x + 1) * block]
                two = total[(2 * x + 1) * block : (2 * x + 2) * block]
                keep[which, x, :, h : h + piece] = jnp.where(core == 0, one, two)
                send[which, x, :, h : h + piece] = jnp.where(core == 0, two, one).astype(BF16)


def whole_grads_kernel(owners, *refs):
    chunks, acts, dpres = refs[:owners], refs[owners : 2 * owners], refs[2 * owners : 3 * owners]
    out = refs[3 * owners]
    feats = chunks[0].shape[1] // 2
    cols = jnp.concatenate([c[:, :feats] for c in chunks], axis=0).T
    cots = jnp.concatenate([c[:, feats:] for c in chunks], axis=0)
    dtend = (0.5 * cots.astype(F32)).astype(BF16).T
    piece = 256
    for h in range(0, acts[0].shape[1], piece):
        dpre, act = grads_of(chunks, acts, dpres, h, piece, feats)
        out[:feats, h : h + piece] = nn(cols, dpre)
        out[feats:, h : h + piece] = nn(dtend, act)


def share_kernel(keep, got, mine, *sends):
    row = lax.axis_index("row")
    y, x = lax.div(row, 2), lax.rem(row, 2)
    mine[...] = keep[y, x] + got[y, x].astype(F32)
    for send, (dy, dx) in zip(sends, ((0, 1), (1, 0), (1, 1))):
        send[...] = (keep[y ^ dy, x ^ dx] + got[y ^ dy, x ^ dx].astype(F32)).astype(BF16)


def gather_kernel(mine, one, two, three, out):
    rows, hidden = mine.shape
    for j in range(hidden // 128):
        at = slice(j * 128, (j + 1) * 128)
        total = mine[:, at] + one[:, at].astype(F32) + (two[:, at].astype(F32) + three[:, at].astype(F32))
        out[pl.ds(j, rows, stride=hidden // 128), :] = total


def finish_kernel(owners, field, places, *refs):
    backs, new_state, column_adjoint = refs[:owners], refs[owners], refs[owners + 1]
    feats = field.shape[1]
    cap = backs[0].shape[0]
    rows = nn(places[...], jnp.concatenate([b[...] for b in backs], axis=0))
    new_state[...] = field[...] + 0.5 * rows[:, :feats]
    column_adjoint[...] = rows[:, feats:].astype(BF16)


def swap(axis, bit):
    return [(i, i ^ bit) for i in range(lax.axis_size(axis))]


def partners(k):
    owners, cores = lax.axis_size("grp"), lax.axis_size("col")
    return [
        (g * cores + c, (g ^ (k if c == 0 else owners - k)) * cores + c)
        for g in range(owners)
        for c in range(cores)
    ]


def outward(axis):
    count = lax.axis_size(axis)
    return [(i, (i + 2 * (i % 2) - 1) % count) for i in range(count)]


def local(state, rate, cotangent, dest, w_in, w_out):
    high, wide, feats = state.shape
    count = high * wide
    owners = lax.axis_size("grp")
    cap = 2 * count // owners
    hidden = w_in.shape[2]
    flat_state = state.reshape(count, feats)
    flat_cot = cotangent.reshape(count, feats)

    strip = shape((STEPS * wide, feats + 128), BF16)
    *chunks, inner, outer, rate_col, place_row = call(
        functools.partial(pack_kernel, owners, cap, wide, high),
        [dest.reshape(1, count), rate, flat_state, flat_cot],
        [shape((cap, 2 * feats), BF16)] * owners + [strip, strip, shape((count, 1), F32), shape((1, count), jnp.int32)],
        [
            pltpu.VMEM((1, count), jnp.int32),
            pltpu.VMEM((high, wide), F32),
            pltpu.VMEM((count, feats), F32),
            pltpu.VMEM((count, feats), BF16),
            pltpu.SemaphoreType.DMA((4,)),
        ],
        far=(0, 1, 2, 3),
        vmem=60 << 20,
    )
    got = [chunks[0]] + [None] * (owners - 1)
    for k in range(owners - 1, 0, -1):
        got[k] = lax.ppermute(chunks[k], ("grp", "col"), partners(k))
    near = lax.ppermute(inner, "row", swap("row", 1))
    far = lax.ppermute(outer, "row", outward("row"))

    backs, acts, dpres = [None] * owners, [None] * owners, [None] * owners

    def physics(k, after=()):
        made = [shape((cap, 2 * feats), BF16)] + [shape((cap, hidden), BF16)] * 2
        backs[k], acts[k], dpres[k] = call(
            physics_kernel, [got[k], weight_in, weight_out], made, after=after
        )
        backs[k] = lax.ppermute(backs[k], ("grp", "col"), partners(k))
        return (acts[k],)

    weight = shape((feats, hidden), BF16)
    backs[0], acts[0], dpres[0], weight_in, weight_out = call(
        first_physics_kernel,
        [chunks[0], w_in[0], w_out[0]],
        [shape((cap, 2 * feats), BF16)] + [shape((cap, hidden), BF16)] * 2 + [weight, weight],
        [pltpu.SemaphoreType.DMA((2,))],
        far=(1, 2),
    )
    done = (acts[0],)
    side = shape(((high + 2 * STEPS) * STEPS, feats + 128), BF16)
    inner, outer, places = call(
        functools.partial(edge_kernel, wide, high),
        [flat_state, rate_col, near, far, place_row],
        [side, side, shape((count, owners * cap), BF16)],
        after=done,
    )
    inner_back = lax.ppermute(inner, "col", swap("col", 1))
    outer_back = lax.ppermute(outer, ("grp", "col"), outward(("grp", "col")))
    done = (places,)
    for k in (1, 2, 3, *range(4, owners)):
        done = physics(k, done)

    parts = lax.axis_size("row") * lax.axis_size("col")
    block = 2 * feats // parts
    if lax.axis_size("row") == 4 and lax.axis_size("col") == 2:
        keep, send = call(
            functools.partial(grads_kernel, owners),
            [*got, *acts, *dpres],
            [shape((2, 2, block, hidden), F32), shape((2, 2, block, hidden), BF16)],
        )
        arrived = lax.ppermute(send, "col", swap("col", 1))
        mine, *shares = call(
            share_kernel,
            [keep, arrived],
            [shape((block, hidden), F32)] + [shape((block, hidden), BF16)] * 3,
        )
        done = (mine,)
        shares = [lax.ppermute(s, "row", swap("row", bit + 1)) for bit, s in enumerate(shares)]
        (summed,) = call(
            gather_kernel, [mine, *shares], [shape((block * hidden // 128, 128), F32)]
        )
    else:
        (flat,) = call(
            functools.partial(whole_grads_kernel, owners),
            [*got, *acts, *dpres],
            [shape((2 * feats, hidden), F32)],
        )
        done = (flat,)
        summed = lax.psum_scatter(
            flat.reshape(-1, 128), ("row", "col"), scatter_dimension=0, tiled=True
        )
    (field,) = call(
        functools.partial(flow_kernel, wide, high),
        [flat_state, rate_col, near, far, inner_back, outer_back],
        [shape((count, feats), F32)],
        [
            pltpu.VMEM((2, high + 2 * STEPS, wide + 2 * STEPS, feats), F32),
            pltpu.VMEM((high + 2 * STEPS, wide + 2 * STEPS, 128), F32),
        ],
        after=done,
    )
    new_state, column_adjoint = call(
        functools.partial(finish_kernel, owners),
        [field, places, *backs],
        [shape((count, feats), F32), shape((count, feats), BF16)],
    )
    return (
        new_state.reshape(state.shape),
        column_adjoint.reshape(state.shape),
        summed[None],
    )


def solution(mesh):
    in_specs = (
        P("row", ("grp", "col"), None),
        P("row", ("grp", "col")),
        P("row", ("grp", "col"), None),
        P("row", ("grp", "col"), None, None),
        P("grp", None, None),
        P("grp", None, None),
    )
    out_specs = (
        P("row", ("grp", "col"), None),
        P("row", ("grp", "col"), None),
        P("grp", ("row", "col"), None),
    )
    return jax.shard_map(local, mesh=mesh, in_specs=in_specs, out_specs=out_specs, check_vma=False)
```

time: 50.9 us -> 39.7 us (0.78)
  waiting for transfers between devices: 15.7 us -> 4.48 us
  starting transfers between devices: 18.9 us -> 21.2 us
  Pallas kernels: 10.5 us -> 9.34 us
  local copies, waits for them, and re-layouts: 4.65 us -> 3.63 us
    ppermute x10, waiting for transfers between devices: 15.7 us -> 2.32 us  [the longest x3 2.1 us: physics(): backs[k] = lax.ppermute(backs[k], ('grp', 'col'), partners(k))]
    ppermute x3, waiting for transfers between devices: 0.01 us -> 2.16 us  [local(): lax.ppermute(s, 'row', swap('row', bit + 1))]
    ppermute x10, starting transfers between devices: 14.8 us -> 16.3 us  [the longest x3 5.68 us: local(): got[k] = lax.ppermute(chunks[k], ('grp', 'col'), partners(k))]
    pallas_call x11, Pallas kernels: 10.5 us -> 9.34 us  [call(): pl.pallas_call(body, out_shape=list(outs), in_specs=specs + [ANY] * len(a...]
    reshape x2 -> x0, local copies, waits for them, and re-layouts: 0.98 us -> none  [the longest x1 0.85 us: local(): rate_col = rate.reshape(count, 1)]
    unnamed x14 -> x12, local copies, waits for them, and re-layouts: 3.59 us -> 3.63 us
  transfers between devices with their start and end apart: 14 -> 14, of which waited for: 6 -> 4; matrix products, arithmetic and copies ran while one was open for 0% -> 0% of each run, Pallas kernels for 12% -> 12%
where the time goes in v2:
time: 39.7 us; the launch traced here: 39.4 us
  starting transfers between devices  21.2 us (53%)
  Pallas kernels  9.34 us (24%)
  waiting for transfers between devices  4.48 us (11%)
  local copies, waits for them, and re-layouts  3.63 us (9%)
  between operations  0.76 us (2%)
    pallas_call x11, Pallas kernels, call(): pl.pallas_call(body, out_shape=list(outs), in_specs=specs + [ANY] * len(a...  9.34 us
    ppermute x3, starting transfers between devices, local(): got[k] = lax.ppermute(chunks[k], ('grp', 'col'), partners(k))  5.68 us
    ppermute x3, starting transfers between devices, physics(): backs[k] = lax.ppermute(backs[k], ('grp', 'col'), partners(k))  4.81 us
    ppermute x3, starting transfers between devices, local(): lax.ppermute(s, 'row', swap('row', bit + 1))  4.52 us
    unnamed x12, local copies, waits for them, and re-layouts  3.63 us
    ppermute x1, starting transfers between devices, local(): inner_back = lax.ppermute(inner, 'col', swap('col', 1))  2.36 us
    ppermute x3, waiting for transfers between devices, local(): lax.ppermute(s, 'row', swap('row', bit + 1))  2.16 us
    ppermute x3, waiting for transfers between devices, physics(): backs[k] = lax.ppermute(backs[k], ('grp', 'col'), partners(k))  2.1 us
  transfers between devices with their start and end apart: 14, of which 4 were waited for; matrix products, arithmetic and copies ran while one was open for 0% of the time, Pallas kernels for 12%

profile of v2, /device:TPU:0, one launch (start us, length us, event | category | flops | bytes accessed | tf_op | source)
XLA Modules:
  0.0 39.4 jit_solution(7149804814829553410)
XLA Ops:
  0.6 2.1 %shard_map.85 = (bf16[128,512]{1,0:T(8,128)(2,1)}, bf16[128,512]{1,0:T(8,128)(2,1)}, bf16[128,512]{1,0:T(8,128)(2,1)}, bf16[128,512]{1,0:T(8,128)(2,1)}, bf16[64...) custom-call(s32[1,256]{1,0:T(1,128)} %bitcast.15, f32[16,16]{1,0:T(8,128)} %refs_1_.1, ...), custom_call_target="tpu_custom_call" | custom-call | tf_op jit(solution)/shard_map/pallas_call | solution.py:25
  2.8 3.1 %collective-permute-start.4 = (bf16[128,512]{1,0:T(8,128)(2,1)}, bf16[128,512]{1,0:T(8,128)(2,1)S(1)}, u32[]{:S(2)}, u32[]{:S(2)}) collective-permute-start(bf16[128,512]{1,0:T(8,128)(2,1)} %get-tuple-element.44), channel_id=1, source_target_pairs={{0,2},{1,7},{2,0},{3,5},{4,6},{5,3},{6,4},{7,1},{8,10},{9,15},{10,... | collective-permute-start | bytes 393224 | tf_op jit(solution)/shard_map/ppermute | solution.py:316
  5.9 2.6 %collective-permute-start.5 = (bf16[128,512]{1,0:T(8,128)(2,1)}, bf16[128,512]{1,0:T(8,128)(2,1)S(1)}, u32[]{:S(2)}, u32[]{:S(2)}) collective-permute-start(bf16[128,512]{1,0:T(8,128)(2,1)} %get-tuple-element.45), channel_id=1, source_target_pairs={{0,4},{1,5},{2,6},{3,7},{4,0},{5,1},{6,2},{7,3},{8,12},{9,13},{10,... | collective-permute-start | bytes 393224 | tf_op jit(solution)/shard_map/ppermute | solution.py:316
  8.4 0.0 collective-permute-start.6
  8.5 1.7 %collective-permute-start = (bf16[64,384]{1,0:T(8,128)(2,1)}, bf16[64,384]{1,0:T(8,128)(2,1)S(1)}, u32[]{:S(2)}, u32[]{:S(2)}) collective-permute-start(bf16[64,384]{1,0:T(8,128)(2,1)} %get-tuple-element.37), channel_id=1, source_target_pairs={{0,8},{8,0},{16,24},{24,16},{1,9},{9,1},{17,25},{25,17},{2,10},{10... | collective-permute-start | bytes 147464 | tf_op jit(solution)/shard_map/ppermute | solution.py:317
  10.2 1.5 %collective-permute-start.1 = (bf16[64,384]{1,0:T(8,128)(2,1)}, bf16[64,384]{1,0:T(8,128)(2,1)S(1)}, u32[]{:S(2)}, u32[]{:S(2)}) collective-permute-start(bf16[64,384]{1,0:T(8,128)(2,1)} %get-tuple-element.38), channel_id=1, source_target_pairs={{0,24},{8,16},{16,8},{24,0},{1,25},{9,17},{17,9},{25,1},{2,26},{10... | collective-permute-start | bytes 147464 | tf_op jit(solution)/shard_map/ppermute | solution.py:318
  11.7 0.0 copy-start.1
  11.7 0.9 %copy-done.1 = bf16[128,512]{1,0:T(8,128)(2,1)S(1)} copy-done((bf16[128,512]{1,0:T(8,128)(2,1)S(1)}, bf16[128,512]{1,0:T(8,128)(2,1)}, u32[]{:S(2)}) %copy-start.1) | copy-done | bytes 131096
  12.6 0.0 copy-start.2
  12.6 1.0 %copy-done.2 = bf16[1,256,1024]{2,1,0:T(8,128)(2,1)S(1)} copy-done((bf16[1,256,1024]{2,1,0:T(8,128)(2,1)S(1)}, bf16[1,256,1024]{2,1,0:T(8,128)(2,1)}, u32[]{:S(2)}) %copy-start.2) | copy-done | bytes 524312
  13.6 0.0 copy-start.3
  13.6 1.0 %copy-done.3 = bf16[1,256,1024]{2,1,0:T(8,128)(2,1)S(1)} copy-done((bf16[1,256,1024]{2,1,0:T(8,128)(2,1)S(1)}, bf16[1,256,1024]{2,1,0:T(8,128)(2,1)}, u32[]{:S(2)}) %copy-start.3) | copy-done | bytes 524312
  14.6 0.0 copy-start
  14.6 0.0 copy-start.4
  14.6 1.0 %shard_map.86 = (bf16[128,512]{1,0:T(8,128)(2,1)S(1)}, bf16[128,1024]{1,0:T(8,128)(2,1)S(1)}, bf16[128,1024]{1,0:T(8,128)(2,1)S(1)}, bf16[256,1024]{1,0:T(8,128)(2,1)S(1)}, bf16[256,1024]{1,0:T(8,128)(2,1)S(1)}) custom-call(bf16[128,512]{1,0:T(8,128)(2,1)S(1)} %copy-done.1, bf16[256,1024]{1,0:T(8,128)(2,1)S(1)} %bitcast.11, bf16[256,1024]{1,0:T(8,128)(2,1)S(1)} %bitcast.12), custom_call_target="tpu_custom_call" | custom-call | tf_op jit(solution)/shard_map/pallas_call | solution.py:25
  15.6 0.0 collective-permute-done.refs_2_
  15.6 0.0 collective-permute-done.1.refs_3_
  15.7 0.0 copy-start.5
  15.7 0.0 copy-done
  15.7 0.0 copy-done.4
  15.7 0.6 %copy-done.5 = s32[1,256]{1,0:T(1,128)S(1)} copy-done((s32[1,256]{1,0:T(1,128)S(1)}, s32[1,256]{1,0:T(1,128)}, u32[]{:S(2)}) %copy-start.5) | copy-done | bytes 1048
  16.3 0.2 shard_map.87
  16.5 0.0 collective-permute-done.4.refs_0_.refs_1_
  16.5 0.9 %shard_map.88 = (bf16[128,512]{1,0:T(8,128)(2,1)S(1)}, bf16[128,1024]{1,0:T(8,128)(2,1)S(1)}, bf16[128,1024]{1,0:T(8,128)(2,1)S(1)}) custom-call(bf16[128,512]{1,0:T(8,128)(2,1)S(1)} %collective-permute-done.4.refs_0_.refs_1_, bf16[256,1024]{1,0:T(8,128)(2,1)S(1)} %get-tuple-element.47.refs_1_, bf16[256,1024]{1,0:T(8,128)(2,1)S(1)} %get-tuple-element.48.refs_2_, ...), custom_call_target="tpu_custom_call" | custom-call | tf_op jit(solution)/shard_map/pallas_call | solution.py:25
  17.4 0.1 collective-permute-done.5.refs_0_.refs_2_
  17.5 0.9 %shard_map.89 = (bf16[128,512]{1,0:T(8,128)(2,1)S(1)}, bf16[128,1024]{1,0:T(8,128)(2,1)S(1)}, bf16[128,1024]{1,0:T(8,128)(2,1)S(1)}) custom-call(bf16[128,512]{1,0:T(8,128)(2,1)S(1)} %collective-permute-done.5.refs_0_.refs_2_, bf16[256,1024]{1,0:T(8,128)(2,1)S(1)} %get-tuple-element.47.refs_1_, bf16[256,1024]{1,0:T(8,128)(2,1)S(1)} %get-tuple-element.48.refs_2_, ...), custom_call_target="tpu_custom_call" | custom-call | tf_op jit(solution)/shard_map/pallas_call | solution.py:25
  18.4 0.0 collective-permute-done.6.refs_0_.refs_3_
  18.4 0.9 %shard_map.90 = (bf16[128,512]{1,0:T(8,128)(2,1)S(1)}, bf16[128,1024]{1,0:T(8,128)(2,1)S(1)}, bf16[128,1024]{1,0:T(8,128)(2,1)S(1)}) custom-call(bf16[128,512]{1,0:T(8,128)(2,1)S(1)} %collective-permute-done.6.refs_0_.refs_3_, bf16[256,1024]{1,0:T(8,128)(2,1)S(1)} %get-tuple-element.47.refs_1_, bf16[256,1024]{1,0:T(8,128)(2,1)S(1)} %get-tuple-element.48.refs_2_, ...), custom_call_target="tpu_custom_call" | custom-call | tf_op jit(solution)/shard_map/pallas_call | solution.py:25
  19.3 0.8 %shard_map.91 = (f32[2,2,64,1024]{3,2,1,0:T(8,128)S(1)}, bf16[2,2,64,1024]{3,2,1,0:T(8,128)(2,1)S(1)}) custom-call(bf16[128,512]{1,0:T(8,128)(2,1)S(1)} %copy-done.1, bf16[128,512]{1,0:T(8,128)(2,1)S(1)} %collective-permute-done.4.refs_0_.refs_1_, bf16[128,512]{1,0:T(8,128)(2,1)S(1)} %collective-permute-done.5.refs_0_.refs_2_, ...), custom_call_target="tpu_custom_call" | custom-call | tf_op jit(solution)/shard_map/pallas_call | solution.py:25
  20.1 0.4 collective-permute-start.7
  20.5 1.1 %collective-permute-start.8 = (bf16[128,512]{1,0:T(8,128)(2,1)S(1)}, bf16[128,512]{1,0:T(8,128)(2,1)S(1)}, u32[]{:S(2)}, u32[]{:S(2)}) collective-permute-start(bf16[128,512]{1,0:T(8,128)(2,1)S(1)} %get-tuple-element.61), channel_id=1, source_target_pairs={{0,2},{1,7},{2,0},{3,5},{4,6},{5,3},{6,4},{7,1},{8,10},{9,15},{10,... | collective-permute-start | bytes 393224 | tf_op jit(solution)/shard_map/ppermute | solution.py:327
  21.6 2.4 %collective-permute-start.2 = (bf16[96,384]{1,0:T(8,128)(2,1)S(1)}, bf16[96,384]{1,0:T(8,128)(2,1)S(1)}, u32[]{:S(2)}, u32[]{:S(2)}) collective-permute-start(bf16[96,384]{1,0:T(8,128)(2,1)S(1)} %get-tuple-element.42), channel_id=1, source_target_pairs={{0,1},{1,0},{2,3},{3,2},{4,5},{5,4},{6,7},{7,6},{8,9},{9,8},{10,11... | collective-permute-start | bytes 221192 | tf_op jit(solution)/shard_map/ppermute | solution.py:346
  23.9 0.3 collective-permute-start.3
  24.2 0.2 collective-permute-start.9
  24.4 0.0 collective-permute-done.7.refs_1_
  24.4 3.5 %collective-permute-start.10 = (bf16[128,512]{1,0:T(8,128)(2,1)S(1)}, bf16[128,512]{1,0:T(8,128)(2,1)S(1)}, u32[]{:S(2)}, u32[]{:S(2)}) collective-permute-start(bf16[128,512]{1,0:T(8,128)(2,1)S(1)} %get-tuple-element.63), channel_id=1, source_target_pairs={{0,6},{1,3},{2,4},{3,1},{4,2},{5,7},{6,0},{7,5},{8,14},{9,11},{10,... | collective-permute-start | bytes 393224 | tf_op jit(solution)/shard_map/ppermute | solution.py:327
  27.9 0.1 shard_map.92
  28.0 0.0 collective-permute-done.2.refs_4_
  28.0 1.6 %collective-permute-start.11 = (bf16[64,1024]{1,0:T(8,128)(2,1)S(1)}, bf16[64,1024]{1,0:T(8,128)(2,1)S(1)}, u32[]{:S(2)}, u32[]{:S(2)}) collective-permute-start(bf16[64,1024]{1,0:T(8,128)(2,1)S(1)} %get-tuple-element.66), channel_id=1, source_target_pairs={{0,8},{8,0},{16,24},{24,16},{1,9},{9,1},{17,25},{25,17},{2,10},{10... | collective-permute-start | bytes 393224 | tf_op jit(solution)/shard_map/ppermute | solution.py:367
  29.6 0.1 collective-permute-done.3.refs_5_
  29.7 1.8 %collective-permute-start.12 = (bf16[64,1024]{1,0:T(8,128)(2,1)S(1)}, bf16[64,1024]{1,0:T(8,128)(2,1)S(1)}, u32[]{:S(2)}, u32[]{:S(2)}) collective-permute-start(bf16[64,1024]{1,0:T(8,128)(2,1)S(1)} %get-tuple-element.67), channel_id=1, source_target_pairs={{0,16},{8,24},{16,0},{24,8},{1,17},{9,25},{17,1},{25,9},{2,18},{10... | collective-permute-start | bytes 393224 | tf_op jit(solution)/shard_map/ppermute | solution.py:367
  31.5 0.0 collective-permute-done.8.refs_3_
  31.5 1.2 %collective-permute-start.13 = (bf16[64,1024]{1,0:T(8,128)(2,1)S(1)}, bf16[64,1024]{1,0:T(8,128)(2,1)S(1)}, u32[]{:S(2)}, u32[]{:S(2)}) collective-permute-start(bf16[64,1024]{1,0:T(8,128)(2,1)S(1)} %get-tuple-element.68), channel_id=1, source_target_pairs={{0,24},{8,16},{16,8},{24,0},{1,25},{9,17},{17,9},{25,1},{2,26},{10... | collective-permute-start | bytes 393224 | tf_op jit(solution)/shard_map/ppermute | solution.py:367
  32.6 0.7 %shard_map.93.refs_0_ = f32[256,256]{1,0:T(8,128)S(1)} custom-call(f32[256,256]{1,0:T(8,128)S(1)} %bitcast.10, f32[256,1]{1,0:T(8,128)S(1)} %copy-done.4, bf16[64,384]{1,0:T(8,128)(2,1)S(1)} %collective-permute-done.refs_2_, bf16[64,384]{1,0:T(8,128)(2,1)S(1)} %collective-permute-done.1.refs_3_, bf16[96,384]{1,0:T(8,128)(2,1)S(1)} %collective-permute-done.2.refs_4_, ...), custom_call_target="tpu_custom_call" | custom-call | tf_op jit(solution)/shard_map/pallas_call | solution.py:25
  33.3 2.1 %collective-permute-done.9.refs_4_ = bf16[128,512]{1,0:T(8,128)(2,1)S(1)} collective-permute-done((bf16[128,512]{1,0:T(8,128)(2,1)S(1)}, bf16[128,512]{1,0:T(8,128)(2,1)S(1)}, u32[]{:S(2)}, u32[]{:S(2)}) %collective-permute-start.9) | collective-permute-done | bytes 131104 | tf_op jit(solution)/shard_map/ppermute | solution.py:327
  35.4 0.0 collective-permute-done.10.refs_5_
  35.4 1.1 %shard_map.94 = (f32[256,256]{1,0:T(8,128)}, bf16[256,256]{1,0:T(8,128)(2,1)}) custom-call(f32[256,256]{1,0:T(8,128)S(1)} %shard_map.93.refs_0_, bf16[256,512]{1,0:T(8,128)(2,1)S(1)} %get-tuple-element.49.refs_3_.refs_1_, bf16[128,512]{1,0:T(8,128)(2,1)S(1)} %get-tuple-element.60.refs_2_, bf16[128,512]{1,0:T(8,128)(2,1)S(1)} %collective-permute-done.8.refs_3_, ...), custom_call_target="tpu_custom_call" | custom-call | tf_op jit(solution)/shard_map/pallas_call | solution.py:25
  36.5 0.0 collective-permute-done.11.refs_1_
  36.5 2.2 %collective-permute-done.12.refs_2_ = bf16[64,1024]{1,0:T(8,128)(2,1)S(1)} collective-permute-done((bf16[64,1024]{1,0:T(8,128)(2,1)S(1)}, bf16[64,1024]{1,0:T(8,128)(2,1)S(1)}, u32[]{:S(2)}, u32[]{:S(2)}) %collective-permute-start.12) | collective-permute-done | bytes 131104 | tf_op jit(solution)/shard_map/ppermute | solution.py:367
  38.6 0.0 collective-permute-done.13.refs_3_
  38.6 0.8 %shard_map.95 = f32[512,128]{1,0:T(8,128)} custom-call(f32[64,1024]{1,0:T(8,128)S(1)} %get-tuple-element.59.refs_6_.refs_0_, bf16[64,1024]{1,0:T(8,128)(2,1)S(1)} %collective-permute-done.11.refs_1_, bf16[64,1024]{1,0:T(8,128)(2,1)S(1)} %collective-permute-done.12.refs_2_, bf16[64,1024]{1,0:T(8,128)(2,1)S(1)} %collective-permute-done.13.refs_3_), custom_call_target="tpu_custom_call" | custom-call | tf_op jit(solution)/shard_map/pallas_call | solution.py:25
Async XLA Ops:
  2.8 13.7 %collective-permute-start.4 = (bf16[128,512]{1,0:T(8,128)(2,1)}, bf16[128,512]{1,0:T(8,128)(2,1)S(1)}, u32[]{:S(2)}, u32[]{:S(2)}) collective-permute-start(bf16[128,512]{1,0:T(8,128)(2,1)} %get-tuple-element.44), channel_id=1, source_target_pairs={{0,2},{1,7},{2,0},{3,5},{4,6},{5,3},{6,4},{7,1},{8,10},{9,15},{10,... | collective-permute-start | bytes 393224 | tf_op jit(solution)/shard_map/ppermute | solution.py:316
  5.9 11.7 %collective-permute-start.5 = (bf16[128,512]{1,0:T(8,128)(2,1)}, bf16[128,512]{1,0:T(8,128)(2,1)S(1)}, u32[]{:S(2)}, u32[]{:S(2)}) collective-permute-start(bf16[128,512]{1,0:T(8,128)(2,1)} %get-tuple-element.45), channel_id=1, source_target_pairs={{0,4},{1,5},{2,6},{3,7},{4,0},{5,1},{6,2},{7,3},{8,12},{9,13},{10,... | collective-permute-start | bytes 393224 | tf_op jit(solution)/shard_map/ppermute | solution.py:316
  8.4 10.0 %collective-permute-start.6 = (bf16[128,512]{1,0:T(8,128)(2,1)}, bf16[128,512]{1,0:T(8,128)(2,1)S(1)}, u32[]{:S(2)}, u32[]{:S(2)}) collective-permute-start(bf16[128,512]{1,0:T(8,128)(2,1)} %get-tuple-element.46), channel_id=1, source_target_pairs={{0,6},{1,3},{2,4},{3,1},{4,2},{5,7},{6,0},{7,5},{8,14},{9,11},{10,... | collective-permute-start | bytes 393224 | tf_op jit(solution)/shard_map/ppermute | solution.py:316
  8.5 7.2 %collective-permute-start = (bf16[64,384]{1,0:T(8,128)(2,1)}, bf16[64,384]{1,0:T(8,128)(2,1)S(1)}, u32[]{:S(2)}, u32[]{:S(2)}) collective-permute-start(bf16[64,384]{1,0:T(8,128)(2,1)} %get-tuple-element.37), channel_id=1, source_target_pairs={{0,8},{8,0},{16,24},{24,16},{1,9},{9,1},{17,25},{25,17},{2,10},{10... | collective-permute-start | bytes 147464 | tf_op jit(solution)/shard_map/ppermute | solution.py:317
  10.2 5.5 %collective-permute-start.1 = (bf16[64,384]{1,0:T(8,128)(2,1)}, bf16[64,384]{1,0:T(8,128)(2,1)S(1)}, u32[]{:S(2)}, u32[]{:S(2)}) collective-permute-start(bf16[64,384]{1,0:T(8,128)(2,1)} %get-tuple-element.38), channel_id=1, source_target_pairs={{0,24},{8,16},{16,8},{24,0},{1,25},{9,17},{17,9},{25,1},{2,26},{10... | collective-permute-start | bytes 147464 | tf_op jit(solution)/shard_map/ppermute | solution.py:318
  11.7 0.9 %copy-start.1 = (bf16[128,512]{1,0:T(8,128)(2,1)S(1)}, bf16[128,512]{1,0:T(8,128)(2,1)}, u32[]{:S(2)}) copy-start(bf16[128,512]{1,0:T(8,128)(2,1)} %get-tuple-element.40.refs_0_) | copy-start | bytes 393220
  12.6 1.0 %copy-start.2 = (bf16[1,256,1024]{2,1,0:T(8,128)(2,1)S(1)}, bf16[1,256,1024]{2,1,0:T(8,128)(2,1)}, u32[]{:S(2)}) copy-start(bf16[1,256,1024]{2,1,0:T(8,128)(2,1)} %param.10) | copy-start | bytes 1572868
  13.6 1.0 %copy-start.3 = (bf16[1,256,1024]{2,1,0:T(8,128)(2,1)S(1)}, bf16[1,256,1024]{2,1,0:T(8,128)(2,1)}, u32[]{:S(2)}) copy-start(bf16[1,256,1024]{2,1,0:T(8,128)(2,1)} %param.11) | copy-start | bytes 1572868
  14.6 1.0 %copy-start = (f32[16,16,256]{2,1,0:T(8,128)S(1)}, f32[16,16,256]{2,1,0:T(8,128)}, u32[]{:S(2)}) copy-start(f32[16,16,256]{2,1,0:T(8,128)} %param.6) | copy-start | bytes 786436
  14.6 1.0 %copy-start.4 = (f32[256,1]{1,0:T(8,128)S(1)}, f32[256,1]{1,0:T(8,128)}, u32[]{:S(2)}) copy-start(f32[256,1]{1,0:T(8,128)} %get-tuple-element.36.refs_1_) | copy-start | bytes 3076
  15.7 0.7 %copy-start.5 = (s32[1,256]{1,0:T(1,128)S(1)}, s32[1,256]{1,0:T(1,128)}, u32[]{:S(2)}) copy-start(s32[1,256]{1,0:T(1,128)} %get-tuple-element.39.refs_4_) | copy-start | bytes 3076
  20.1 4.3 %collective-permute-start.7 = (bf16[2,2,64,1024]{3,2,1,0:T(8,128)(2,1)S(1)}, bf16[2,2,64,1024]{3,2,1,0:T(8,128)(2,1)S(1)}, u32[]{:S(2)}, u32[]{:S(2)}) collective-permute-start(bf16[2,2,64,1024]{3,2,1,0:T(8,128)(2,1)S(1)} %get-tuple-element.58), channel_id=1, source_target_pairs={{0,1},{1,0},{2,3},{3,2},{4,5},{5,4},{6,7},{7,6},{8,9},{9,8},{10,11... | collective-permute-start | bytes 1572872 | tf_op jit(solution)/shard_map/ppermute | solution.py:360
  20.5 11.0 %collective-permute-start.8 = (bf16[128,512]{1,0:T(8,128)(2,1)S(1)}, bf16[128,512]{1,0:T(8,128)(2,1)S(1)}, u32[]{:S(2)}, u32[]{:S(2)}) collective-permute-start(bf16[128,512]{1,0:T(8,128)(2,1)S(1)} %get-tuple-element.61), channel_id=1, source_target_pairs={{0,2},{1,7},{2,0},{3,5},{4,6},{5,3},{6,4},{7,1},{8,10},{9,15},{10,... | collective-permute-start | bytes 393224 | tf_op jit(solution)/shard_map/ppermute | solution.py:327
  21.6 6.5 %collective-permute-start.2 = (bf16[96,384]{1,0:T(8,128)(2,1)S(1)}, bf16[96,384]{1,0:T(8,128)(2,1)S(1)}, u32[]{:S(2)}, u32[]{:S(2)}) collective-permute-start(bf16[96,384]{1,0:T(8,128)(2,1)S(1)} %get-tuple-element.42), channel_id=1, source_target_pairs={{0,1},{1,0},{2,3},{3,2},{4,5},{5,4},{6,7},{7,6},{8,9},{9,8},{10,11... | collective-permute-start | bytes 221192 | tf_op jit(solution)/shard_map/ppermute | solution.py:346
  23.9 5.8 %collective-permute-start.3 = (bf16[96,384]{1,0:T(8,128)(2,1)S(1)}, bf16[96,384]{1,0:T(8,128)(2,1)S(1)}, u32[]{:S(2)}, u32[]{:S(2)}) collective-permute-start(bf16[96,384]{1,0:T(8,128)(2,1)S(1)} %get-tuple-element.43), channel_id=1, source_target_pairs={{0,7},{1,2},{2,1},{3,4},{4,3},{5,6},{6,5},{7,0},{8,15},{9,10},{10,... | collective-permute-start | bytes 221192 | tf_op jit(solution)/shard_map/ppermute | solution.py:347
  24.2 11.2 %collective-permute-start.9 = (bf16[128,512]{1,0:T(8,128)(2,1)S(1)}, bf16[128,512]{1,0:T(8,128)(2,1)S(1)}, u32[]{:S(2)}, u32[]{:S(2)}) collective-permute-start(bf16[128,512]{1,0:T(8,128)(2,1)S(1)} %get-tuple-element.62), channel_id=1, source_target_pairs={{0,4},{1,5},{2,6},{3,7},{4,0},{5,1},{6,2},{7,3},{8,12},{9,13},{10,... | collective-permute-start | bytes 393224 | tf_op jit(solution)/shard_map/ppermute | solution.py:327
  24.4 11.0 %collective-permute-start.10 = (bf16[128,512]{1,0:T(8,128)(2,1)S(1)}, bf16[128,512]{1,0:T(8,128)(2,1)S(1)}, u32[]{:S(2)}, u32[]{:S(2)}) collective-permute-start(bf16[128,512]{1,0:T(8,128)(2,1)S(1)} %get-tuple-element.63), channel_id=1, source_target_pairs={{0,6},{1,3},{2,4},{3,1},{4,2},{5,7},{6,0},{7,5},{8,14},{9,11},{10,... | collective-permute-start | bytes 393224 | tf_op jit(solution)/shard_map/ppermute | solution.py:327
  28.0 8.5 %collective-permute-start.11 = (bf16[64,1024]{1,0:T(8,128)(2,1)S(1)}, bf16[64,1024]{1,0:T(8,128)(2,1)S(1)}, u32[]{:S(2)}, u32[]{:S(2)}) collective-permute-start(bf16[64,1024]{1,0:T(8,128)(2,1)S(1)} %get-tuple-element.66), channel_id=1, source_target_pairs={{0,8},{8,0},{16,24},{24,16},{1,9},{9,1},{17,25},{25,17},{2,10},{10... | collective-permute-start | bytes 393224 | tf_op jit(solution)/shard_map/ppermute | solution.py:367
  29.7 9.0 %collective-permute-start.12 = (bf16[64,1024]{1,0:T(8,128)(2,1)S(1)}, bf16[64,1024]{1,0:T(8,128)(2,1)S(1)}, u32[]{:S(2)}, u32[]{:S(2)}) collective-permute-start(bf16[64,1024]{1,0:T(8,128)(2,1)S(1)} %get-tuple-element.67), channel_id=1, source_target_pairs={{0,16},{8,24},{16,0},{24,8},{1,17},{9,25},{17,1},{25,9},{2,18},{10... | collective-permute-start | bytes 393224 | tf_op jit(solution)/shard_map/ppermute | solution.py:367
  31.5 7.2 %collective-permute-start.13 = (bf16[64,1024]{1,0:T(8,128)(2,1)S(1)}, bf16[64,1024]{1,0:T(8,128)(2,1)S(1)}, u32[]{:S(2)}, u32[]{:S(2)}) collective-permute-start(bf16[64,1024]{1,0:T(8,128)(2,1)S(1)} %get-tuple-element.68), channel_id=1, source_target_pairs={{0,24},{8,16},{16,8},{24,0},{1,25},{9,17},{17,9},{25,1},{2,26},{10... | collective-permute-start | bytes 393224 | tf_op jit(solution)/shard_map/ppermute | solution.py:367

commit v3 on v2

--- a/solution.py
+++ b/solution.py
@@ -15,7 +15,8 @@
 ANY = pl.BlockSpec(memory_space=pl.ANY)
 
 
-def call(kernel, ins, outs, scratch=(), after=(), far=(), vmem=24 << 20):
+def call(kernel, ins, outs, scratch=(), after=(), far=(), vmem=24 << 20, flops=None):
+    ins = [pltpu.with_memory_space_constraint(x, pltpu.HBM) if n in far else x for n, x in enumerate(ins)]
     specs = [HBM if n in far else VMEM for n in range(len(ins))]
     count = len(ins)
 
@@ -29,6 +30,7 @@
         out_specs=[VMEM] * len(outs),
         scratch_shapes=list(scratch),
         compiler_params=pltpu.CompilerParams(vmem_limit_bytes=vmem),
+        cost_estimate=flops and pl.CostEstimate(flops=flops, bytes_accessed=0, transcendentals=0),
     )(*ins, *after)
 
 
@@ -59,8 +61,9 @@
     )
     ranks = nn(named.astype(F32).astype(BF16), earlier.astype(F32).astype(BF16))
     slot = jnp.sum(jnp.where(named, ranks, 0.0), axis=0, keepdims=True).astype(jnp.int32)
-    apart = dest[...] ^ lax.axis_index("grp")
-    place = jnp.where(lax.axis_index("col") == 0, apart, (owners - apart) & (owners - 1)) * cap + slot
+    ahead = dest[...] - lax.axis_index("grp")
+    turn = jnp.where(lax.axis_index("col") == 0, -ahead, ahead)
+    place = jnp.where(turn < 0, turn + owners, turn) * cap + slot
     places[...] = place
     for copy in copies[1:]:
         copy.wait()
@@ -192,9 +195,12 @@
 
 
 def first_physics_kernel(chunk, w_in_far, w_out_far, back, act_out, dpre_out, w_in, w_out, sems):
+    feats, hidden = w_in.shape
+    piece = feats // 4
     copies = [
-        pltpu.make_async_copy(w_in_far, w_in, sems.at[0]),
-        pltpu.make_async_copy(w_out_far, w_out, sems.at[1]),
+        pltpu.make_async_copy(far.at[at], near.at[at], sems.at[n, r])
+        for r, at in enumerate(pl.ds(r * piece, piece) for r in range(4))
+        for n, (far, near) in enumerate(((w_in_far, w_in), (w_out_far, w_out)))
     ]
     for copy in copies:
         copy.start()
@@ -244,6 +250,10 @@
         out[feats:, h : h + piece] = nn(dtend, act)
 
 
+def gap_kernel(out):
+    out[...] = jnp.zeros_like(out)
+
+
 def share_kernel(keep, got, mine, *sends):
     row = lax.axis_index("row")
     y, x = lax.div(row, 2), lax.rem(row, 2)
@@ -275,11 +285,8 @@
 
 def partners(k):
     owners, cores = lax.axis_size("grp"), lax.axis_size("col")
-    return [
-        (g * cores + c, (g ^ (k if c == 0 else owners - k)) * cores + c)
-        for g in range(owners)
-        for c in range(cores)
-    ]
+    pairs = [(g * cores, (g - k) % owners * cores + 1) for g in range(owners)]
+    return pairs + [(b, a) for a, b in pairs]
 
 
 def outward(axis):
@@ -309,7 +316,6 @@
             pltpu.SemaphoreType.DMA((4,)),
         ],
         far=(0, 1, 2, 3),
-        vmem=60 << 20,
     )
     got = [chunks[0]] + [None] * (owners - 1)
     for k in range(owners - 1, 0, -1):
@@ -332,7 +338,7 @@
         first_physics_kernel,
         [chunks[0], w_in[0], w_out[0]],
         [shape((cap, 2 * feats), BF16)] + [shape((cap, hidden), BF16)] * 2 + [weight, weight],
-        [pltpu.SemaphoreType.DMA((2,))],
+        [pltpu.SemaphoreType.DMA((2, 4))],
         far=(1, 2),
     )
     done = (acts[0],)
@@ -343,8 +349,8 @@
         [side, side, shape((count, owners * cap), BF16)],
         after=done,
     )
+    outer_back = lax.ppermute(outer, ("grp", "col"), outward(("grp", "col")))
     inner_back = lax.ppermute(inner, "col", swap("col", 1))
-    outer_back = lax.ppermute(outer, ("grp", "col"), outward(("grp", "col")))
     done = (places,)
     for k in (1, 2, 3, *range(4, owners)):
         done = physics(k, done)
@@ -358,10 +364,12 @@
             [shape((2, 2, block, hidden), F32), shape((2, 2, block, hidden), BF16)],
         )
         arrived = lax.ppermute(send, "col", swap("col", 1))
+        (gap,) = call(gap_kernel, [], [shape((8, 128), F32)], after=(keep,), flops=10000000000)
         mine, *shares = call(
             share_kernel,
             [keep, arrived],
             [shape((block, hidden), F32)] + [shape((block, hidden), BF16)] * 3,
+            after=(gap,),
         )
         done = (mine,)
         shares = [lax.ppermute(s, "row", swap("row", bit + 1)) for bit, s in enumerate(shares)]

time: 39.7 us -> 35.5 us (0.89)
  starting transfers between devices: 21.2 us -> 17.1 us
  local copies, waits for them, and re-layouts: 3.63 us -> 0.01 us
  waiting for transfers between devices: 4.48 us -> 7.66 us
  Pallas kernels: 9.34 us -> 9.91 us
    unnamed x12 -> x2, local copies, waits for them, and re-layouts: 3.63 us -> 0.01 us
    ppermute x1, starting transfers between devices: 2.36 us -> 0.32 us  [local(): inner_back = lax.ppermute(inner, 'col', swap('col', 1))]
    ppermute x3, starting transfers between devices: 4.81 us -> 2.96 us  [physics(): backs[k] = lax.ppermute(backs[k], ('grp', 'col'), partners(k))]
    ppermute x3, waiting for transfers between devices: 2.1 us -> 3.89 us  [physics(): backs[k] = lax.ppermute(backs[k], ('grp', 'col'), partners(k))]
    ppermute x1, waiting for transfers between devices: 0.01 us -> 1.59 us  [local(): far = lax.ppermute(outer, 'row', outward('row'))]
    ppermute x1, starting transfers between devices: 0.27 us -> 1.72 us  [local(): outer_back = lax.ppermute(outer, ('grp', 'col'), outward(('grp', 'col')))]
    ppermute x1, waiting for transfers between devices: 0.01 us -> 1.3 us  [local(): arrived = lax.ppermute(send, 'col', swap('col', 1))]
    ppermute x3, waiting for transfers between devices: 2.16 us -> 0.87 us  [local(): lax.ppermute(s, 'row', swap('row', bit + 1))]
  transfers between devices with their start and end apart: 14 -> 14, of which waited for: 4 -> 4; matrix products, arithmetic and copies ran while one was open for 0% -> 0% of each run, Pallas kernels for 12% -> 22%
where the time goes in v3:
time: 35.5 us; the launch traced here: 35.4 us
  starting transfers between devices  17.1 us (48%)
  Pallas kernels  9.91 us (28%)
  waiting for transfers between devices  7.66 us (22%)
  between operations  0.73 us (2%)
    pallas_call x12, Pallas kernels, call(): pl.pallas_call(body, out_shape=list(outs), in_specs=specs + [ANY] * len(a...  9.91 us
    ppermute x3, starting transfers between devices, local(): got[k] = lax.ppermute(chunks[k], ('grp', 'col'), partners(k))  5.48 us
    ppermute x3, waiting for transfers between devices, physics(): backs[k] = lax.ppermute(backs[k], ('grp', 'col'), partners(k))  3.89 us
    ppermute x3, starting transfers between devices, local(): lax.ppermute(s, 'row', swap('row', bit + 1))  3.55 us
    ppermute x3, starting transfers between devices, physics(): backs[k] = lax.ppermute(backs[k], ('grp', 'col'), partners(k))  2.96 us
    ppermute x1, starting transfers between devices, local(): outer_back = lax.ppermute(outer, ('grp', 'col'), outward(('grp', 'col')))  1.72 us
    ppermute x1, waiting for transfers between devices, local(): far = lax.ppermute(outer, 'row', outward('row'))  1.59 us
    ppermute x1, starting transfers between devices, local(): far = lax.ppermute(outer, 'row', outward('row'))  1.49 us
  transfers between devices with their start and end apart: 14, of which 4 were waited for; matrix products, arithmetic and copies ran while one was open for 0% of the time, Pallas kernels for 22%

profile of v3, /device:TPU:0, one launch (start us, length us, event | category | flops | bytes accessed | tf_op | source)
XLA Modules:
  0.0 35.4 jit_solution(10450568604224985946)
XLA Ops:
  0.6 1.4 %shard_map.85 = (bf16[128,512]{1,0:T(8,128)(2,1)S(1)}, bf16[128,512]{1,0:T(8,128)(2,1)S(1)}, bf16[128,512]{1,0:T(8,128)(2,1)S(1)}, bf16[128,512]{1,0:T(8,128)(2,...) custom-call(s32[1,256]{1,0:T(1,128)} %bitcast.15, ...), custom_call_target="tpu_custom_call" | custom-call | tf_op jit(solution)/shard_map/pallas_call | solution.py:26
  2.0 4.6 %collective-permute-start.4 = (bf16[128,512]{1,0:T(8,128)(2,1)S(1)}, bf16[128,512]{1,0:T(8,128)(2,1)S(1)}, u32[]{:S(2)}, u32[]{:S(2)}) collective-permute-start(bf16[128,512]{1,0:T(8,128)(2,1)S(1)} %get-tuple-element.44), channel_id=1, source_target_pairs={{0,7},{2,1},{4,3},{6,5},{7,0},{1,2},{3,4},{5,6},{8,15},{10,9},{12,... | collective-permute-start | bytes 393224 | tf_op jit(solution)/shard_map/ppermute | solution.py:322
  6.6 0.8 %collective-permute-start.5 = (bf16[128,512]{1,0:T(8,128)(2,1)S(1)}, bf16[128,512]{1,0:T(8,128)(2,1)S(1)}, u32[]{:S(2)}, u32[]{:S(2)}) collective-permute-start(bf16[128,512]{1,0:T(8,128)(2,1)S(1)} %get-tuple-element.45), channel_id=1, source_target_pairs={{0,5},{2,7},{4,1},{6,3},{5,0},{7,2},{1,4},{3,6},{8,13},{10,15},{12... | collective-permute-start | bytes 393224 | tf_op jit(solution)/shard_map/ppermute | solution.py:322
  7.4 0.1 collective-permute-start.6
  7.5 1.5 %collective-permute-start = (bf16[64,384]{1,0:T(8,128)(2,1)S(1)}, bf16[64,384]{1,0:T(8,128)(2,1)S(1)}, u32[]{:S(2)}, u32[]{:S(2)}) collective-permute-start(bf16[64,384]{1,0:T(8,128)(2,1)S(1)} %get-tuple-element.37), channel_id=1, source_target_pairs={{0,8},{8,0},{16,24},{24,16},{1,9},{9,1},{17,25},{25,17},{2,10},{10... | collective-permute-start | bytes 147464 | tf_op jit(solution)/shard_map/ppermute | solution.py:323
  9.0 1.5 %collective-permute-start.1 = (bf16[64,384]{1,0:T(8,128)(2,1)S(1)}, bf16[64,384]{1,0:T(8,128)(2,1)S(1)}, u32[]{:S(2)}, u32[]{:S(2)}) collective-permute-start(bf16[64,384]{1,0:T(8,128)(2,1)S(1)} %get-tuple-element.38), channel_id=1, source_target_pairs={{0,24},{8,16},{16,8},{24,0},{1,25},{9,17},{17,9},{25,1},{2,26},{10... | collective-permute-start | bytes 147464 | tf_op jit(solution)/shard_map/ppermute | solution.py:324
  10.5 0.0 copy-start
  10.5 2.3 %shard_map.86 = (bf16[128,512]{1,0:T(8,128)(2,1)S(1)}, bf16[128,1024]{1,0:T(8,128)(2,1)S(1)}, bf16[128,1024]{1,0:T(8,128)(2,1)S(1)}, bf16[256,1024]{1,0:T(8,128)(2,1)S(1)}, bf16[256,1024]{1,0:T(8,128)(2,1)S(1)}) custom-call(bf16[128,512]{1,0:T(8,128)(2,1)S(1)} %get-tuple-element.40.refs_0_, bf16[256,1024]{1,0:T(8,128)(2,1)} %bitcast.11, ...), custom_call_target="tpu_custom_call" | custom-call | tf_op jit(solution)/shard_map/pallas_call | solution.py:26
  12.8 0.0 collective-permute-done.refs_2_
  12.8 1.6 %collective-permute-done.1.refs_3_ = bf16[64,384]{1,0:T(8,128)(2,1)S(1)} collective-permute-done((bf16[64,384]{1,0:T(8,128)(2,1)S(1)}, bf16[64,384]{1,0:T(8,128)(2,1)S(1)}, u32[]{:S(2)}, u32[]{:S(2)}) %collective-permute-start.1) | collective-permute-done | bytes 49184 | tf_op jit(solution)/shard_map/ppermute | solution.py:324
  14.4 0.0 copy-done
  14.4 0.2 shard_map.87
  14.5 0.3 collective-permute-start.2
  14.9 1.7 %collective-permute-start.3 = (bf16[96,384]{1,0:T(8,128)(2,1)S(1)}, bf16[96,384]{1,0:T(8,128)(2,1)S(1)}, u32[]{:S(2)}, u32[]{:S(2)}) collective-permute-start(bf16[96,384]{1,0:T(8,128)(2,1)S(1)} %get-tuple-element.43), channel_id=1, source_target_pairs={{0,7},{1,2},{2,1},{3,4},{4,3},{5,6},{6,5},{7,0},{8,15},{9,10},{10,... | collective-permute-start | bytes 221192 | tf_op jit(solution)/shard_map/ppermute | solution.py:352
  16.6 0.0 collective-permute-done.4.refs_0_.refs_1_
  16.6 0.9 %shard_map.88 = (bf16[128,512]{1,0:T(8,128)(2,1)S(1)}, bf16[128,1024]{1,0:T(8,128)(2,1)S(1)}, bf16[128,1024]{1,0:T(8,128)(2,1)S(1)}) custom-call(bf16[128,512]{1,0:T(8,128)(2,1)S(1)} %collective-permute-done.4.refs_0_.refs_1_, bf16[256,1024]{1,0:T(8,128)(2,1)S(1)} %get-tuple-element.47.refs_1_, bf16[256,1024]{1,0:T(8,128)(2,1)S(1)} %get-tuple-element.48.refs_2_, ...), custom_call_target="tpu_custom_call" | custom-call | tf_op jit(solution)/shard_map/pallas_call | solution.py:26
  17.5 1.9 %collective-permute-start.8 = (bf16[128,512]{1,0:T(8,128)(2,1)S(1)}, bf16[128,512]{1,0:T(8,128)(2,1)S(1)}, u32[]{:S(2)}, u32[]{:S(2)}) collective-permute-start(bf16[128,512]{1,0:T(8,128)(2,1)S(1)} %get-tuple-element.61), channel_id=1, source_target_pairs={{0,7},{2,1},{4,3},{6,5},{7,0},{1,2},{3,4},{5,6},{8,15},{10,9},{12,... | collective-permute-start | bytes 393224 | tf_op jit(solution)/shard_map/ppermute | solution.py:333
  19.4 0.0 collective-permute-done.5.refs_0_.refs_2_
  19.4 0.9 %shard_map.89 = (bf16[128,512]{1,0:T(8,128)(2,1)S(1)}, bf16[128,1024]{1,0:T(8,128)(2,1)S(1)}, bf16[128,1024]{1,0:T(8,128)(2,1)S(1)}) custom-call(bf16[128,512]{1,0:T(8,128)(2,1)S(1)} %collective-permute-done.5.refs_0_.refs_2_, bf16[256,1024]{1,0:T(8,128)(2,1)S(1)} %get-tuple-element.47.refs_1_, bf16[256,1024]{1,0:T(8,128)(2,1)S(1)} %get-tuple-element.48.refs_2_, ...), custom_call_target="tpu_custom_call" | custom-call | tf_op jit(solution)/shard_map/pallas_call | solution.py:26
  20.3 0.0 collective-permute-done.6.refs_0_.refs_3_
  20.3 0.9 %shard_map.90 = (bf16[128,512]{1,0:T(8,128)(2,1)S(1)}, bf16[128,1024]{1,0:T(8,128)(2,1)S(1)}, bf16[128,1024]{1,0:T(8,128)(2,1)S(1)}) custom-call(bf16[128,512]{1,0:T(8,128)(2,1)S(1)} %collective-permute-done.6.refs_0_.refs_3_, bf16[256,1024]{1,0:T(8,128)(2,1)S(1)} %get-tuple-element.47.refs_1_, bf16[256,1024]{1,0:T(8,128)(2,1)S(1)} %get-tuple-element.48.refs_2_, ...), custom_call_target="tpu_custom_call" | custom-call | tf_op jit(solution)/shard_map/pallas_call | solution.py:26
  21.2 0.8 %shard_map.91 = (f32[2,2,64,1024]{3,2,1,0:T(8,128)S(1)}, bf16[2,2,64,1024]{3,2,1,0:T(8,128)(2,1)S(1)}) custom-call(bf16[128,512]{1,0:T(8,128)(2,1)S(1)} %get-tuple-element.40.refs_0_, bf16[128,512]{1,0:T(8,128)(2,1)S(1)} %collective-permute-done.4.refs_0_.refs_1_, bf16[128,512]{1,0:T(8,128)(2,1)S(1)} %collective-permute-done.5.refs_0_.refs_2_, ...), custom_call_target="tpu_custom_call" | custom-call | tf_op jit(solution)/shard_map/pallas_call | solution.py:26
  22.0 0.1 collective-permute-start.7
  22.0 0.6 %collective-permute-start.9 = (bf16[128,512]{1,0:T(8,128)(2,1)S(1)}, bf16[128,512]{1,0:T(8,128)(2,1)S(1)}, u32[]{:S(2)}, u32[]{:S(2)}) collective-permute-start(bf16[128,512]{1,0:T(8,128)(2,1)S(1)} %get-tuple-element.62), channel_id=1, source_target_pairs={{0,5},{2,7},{4,1},{6,3},{5,0},{7,2},{1,4},{3,6},{8,13},{10,15},{12... | collective-permute-start | bytes 393224 | tf_op jit(solution)/shard_map/ppermute | solution.py:333
  22.6 1.3 %collective-permute-done.7.refs_1_ = bf16[2,2,64,1024]{3,2,1,0:T(8,128)(2,1)S(1)} collective-permute-done((bf16[2,2,64,1024]{3,2,1,0:T(8,128)(2,1)S(1)}, bf16[2,2,64,1024]{3,2,1,0:T(8,128)(2,1)S(1)}, u32[]{:S(2)}, u32[]{:S(2)}) %collective-permute-start.7) | collective-permute-done | bytes 524320 | tf_op jit(solution)/shard_map/ppermute | solution.py:366
  23.9 0.5 %collective-permute-start.10 = (bf16[128,512]{1,0:T(8,128)(2,1)S(1)}, bf16[128,512]{1,0:T(8,128)(2,1)S(1)}, u32[]{:S(2)}, u32[]{:S(2)}) collective-permute-start(bf16[128,512]{1,0:T(8,128)(2,1)S(1)} %get-tuple-element.63), channel_id=1, source_target_pairs={{0,3},{2,5},{4,7},{6,1},{3,0},{5,2},{7,4},{1,6},{8,11},{10,13},{12... | collective-permute-start | bytes 393224 | tf_op jit(solution)/shard_map/ppermute | solution.py:333
  24.4 0.1 shard_map.93
  24.5 0.0 collective-permute-done.2.refs_4_
  24.5 1.3 %collective-permute-start.11 = (bf16[64,1024]{1,0:T(8,128)(2,1)S(1)}, bf16[64,1024]{1,0:T(8,128)(2,1)S(1)}, u32[]{:S(2)}, u32[]{:S(2)}) collective-permute-start(bf16[64,1024]{1,0:T(8,128)(2,1)S(1)} %get-tuple-element.66), channel_id=1, source_target_pairs={{0,8},{8,0},{16,24},{24,16},{1,9},{9,1},{17,25},{25,17},{2,10},{10... | collective-permute-start | bytes 393224 | tf_op jit(solution)/shard_map/ppermute | solution.py:375
  25.8 0.0 collective-permute-done.3.refs_5_
  25.8 1.4 %collective-permute-start.12 = (bf16[64,1024]{1,0:T(8,128)(2,1)S(1)}, bf16[64,1024]{1,0:T(8,128)(2,1)S(1)}, u32[]{:S(2)}, u32[]{:S(2)}) collective-permute-start(bf16[64,1024]{1,0:T(8,128)(2,1)S(1)} %get-tuple-element.67), channel_id=1, source_target_pairs={{0,16},{8,24},{16,0},{24,8},{1,17},{9,25},{17,1},{25,9},{2,18},{10... | collective-permute-start | bytes 393224 | tf_op jit(solution)/shard_map/ppermute | solution.py:375
  27.3 0.0 collective-permute-done.8.refs_3_
  27.3 0.8 %collective-permute-start.13 = (bf16[64,1024]{1,0:T(8,128)(2,1)S(1)}, bf16[64,1024]{1,0:T(8,128)(2,1)S(1)}, u32[]{:S(2)}, u32[]{:S(2)}) collective-permute-start(bf16[64,1024]{1,0:T(8,128)(2,1)S(1)} %get-tuple-element.68), channel_id=1, source_target_pairs={{0,24},{8,16},{16,8},{24,0},{1,25},{9,17},{17,9},{25,1},{2,26},{10... | collective-permute-start | bytes 393224 | tf_op jit(solution)/shard_map/ppermute | solution.py:375
  28.1 0.7 %shard_map.94.refs_0_ = f32[256,256]{1,0:T(8,128)S(1)} custom-call(f32[256,256]{1,0:T(8,128)S(1)} %bitcast.10, f32[256,1]{1,0:T(8,128)S(1)} %get-tuple-element.36.refs_1_, bf16[64,384]{1,0:T(8,128)(2,1)S(1)} %collective-permute-done.refs_2_, bf16[64,384]{1,0:T(8,128)(2,1)S(1)} %collective-permute-done.1.refs_3_, ...), custom_call_target="tpu_custom_call" | custom-call | tf_op jit(solution)/shard_map/pallas_call | solution.py:26
  28.8 3.9 %collective-permute-done.9.refs_4_ = bf16[128,512]{1,0:T(8,128)(2,1)S(1)} collective-permute-done((bf16[128,512]{1,0:T(8,128)(2,1)S(1)}, bf16[128,512]{1,0:T(8,128)(2,1)S(1)}, u32[]{:S(2)}, u32[]{:S(2)}) %collective-permute-start.9) | collective-permute-done | bytes 131104 | tf_op jit(solution)/shard_map/ppermute | solution.py:333
  32.7 0.0 collective-permute-done.10.refs_5_
  32.7 1.1 %shard_map.95 = (f32[256,256]{1,0:T(8,128)}, bf16[256,256]{1,0:T(8,128)(2,1)}) custom-call(f32[256,256]{1,0:T(8,128)S(1)} %shard_map.94.refs_0_, bf16[256,512]{1,0:T(8,128)(2,1)S(1)} %get-tuple-element.49.refs_3_.refs_1_, bf16[128,512]{1,0:T(8,128)(2,1)S(1)} %get-tuple-element.60.refs_2_, bf16[128,512]{1,0:T(8,128)(2,1)S(1)} %collective-permute-done.8.refs_3_, ...), custom_call_target="tpu_custom_call" | custom-call | tf_op jit(solution)/shard_map/pallas_call | solution.py:26
  33.7 0.0 collective-permute-done.11.refs_1_
  33.7 0.0 collective-permute-done.12.refs_2_
  33.7 0.9 %collective-permute-done.13.refs_3_ = bf16[64,1024]{1,0:T(8,128)(2,1)S(1)} collective-permute-done((bf16[64,1024]{1,0:T(8,128)(2,1)S(1)}, bf16[64,1024]{1,0:T(8,128)(2,1)S(1)}, u32[]{:S(2)}, u32[]{:S(2)}) %collective-permute-start.13) | collective-permute-done | bytes 131104 | tf_op jit(solution)/shard_map/ppermute | solution.py:375
  34.6 0.8 %shard_map.96 = f32[512,128]{1,0:T(8,128)} custom-call(f32[64,1024]{1,0:T(8,128)S(1)} %get-tuple-element.59.refs_6_.refs_0_, bf16[64,1024]{1,0:T(8,128)(2,1)S(1)} %collective-permute-done.11.refs_1_, bf16[64,1024]{1,0:T(8,128)(2,1)S(1)} %collective-permute-done.12.refs_2_, bf16[64,1024]{1,0:T(8,128)(2,1)S(1)} %collective-permute-done.13.refs_3_), custom_call_target="tpu_custom_call" | custom-call | tf_op jit(solution)/shard_map/pallas_call | solution.py:26
  (1 shorter events, 0.0 us)
Async XLA Ops:
  2.0 14.6 %collective-permute-start.4 = (bf16[128,512]{1,0:T(8,128)(2,1)S(1)}, bf16[128,512]{1,0:T(8,128)(2,1)S(1)}, u32[]{:S(2)}, u32[]{:S(2)}) collective-permute-start(bf16[128,512]{1,0:T(8,128)(2,1)S(1)} %get-tuple-element.44), channel_id=1, source_target_pairs={{0,7},{2,1},{4,3},{6,5},{7,0},{1,2},{3,4},{5,6},{8,15},{10,9},{12,... | collective-permute-start | bytes 393224 | tf_op jit(solution)/shard_map/ppermute | solution.py:322
  6.6 12.8 %collective-permute-start.5 = (bf16[128,512]{1,0:T(8,128)(2,1)S(1)}, bf16[128,512]{1,0:T(8,128)(2,1)S(1)}, u32[]{:S(2)}, u32[]{:S(2)}) collective-permute-start(bf16[128,512]{1,0:T(8,128)(2,1)S(1)} %get-tuple-element.45), channel_id=1, source_target_pairs={{0,5},{2,7},{4,1},{6,3},{5,0},{7,2},{1,4},{3,6},{8,13},{10,15},{12... | collective-permute-start | bytes 393224 | tf_op jit(solution)/shard_map/ppermute | solution.py:322
  7.4 12.9 %collective-permute-start.6 = (bf16[128,512]{1,0:T(8,128)(2,1)S(1)}, bf16[128,512]{1,0:T(8,128)(2,1)S(1)}, u32[]{:S(2)}, u32[]{:S(2)}) collective-permute-start(bf16[128,512]{1,0:T(8,128)(2,1)S(1)} %get-tuple-element.46), channel_id=1, source_target_pairs={{0,3},{2,5},{4,7},{6,1},{3,0},{5,2},{7,4},{1,6},{8,11},{10,13},{12... | collective-permute-start | bytes 393224 | tf_op jit(solution)/shard_map/ppermute | solution.py:322
  7.5 5.3 %collective-permute-start = (bf16[64,384]{1,0:T(8,128)(2,1)S(1)}, bf16[64,384]{1,0:T(8,128)(2,1)S(1)}, u32[]{:S(2)}, u32[]{:S(2)}) collective-permute-start(bf16[64,384]{1,0:T(8,128)(2,1)S(1)} %get-tuple-element.37), channel_id=1, source_target_pairs={{0,8},{8,0},{16,24},{24,16},{1,9},{9,1},{17,25},{25,17},{2,10},{10... | collective-permute-start | bytes 147464 | tf_op jit(solution)/shard_map/ppermute | solution.py:323
  9.0 5.4 %collective-permute-start.1 = (bf16[64,384]{1,0:T(8,128)(2,1)S(1)}, bf16[64,384]{1,0:T(8,128)(2,1)S(1)}, u32[]{:S(2)}, u32[]{:S(2)}) collective-permute-start(bf16[64,384]{1,0:T(8,128)(2,1)S(1)} %get-tuple-element.38), channel_id=1, source_target_pairs={{0,24},{8,16},{16,8},{24,0},{1,25},{9,17},{17,9},{25,1},{2,26},{10... | collective-permute-start | bytes 147464 | tf_op jit(solution)/shard_map/ppermute | solution.py:324
  10.5 3.9 %copy-start = (f32[16,16,256]{2,1,0:T(8,128)S(1)}, f32[16,16,256]{2,1,0:T(8,128)}, u32[]{:S(2)}) copy-start(f32[16,16,256]{2,1,0:T(8,128)} %param.6) | copy-start | bytes 786436
  14.5 10.0 %collective-permute-start.2 = (bf16[96,384]{1,0:T(8,128)(2,1)S(1)}, bf16[96,384]{1,0:T(8,128)(2,1)S(1)}, u32[]{:S(2)}, u32[]{:S(2)}) collective-permute-start(bf16[96,384]{1,0:T(8,128)(2,1)S(1)} %get-tuple-element.42), channel_id=1, source_target_pairs={{0,1},{1,0},{2,3},{3,2},{4,5},{5,4},{6,7},{7,6},{8,9},{9,8},{10,11... | collective-permute-start | bytes 221192 | tf_op jit(solution)/shard_map/ppermute | solution.py:353
  14.9 11.0 %collective-permute-start.3 = (bf16[96,384]{1,0:T(8,128)(2,1)S(1)}, bf16[96,384]{1,0:T(8,128)(2,1)S(1)}, u32[]{:S(2)}, u32[]{:S(2)}) collective-permute-start(bf16[96,384]{1,0:T(8,128)(2,1)S(1)} %get-tuple-element.43), channel_id=1, source_target_pairs={{0,7},{1,2},{2,1},{3,4},{4,3},{5,6},{6,5},{7,0},{8,15},{9,10},{10,... | collective-permute-start | bytes 221192 | tf_op jit(solution)/shard_map/ppermute | solution.py:352
  17.5 9.8 %collective-permute-start.8 = (bf16[128,512]{1,0:T(8,128)(2,1)S(1)}, bf16[128,512]{1,0:T(8,128)(2,1)S(1)}, u32[]{:S(2)}, u32[]{:S(2)}) collective-permute-start(bf16[128,512]{1,0:T(8,128)(2,1)S(1)} %get-tuple-element.61), channel_id=1, source_target_pairs={{0,7},{2,1},{4,3},{6,5},{7,0},{1,2},{3,4},{5,6},{8,15},{10,9},{12,... | collective-permute-start | bytes 393224 | tf_op jit(solution)/shard_map/ppermute | solution.py:333
  22.0 2.0 %collective-permute-start.7 = (bf16[2,2,64,1024]{3,2,1,0:T(8,128)(2,1)S(1)}, bf16[2,2,64,1024]{3,2,1,0:T(8,128)(2,1)S(1)}, u32[]{:S(2)}, u32[]{:S(2)}) collective-permute-start(bf16[2,2,64,1024]{3,2,1,0:T(8,128)(2,1)S(1)} %get-tuple-element.58), channel_id=1, source_target_pairs={{0,1},{1,0},{2,3},{3,2},{4,5},{5,4},{6,7},{7,6},{8,9},{9,8},{10,11... | collective-permute-start | bytes 1572872 | tf_op jit(solution)/shard_map/ppermute | solution.py:366
  22.0 10.6 %collective-permute-start.9 = (bf16[128,512]{1,0:T(8,128)(2,1)S(1)}, bf16[128,512]{1,0:T(8,128)(2,1)S(1)}, u32[]{:S(2)}, u32[]{:S(2)}) collective-permute-start(bf16[128,512]{1,0:T(8,128)(2,1)S(1)} %get-tuple-element.62), channel_id=1, source_target_pairs={{0,5},{2,7},{4,1},{6,3},{5,0},{7,2},{1,4},{3,6},{8,13},{10,15},{12... | collective-permute-start | bytes 393224 | tf_op jit(solution)/shard_map/ppermute | solution.py:333
  23.9 8.7 %collective-permute-start.10 = (bf16[128,512]{1,0:T(8,128)(2,1)S(1)}, bf16[128,512]{1,0:T(8,128)(2,1)S(1)}, u32[]{:S(2)}, u32[]{:S(2)}) collective-permute-start(bf16[128,512]{1,0:T(8,128)(2,1)S(1)} %get-tuple-element.63), channel_id=1, source_target_pairs={{0,3},{2,5},{4,7},{6,1},{3,0},{5,2},{7,4},{1,6},{8,11},{10,13},{12... | collective-permute-start | bytes 393224 | tf_op jit(solution)/shard_map/ppermute | solution.py:333
  24.5 9.2 %collective-permute-start.11 = (bf16[64,1024]{1,0:T(8,128)(2,1)S(1)}, bf16[64,1024]{1,0:T(8,128)(2,1)S(1)}, u32[]{:S(2)}, u32[]{:S(2)}) collective-permute-start(bf16[64,1024]{1,0:T(8,128)(2,1)S(1)} %get-tuple-element.66), channel_id=1, source_target_pairs={{0,8},{8,0},{16,24},{24,16},{1,9},{9,1},{17,25},{25,17},{2,10},{10... | collective-permute-start | bytes 393224 | tf_op jit(solution)/shard_map/ppermute | solution.py:375
  25.8 7.9 %collective-permute-start.12 = (bf16[64,1024]{1,0:T(8,128)(2,1)S(1)}, bf16[64,1024]{1,0:T(8,128)(2,1)S(1)}, u32[]{:S(2)}, u32[]{:S(2)}) collective-permute-start(bf16[64,1024]{1,0:T(8,128)(2,1)S(1)} %get-tuple-element.67), channel_id=1, source_target_pairs={{0,16},{8,24},{16,0},{24,8},{1,17},{9,25},{17,1},{25,9},{2,18},{10... | collective-permute-start | bytes 393224 | tf_op jit(solution)/shard_map/ppermute | solution.py:375
  27.3 7.3 %collective-permute-start.13 = (bf16[64,1024]{1,0:T(8,128)(2,1)S(1)}, bf16[64,1024]{1,0:T(8,128)(2,1)S(1)}, u32[]{:S(2)}, u32[]{:S(2)}) collective-permute-start(bf16[64,1024]{1,0:T(8,128)(2,1)S(1)} %get-tuple-element.68), channel_id=1, source_target_pairs={{0,24},{8,16},{16,8},{24,0},{1,25},{9,17},{17,9},{25,1},{2,26},{10... | collective-permute-start | bytes 393224 | tf_op jit(solution)/shard_map/ppermute | solution.py:375

commit v4 on v3

--- a/solution.py
+++ b/solution.py
@@ -47,12 +47,12 @@
 
 
 def pack_kernel(owners, cap, wide, high, *refs):
-    far, near, sems = refs[:4], refs[-5:-1], refs[-1]
-    chunks, inner, outer, rate_cols, places = refs[4 : owners + 4], *refs[owners + 4 : -5]
+    far, near, sems = refs[:6], [*refs[-5:-1], *refs[-7:-5]], refs[-1]
+    chunks, inner, outer, rate_cols, places = refs[6 : owners + 6], *refs[owners + 6 : -7]
     copies = [pltpu.make_async_copy(a, b, sems.at[n]) for n, (a, b) in enumerate(zip(far, near))]
     for copy in copies:
         copy.start()
-    dest, rate, state, cot = near
+    dest, rate, state, cot, _, _ = near
     count, feats = state.shape
     copies[0].wait()
     named = lax.broadcasted_iota(jnp.int32, (max(8, owners), count), 0) == dest[...]
@@ -65,7 +65,7 @@
     turn = jnp.where(lax.axis_index("col") == 0, -ahead, ahead)
     place = jnp.where(turn < 0, turn + owners, turn) * cap + slot
     places[...] = place
-    for copy in copies[1:]:
+    for copy in copies[1:4]:
         copy.wait()
     turned = rate[...].T
     for r in range(high):
@@ -83,6 +83,8 @@
         start = pl.multiple_of((1 - top) * (count - strip), strip)
         out[:, :feats] = state[pl.ds(start, strip)].astype(BF16)
         out[:, feats:] = jnp.broadcast_to(rate_cols[pl.ds(start, strip)], (strip, 128)).astype(BF16)
+    for copy in copies[4:]:
+        copy.wait()
 
 
 def edge_kernel(wide, high, state, rate, near, far, place_row, inner, outer, places):
@@ -177,7 +179,7 @@
     cols = chunk[:, :feats]
     dtend = (0.5 * chunk[:, feats:].astype(F32)).astype(BF16)
     tend = adjoint = None
-    piece = 256
+    piece = hidden
     for h in range(0, hidden, piece):
         win, wout = w_in[:, h : h + piece], w_out[:, h : h + piece]
         pre = nn(cols, win)
@@ -194,21 +196,6 @@
     back[:, feats:] = adjoint.astype(BF16)
 
 
-def first_physics_kernel(chunk, w_in_far, w_out_far, back, act_out, dpre_out, w_in, w_out, sems):
-    feats, hidden = w_in.shape
-    piece = feats // 4
-    copies = [
-        pltpu.make_async_copy(far.at[at], near.at[at], sems.at[n, r])
-        for r, at in enumerate(pl.ds(r * piece, piece) for r in range(4))
-        for n, (far, near) in enumerate(((w_in_far, w_in), (w_out_far, w_out)))
-    ]
-    for copy in copies:
-        copy.start()
-    for copy in copies:
-        copy.wait()
-    physics_kernel(chunk, w_in, w_out, back, act_out, dpre_out)
-
-
 def grads_of(chunks, acts, dpres, h, piece, feats):
     dpre = jnp.concatenate([d[:, h : h + piece] for d in dpres], axis=0)
     act = jnp.concatenate([a[:, h : h + piece] for a in acts], axis=0)
@@ -225,7 +212,7 @@
     cots = jnp.concatenate([c[:, feats:] for c in chunks], axis=0)
     dtend = (0.5 * cots.astype(F32)).astype(BF16).T
     core = lax.axis_index("col")
-    piece = 256
+    piece = 512
     for h in range(0, hidden, piece):
         dpre, act = grads_of(chunks, acts, dpres, h, piece, feats)
         for which, total in ((0, nn(cols, dpre)), (1, nn(dtend, act))):
@@ -303,19 +290,20 @@
     flat_state = state.reshape(count, feats)
     flat_cot = cotangent.reshape(count, feats)
 
+    weight = shape((feats, hidden), BF16)
     strip = shape((STEPS * wide, feats + 128), BF16)
-    *chunks, inner, outer, rate_col, place_row = call(
+    *chunks, inner, outer, rate_col, place_row, weight_in, weight_out = call(
         functools.partial(pack_kernel, owners, cap, wide, high),
-        [dest.reshape(1, count), rate, flat_state, flat_cot],
-        [shape((cap, 2 * feats), BF16)] * owners + [strip, strip, shape((count, 1), F32), shape((1, count), jnp.int32)],
+        [dest.reshape(1, count), rate, flat_state, flat_cot, w_in[0], w_out[0]],
+        [shape((cap, 2 * feats), BF16)] * owners + [strip, strip, shape((count, 1), F32), shape((1, count), jnp.int32), weight, weight],
         [
             pltpu.VMEM((1, count), jnp.int32),
             pltpu.VMEM((high, wide), F32),
             pltpu.VMEM((count, feats), F32),
             pltpu.VMEM((count, feats), BF16),
-            pltpu.SemaphoreType.DMA((4,)),
+            pltpu.SemaphoreType.DMA((6,)),
         ],
-        far=(0, 1, 2, 3),
+        far=(0, 1, 2, 3, 4, 5),
     )
     got = [chunks[0]] + [None] * (owners - 1)
     for k in range(owners - 1, 0, -1):
@@ -330,17 +318,11 @@
         backs[k], acts[k], dpres[k] = call(
             physics_kernel, [got[k], weight_in, weight_out], made, after=after
         )
-        backs[k] = lax.ppermute(backs[k], ("grp", "col"), partners(k))
+        if k > 0:
+            backs[k] = lax.ppermute(backs[k], ("grp", "col"), partners(k))
         return (acts[k],)
 
-    weight = shape((feats, hidden), BF16)
-    backs[0], acts[0], dpres[0], weight_in, weight_out = call(
-        first_physics_kernel,
-        [chunks[0], w_in[0], w_out[0]],
-        [shape((cap, 2 * feats), BF16)] + [shape((cap, hidden), BF16)] * 2 + [weight, weight],
-        [pltpu.SemaphoreType.DMA((2, 4))],
-        far=(1, 2),
-    )
+    physics(0)
     done = (acts[0],)
     side = shape(((high + 2 * STEPS) * STEPS, feats + 128), BF16)
     inner, outer, places = call(
@@ -352,7 +334,7 @@
     outer_back = lax.ppermute(outer, ("grp", "col"), outward(("grp", "col")))
     inner_back = lax.ppermute(inner, "col", swap("col", 1))
     done = (places,)
-    for k in (1, 2, 3, *range(4, owners)):
+    for k in (3, 2, 1, *range(4, owners)):
         done = physics(k, done)
 
     parts = lax.axis_size("row") * lax.axis_size("col")

time: 35.5 us -> 34.3 us (0.966)
  Pallas kernels: 9.91 us -> 7.9 us
  starting transfers between devices: 17.1 us -> 18.6 us
  waiting for transfers between devices: 7.66 us -> 6.9 us
    pallas_call x12, Pallas kernels: 9.91 us -> 7.9 us  [call(): pl.pallas_call(body, out_shape=list(outs), in_specs=specs + [ANY] * len(a...]
    ppermute x1, starting transfers between devices: 0.07 us -> 1.39 us  [local(): arrived = lax.ppermute(send, 'col', swap('col', 1))]
    ppermute x3, waiting for transfers between devices: 3.89 us -> 2.82 us  [physics(): backs[k] = lax.ppermute(backs[k], ('grp', 'col'), partners(k))]
    ppermute x1, starting transfers between devices: 1.72 us -> 0.76 us  [local(): outer_back = lax.ppermute(outer, ('grp', 'col'), outward(('grp', 'col')))]
    ppermute x1, waiting for transfers between devices: 1.3 us -> 0.48 us  [local(): arrived = lax.ppermute(send, 'col', swap('col', 1))]
    ppermute x1, waiting for transfers between devices: 1.59 us -> 2.39 us  [local(): far = lax.ppermute(outer, 'row', outward('row'))]
    ppermute x3, starting transfers between devices: 2.96 us -> 3.7 us  [physics(): backs[k] = lax.ppermute(backs[k], ('grp', 'col'), partners(k))]
    ppermute x3, starting transfers between devices: 5.48 us -> 6.19 us  [local(): got[k] = lax.ppermute(chunks[k], ('grp', 'col'), partners(k))]
  transfers between devices with their start and end apart: 14 -> 14, of which waited for: 4 -> 5; matrix products, arithmetic and copies ran while one was open for 0% -> 0% of each run, Pallas kernels for 22% -> 17%
where the time goes in v4:
time: 34.3 us; the launch traced here: 34.2 us
  starting transfers between devices  18.6 us (54%)
  Pallas kernels  7.9 us (23%)
  waiting for transfers between devices  6.9 us (20%)
  between operations  0.72 us (2%)
    pallas_call x12, Pallas kernels, call(): pl.pallas_call(body, out_shape=list(outs), in_specs=specs + [ANY] * len(a...  7.9 us
    ppermute x3, starting transfers between devices, local(): got[k] = lax.ppermute(chunks[k], ('grp', 'col'), partners(k))  6.19 us
    ppermute x3, starting transfers between devices, physics(): backs[k] = lax.ppermute(backs[k], ('grp', 'col'), partners(k))  3.7 us
    ppermute x3, starting transfers between devices, local(): lax.ppermute(s, 'row', swap('row', bit + 1))  3.55 us
    ppermute x3, waiting for transfers between devices, physics(): backs[k] = lax.ppermute(backs[k], ('grp', 'col'), partners(k))  2.82 us
    ppermute x1, waiting for transfers between devices, local(): far = lax.ppermute(outer, 'row', outward('row'))  2.39 us
    ppermute x1, starting transfers between devices, local(): near = lax.ppermute(inner, 'row', swap('row', 1))  1.49 us
    ppermute x1, starting transfers between devices, local(): far = lax.ppermute(outer, 'row', outward('row'))  1.49 us
  transfers between devices with their start and end apart: 14, of which 5 were waited for; matrix products, arithmetic and copies ran while one was open for 0% of the time, Pallas kernels for 17%

profile of v4, /device:TPU:0, one launch (start us, length us, event | category | flops | bytes accessed | tf_op | source)
XLA Modules:
  0.0 34.2 jit_solution(6949787887401246855)
XLA Ops:
  0.6 1.4 %shard_map.85 = (bf16[128,512]{1,0:T(8,128)(2,1)S(1)}, bf16[128,512]{1,0:T(8,128)(2,1)S(1)}, bf16[128,512]{1,0:T(8,128)(2,1)S(1)}, bf16[128,512]{1,0:T(8,128)(2,...) custom-call(s32[1,256]{1,0:T(1,128)} %bitcast.15, ...), custom_call_target="tpu_custom_call" | custom-call | tf_op jit(solution)/shard_map/pallas_call | solution.py:26
  2.1 2.5 %collective-permute-start.6 = (bf16[128,512]{1,0:T(8,128)(2,1)S(1)}, bf16[128,512]{1,0:T(8,128)(2,1)S(1)}, u32[]{:S(2)}, u32[]{:S(2)}) collective-permute-start(bf16[128,512]{1,0:T(8,128)(2,1)S(1)} %get-tuple-element.48), channel_id=1, source_target_pairs={{0,3},{2,5},{4,7},{6,1},{3,0},{5,2},{7,4},{1,6},{8,11},{10,13},{12... | collective-permute-start | bytes 393224 | tf_op jit(solution)/shard_map/ppermute | solution.py:310
  4.6 1.7 %collective-permute-start.5 = (bf16[128,512]{1,0:T(8,128)(2,1)S(1)}, bf16[128,512]{1,0:T(8,128)(2,1)S(1)}, u32[]{:S(2)}, u32[]{:S(2)}) collective-permute-start(bf16[128,512]{1,0:T(8,128)(2,1)S(1)} %get-tuple-element.47), channel_id=1, source_target_pairs={{0,5},{2,7},{4,1},{6,3},{5,0},{7,2},{1,4},{3,6},{8,13},{10,15},{12... | collective-permute-start | bytes 393224 | tf_op jit(solution)/shard_map/ppermute | solution.py:310
  6.3 1.9 %collective-permute-start.4 = (bf16[128,512]{1,0:T(8,128)(2,1)S(1)}, bf16[128,512]{1,0:T(8,128)(2,1)S(1)}, u32[]{:S(2)}, u32[]{:S(2)}) collective-permute-start(bf16[128,512]{1,0:T(8,128)(2,1)S(1)} %get-tuple-element.46), channel_id=1, source_target_pairs={{0,7},{2,1},{4,3},{6,5},{7,0},{1,2},{3,4},{5,6},{8,15},{10,9},{12,... | collective-permute-start | bytes 393224 | tf_op jit(solution)/shard_map/ppermute | solution.py:310
  8.3 1.5 %collective-permute-start = (bf16[64,384]{1,0:T(8,128)(2,1)S(1)}, bf16[64,384]{1,0:T(8,128)(2,1)S(1)}, u32[]{:S(2)}, u32[]{:S(2)}) collective-permute-start(bf16[64,384]{1,0:T(8,128)(2,1)S(1)} %get-tuple-element.37), channel_id=1, source_target_pairs={{0,8},{8,0},{16,24},{24,16},{1,9},{9,1},{17,25},{25,17},{2,10},{10... | collective-permute-start | bytes 147464 | tf_op jit(solution)/shard_map/ppermute | solution.py:311
  9.7 1.5 %collective-permute-start.1 = (bf16[64,384]{1,0:T(8,128)(2,1)S(1)}, bf16[64,384]{1,0:T(8,128)(2,1)S(1)}, u32[]{:S(2)}, u32[]{:S(2)}) collective-permute-start(bf16[64,384]{1,0:T(8,128)(2,1)S(1)} %get-tuple-element.38), channel_id=1, source_target_pairs={{0,24},{8,16},{16,8},{24,0},{1,25},{9,17},{17,9},{25,1},{2,26},{10... | collective-permute-start | bytes 147464 | tf_op jit(solution)/shard_map/ppermute | solution.py:312
  11.2 0.0 copy-start
  11.2 0.7 %shard_map.86 = (bf16[128,512]{1,0:T(8,128)(2,1)S(1)}, bf16[128,1024]{1,0:T(8,128)(2,1)S(1)}, bf16[128,1024]{1,0:T(8,128)(2,1)S(1)}) custom-call(bf16[128,512]{1,0:T(8,128)(2,1)S(1)} %get-tuple-element.40.refs_0_, bf16[256,1024]{1,0:T(8,128)(2,1)S(1)} %get-tuple-element.41.refs_1_, bf16[256,1024]{1,0:T(8,128)(2,1)S(1)} %get-tuple-element.42.refs_2_), custom_call_target="tpu_custom_call" | custom-call | tf_op jit(solution)/shard_map/pallas_call | solution.py:26
  12.0 0.4 %collective-permute-done.refs_2_ = bf16[64,384]{1,0:T(8,128)(2,1)S(1)} collective-permute-done((bf16[64,384]{1,0:T(8,128)(2,1)S(1)}, bf16[64,384]{1,0:T(8,128)(2,1)S(1)}, u32[]{:S(2)}, u32[]{:S(2)}) %collective-permute-start) | collective-permute-done | bytes 49184 | tf_op jit(solution)/shard_map/ppermute | solution.py:311
  12.3 2.4 %collective-permute-done.1.refs_3_ = bf16[64,384]{1,0:T(8,128)(2,1)S(1)} collective-permute-done((bf16[64,384]{1,0:T(8,128)(2,1)S(1)}, bf16[64,384]{1,0:T(8,128)(2,1)S(1)}, u32[]{:S(2)}, u32[]{:S(2)}) %collective-permute-start.1) | collective-permute-done | bytes 49184 | tf_op jit(solution)/shard_map/ppermute | solution.py:312
  14.7 0.0 copy-done
  14.7 0.2 shard_map.87
  14.9 0.1 collective-permute-start.2
  15.0 0.8 %collective-permute-start.3 = (bf16[96,384]{1,0:T(8,128)(2,1)S(1)}, bf16[96,384]{1,0:T(8,128)(2,1)S(1)}, u32[]{:S(2)}, u32[]{:S(2)}) collective-permute-start(bf16[96,384]{1,0:T(8,128)(2,1)S(1)} %get-tuple-element.45), channel_id=1, source_target_pairs={{0,7},{1,2},{2,1},{3,4},{4,3},{5,6},{6,5},{7,0},{8,15},{9,10},{10,... | collective-permute-start | bytes 221192 | tf_op jit(solution)/shard_map/ppermute | solution.py:334
  15.8 0.0 collective-permute-done.6.refs_0_.refs_3_
  15.8 0.7 %shard_map.88 = (bf16[128,512]{1,0:T(8,128)(2,1)S(1)}, bf16[128,1024]{1,0:T(8,128)(2,1)S(1)}, bf16[128,1024]{1,0:T(8,128)(2,1)S(1)}) custom-call(bf16[128,512]{1,0:T(8,128)(2,1)S(1)} %collective-permute-done.6.refs_0_.refs_3_, bf16[256,1024]{1,0:T(8,128)(2,1)S(1)} %get-tuple-element.41.refs_1_, bf16[256,1024]{1,0:T(8,128)(2,1)S(1)} %get-tuple-element.42.refs_2_, ...), custom_call_target="tpu_custom_call" | custom-call | tf_op jit(solution)/shard_map/pallas_call | solution.py:26
  16.5 1.2 %collective-permute-start.10 = (bf16[128,512]{1,0:T(8,128)(2,1)S(1)}, bf16[128,512]{1,0:T(8,128)(2,1)S(1)}, u32[]{:S(2)}, u32[]{:S(2)}) collective-permute-start(bf16[128,512]{1,0:T(8,128)(2,1)S(1)} %get-tuple-element.63), channel_id=1, source_target_pairs={{0,3},{2,5},{4,7},{6,1},{3,0},{5,2},{7,4},{1,6},{8,11},{10,13},{12... | collective-permute-start | bytes 393224 | tf_op jit(solution)/shard_map/ppermute | solution.py:322
  17.7 0.0 collective-permute-done.5.refs_0_.refs_2_
  17.7 0.7 %shard_map.89 = (bf16[128,512]{1,0:T(8,128)(2,1)S(1)}, bf16[128,1024]{1,0:T(8,128)(2,1)S(1)}, bf16[128,1024]{1,0:T(8,128)(2,1)S(1)}) custom-call(bf16[128,512]{1,0:T(8,128)(2,1)S(1)} %collective-permute-done.5.refs_0_.refs_2_, bf16[256,1024]{1,0:T(8,128)(2,1)S(1)} %get-tuple-element.41.refs_1_, bf16[256,1024]{1,0:T(8,128)(2,1)S(1)} %get-tuple-element.42.refs_2_, ...), custom_call_target="tpu_custom_call" | custom-call | tf_op jit(solution)/shard_map/pallas_call | solution.py:26
  18.4 0.0 collective-permute-done.4.refs_0_.refs_1_
  18.5 0.7 %shard_map.90 = (bf16[128,512]{1,0:T(8,128)(2,1)S(1)}, bf16[128,1024]{1,0:T(8,128)(2,1)S(1)}, bf16[128,1024]{1,0:T(8,128)(2,1)S(1)}) custom-call(bf16[128,512]{1,0:T(8,128)(2,1)S(1)} %collective-permute-done.4.refs_0_.refs_1_, bf16[256,1024]{1,0:T(8,128)(2,1)S(1)} %get-tuple-element.41.refs_1_, bf16[256,1024]{1,0:T(8,128)(2,1)S(1)} %get-tuple-element.42.refs_2_, ...), custom_call_target="tpu_custom_call" | custom-call | tf_op jit(solution)/shard_map/pallas_call | solution.py:26
  19.2 0.8 %shard_map.91 = (f32[2,2,64,1024]{3,2,1,0:T(8,128)S(1)}, bf16[2,2,64,1024]{3,2,1,0:T(8,128)(2,1)S(1)}) custom-call(bf16[128,512]{1,0:T(8,128)(2,1)S(1)} %get-tuple-element.40.refs_0_, bf16[128,512]{1,0:T(8,128)(2,1)S(1)} %collective-permute-done.4.refs_0_.refs_1_, bf16[128,512]{1,0:T(8,128)(2,1)S(1)} %collective-permute-done.5.refs_0_.refs_2_, ...), custom_call_target="tpu_custom_call" | custom-call | tf_op jit(solution)/shard_map/pallas_call | solution.py:26
  20.0 1.4 %collective-permute-start.7 = (bf16[2,2,64,1024]{3,2,1,0:T(8,128)(2,1)S(1)}, bf16[2,2,64,1024]{3,2,1,0:T(8,128)(2,1)S(1)}, u32[]{:S(2)}, u32[]{:S(2)}) collective-permute-start(bf16[2,2,64,1024]{3,2,1,0:T(8,128)(2,1)S(1)} %get-tuple-element.58), channel_id=1, source_target_pairs={{0,1},{1,0},{2,3},{3,2},{4,5},{5,4},{6,7},{7,6},{8,9},{9,8},{10,11... | collective-permute-start | bytes 1572872 | tf_op jit(solution)/shard_map/ppermute | solution.py:348
  21.4 1.1 %collective-permute-start.9 = (bf16[128,512]{1,0:T(8,128)(2,1)S(1)}, bf16[128,512]{1,0:T(8,128)(2,1)S(1)}, u32[]{:S(2)}, u32[]{:S(2)}) collective-permute-start(bf16[128,512]{1,0:T(8,128)(2,1)S(1)} %get-tuple-element.62), channel_id=1, source_target_pairs={{0,5},{2,7},{4,1},{6,3},{5,0},{7,2},{1,4},{3,6},{8,13},{10,15},{12... | collective-permute-start | bytes 393224 | tf_op jit(solution)/shard_map/ppermute | solution.py:322
  22.4 0.5 %collective-permute-done.7.refs_1_ = bf16[2,2,64,1024]{3,2,1,0:T(8,128)(2,1)S(1)} collective-permute-done((bf16[2,2,64,1024]{3,2,1,0:T(8,128)(2,1)S(1)}, bf16[2,2,64,1024]{3,2,1,0:T(8,128)(2,1)S(1)}, u32[]{:S(2)}, u32[]{:S(2)}) %collective-permute-start.7) | collective-permute-done | bytes 524320 | tf_op jit(solution)/shard_map/ppermute | solution.py:348
  22.9 1.4 %collective-permute-start.8 = (bf16[128,512]{1,0:T(8,128)(2,1)S(1)}, bf16[128,512]{1,0:T(8,128)(2,1)S(1)}, u32[]{:S(2)}, u32[]{:S(2)}) collective-permute-start(bf16[128,512]{1,0:T(8,128)(2,1)S(1)} %get-tuple-element.61), channel_id=1, source_target_pairs={{0,7},{2,1},{4,3},{6,5},{7,0},{1,2},{3,4},{5,6},{8,15},{10,9},{12,... | collective-permute-start | bytes 393224 | tf_op jit(solution)/shard_map/ppermute | solution.py:322
  24.3 0.1 shard_map.93
  24.4 0.0 collective-permute-done.2.refs_4_
  24.4 1.2 %collective-permute-start.11 = (bf16[64,1024]{1,0:T(8,128)(2,1)S(1)}, bf16[64,1024]{1,0:T(8,128)(2,1)S(1)}, u32[]{:S(2)}, u32[]{:S(2)}) collective-permute-start(bf16[64,1024]{1,0:T(8,128)(2,1)S(1)} %get-tuple-element.66), channel_id=1, source_target_pairs={{0,8},{8,0},{16,24},{24,16},{1,9},{9,1},{17,25},{25,17},{2,10},{10... | collective-permute-start | bytes 393224 | tf_op jit(solution)/shard_map/ppermute | solution.py:357
  25.6 0.0 collective-permute-done.3.refs_5_
  25.6 1.5 %collective-permute-start.12 = (bf16[64,1024]{1,0:T(8,128)(2,1)S(1)}, bf16[64,1024]{1,0:T(8,128)(2,1)S(1)}, u32[]{:S(2)}, u32[]{:S(2)}) collective-permute-start(bf16[64,1024]{1,0:T(8,128)(2,1)S(1)} %get-tuple-element.67), channel_id=1, source_target_pairs={{0,16},{8,24},{16,0},{24,8},{1,17},{9,25},{17,1},{25,9},{2,18},{10... | collective-permute-start | bytes 393224 | tf_op jit(solution)/shard_map/ppermute | solution.py:357
  27.1 0.0 collective-permute-done.10.refs_5_
  27.1 0.9 %collective-permute-start.13 = (bf16[64,1024]{1,0:T(8,128)(2,1)S(1)}, bf16[64,1024]{1,0:T(8,128)(2,1)S(1)}, u32[]{:S(2)}, u32[]{:S(2)}) collective-permute-start(bf16[64,1024]{1,0:T(8,128)(2,1)S(1)} %get-tuple-element.68), channel_id=1, source_target_pairs={{0,24},{8,16},{16,8},{24,0},{1,25},{9,17},{17,9},{25,1},{2,26},{10... | collective-permute-start | bytes 393224 | tf_op jit(solution)/shard_map/ppermute | solution.py:357
  28.0 0.7 %shard_map.94.refs_0_ = f32[256,256]{1,0:T(8,128)S(1)} custom-call(f32[256,256]{1,0:T(8,128)S(1)} %bitcast.10, f32[256,1]{1,0:T(8,128)S(1)} %get-tuple-element.36.refs_1_, bf16[64,384]{1,0:T(8,128)(2,1)S(1)} %collective-permute-done.refs_2_, bf16[64,384]{1,0:T(8,128)(2,1)S(1)} %collective-permute-done.1.refs_3_, ...), custom_call_target="tpu_custom_call" | custom-call | tf_op jit(solution)/shard_map/pallas_call | solution.py:26
  28.7 2.8 %collective-permute-done.9.refs_4_ = bf16[128,512]{1,0:T(8,128)(2,1)S(1)} collective-permute-done((bf16[128,512]{1,0:T(8,128)(2,1)S(1)}, bf16[128,512]{1,0:T(8,128)(2,1)S(1)}, u32[]{:S(2)}, u32[]{:S(2)}) %collective-permute-start.9) | collective-permute-done | bytes 131104 | tf_op jit(solution)/shard_map/ppermute | solution.py:322
  31.5 0.0 collective-permute-done.8.refs_3_
  31.5 1.1 %shard_map.95 = (f32[256,256]{1,0:T(8,128)}, bf16[256,256]{1,0:T(8,128)(2,1)}) custom-call(f32[256,256]{1,0:T(8,128)S(1)} %shard_map.94.refs_0_, bf16[256,512]{1,0:T(8,128)(2,1)S(1)} %get-tuple-element.49.refs_3_.refs_1_, bf16[128,512]{1,0:T(8,128)(2,1)S(1)} %get-tuple-element.60.refs_2_, bf16[128,512]{1,0:T(8,128)(2,1)S(1)} %collective-permute-done.8.refs_3_, ...), custom_call_target="tpu_custom_call" | custom-call | tf_op jit(solution)/shard_map/pallas_call | solution.py:26
  32.6 0.0 collective-permute-done.11.refs_1_
  32.6 0.8 %collective-permute-done.12.refs_2_ = bf16[64,1024]{1,0:T(8,128)(2,1)S(1)} collective-permute-done((bf16[64,1024]{1,0:T(8,128)(2,1)S(1)}, bf16[64,1024]{1,0:T(8,128)(2,1)S(1)}, u32[]{:S(2)}, u32[]{:S(2)}) %collective-permute-start.12) | collective-permute-done | bytes 131104 | tf_op jit(solution)/shard_map/ppermute | solution.py:357
  33.4 0.0 collective-permute-done.13.refs_3_
  33.4 0.8 %shard_map.96 = f32[512,128]{1,0:T(8,128)} custom-call(f32[64,1024]{1,0:T(8,128)S(1)} %get-tuple-element.59.refs_6_.refs_0_, bf16[64,1024]{1,0:T(8,128)(2,1)S(1)} %collective-permute-done.11.refs_1_, bf16[64,1024]{1,0:T(8,128)(2,1)S(1)} %collective-permute-done.12.refs_2_, bf16[64,1024]{1,0:T(8,128)(2,1)S(1)} %collective-permute-done.13.refs_3_), custom_call_target="tpu_custom_call" | custom-call | tf_op jit(solution)/shard_map/pallas_call | solution.py:26
  (1 shorter events, 0.0 us)
Async XLA Ops:
  2.1 13.7 %collective-permute-start.6 = (bf16[128,512]{1,0:T(8,128)(2,1)S(1)}, bf16[128,512]{1,0:T(8,128)(2,1)S(1)}, u32[]{:S(2)}, u32[]{:S(2)}) collective-permute-start(bf16[128,512]{1,0:T(8,128)(2,1)S(1)} %get-tuple-element.48), channel_id=1, source_target_pairs={{0,3},{2,5},{4,7},{6,1},{3,0},{5,2},{7,4},{1,6},{8,11},{10,13},{12... | collective-permute-start | bytes 393224 | tf_op jit(solution)/shard_map/ppermute | solution.py:310
  4.6 13.1 %collective-permute-start.5 = (bf16[128,512]{1,0:T(8,128)(2,1)S(1)}, bf16[128,512]{1,0:T(8,128)(2,1)S(1)}, u32[]{:S(2)}, u32[]{:S(2)}) collective-permute-start(bf16[128,512]{1,0:T(8,128)(2,1)S(1)} %get-tuple-element.47), channel_id=1, source_target_pairs={{0,5},{2,7},{4,1},{6,3},{5,0},{7,2},{1,4},{3,6},{8,13},{10,15},{12... | collective-permute-start | bytes 393224 | tf_op jit(solution)/shard_map/ppermute | solution.py:310
  6.3 12.1 %collective-permute-start.4 = (bf16[128,512]{1,0:T(8,128)(2,1)S(1)}, bf16[128,512]{1,0:T(8,128)(2,1)S(1)}, u32[]{:S(2)}, u32[]{:S(2)}) collective-permute-start(bf16[128,512]{1,0:T(8,128)(2,1)S(1)} %get-tuple-element.46), channel_id=1, source_target_pairs={{0,7},{2,1},{4,3},{6,5},{7,0},{1,2},{3,4},{5,6},{8,15},{10,9},{12,... | collective-permute-start | bytes 393224 | tf_op jit(solution)/shard_map/ppermute | solution.py:310
  8.3 4.1 %collective-permute-start = (bf16[64,384]{1,0:T(8,128)(2,1)S(1)}, bf16[64,384]{1,0:T(8,128)(2,1)S(1)}, u32[]{:S(2)}, u32[]{:S(2)}) collective-permute-start(bf16[64,384]{1,0:T(8,128)(2,1)S(1)} %get-tuple-element.37), channel_id=1, source_target_pairs={{0,8},{8,0},{16,24},{24,16},{1,9},{9,1},{17,25},{25,17},{2,10},{10... | collective-permute-start | bytes 147464 | tf_op jit(solution)/shard_map/ppermute | solution.py:311
  9.7 5.0 %collective-permute-start.1 = (bf16[64,384]{1,0:T(8,128)(2,1)S(1)}, bf16[64,384]{1,0:T(8,128)(2,1)S(1)}, u32[]{:S(2)}, u32[]{:S(2)}) collective-permute-start(bf16[64,384]{1,0:T(8,128)(2,1)S(1)} %get-tuple-element.38), channel_id=1, source_target_pairs={{0,24},{8,16},{16,8},{24,0},{1,25},{9,17},{17,9},{25,1},{2,26},{10... | collective-permute-start | bytes 147464 | tf_op jit(solution)/shard_map/ppermute | solution.py:312
  11.2 3.5 %copy-start = (f32[16,16,256]{2,1,0:T(8,128)S(1)}, f32[16,16,256]{2,1,0:T(8,128)}, u32[]{:S(2)}) copy-start(f32[16,16,256]{2,1,0:T(8,128)} %param.6) | copy-start | bytes 786436
  14.9 9.5 %collective-permute-start.2 = (bf16[96,384]{1,0:T(8,128)(2,1)S(1)}, bf16[96,384]{1,0:T(8,128)(2,1)S(1)}, u32[]{:S(2)}, u32[]{:S(2)}) collective-permute-start(bf16[96,384]{1,0:T(8,128)(2,1)S(1)} %get-tuple-element.44), channel_id=1, source_target_pairs={{0,1},{1,0},{2,3},{3,2},{4,5},{5,4},{6,7},{7,6},{8,9},{9,8},{10,11... | collective-permute-start | bytes 221192 | tf_op jit(solution)/shard_map/ppermute | solution.py:335
  15.0 10.6 %collective-permute-start.3 = (bf16[96,384]{1,0:T(8,128)(2,1)S(1)}, bf16[96,384]{1,0:T(8,128)(2,1)S(1)}, u32[]{:S(2)}, u32[]{:S(2)}) collective-permute-start(bf16[96,384]{1,0:T(8,128)(2,1)S(1)} %get-tuple-element.45), channel_id=1, source_target_pairs={{0,7},{1,2},{2,1},{3,4},{4,3},{5,6},{6,5},{7,0},{8,15},{9,10},{10,... | collective-permute-start | bytes 221192 | tf_op jit(solution)/shard_map/ppermute | solution.py:334
  16.5 10.6 %collective-permute-start.10 = (bf16[128,512]{1,0:T(8,128)(2,1)S(1)}, bf16[128,512]{1,0:T(8,128)(2,1)S(1)}, u32[]{:S(2)}, u32[]{:S(2)}) collective-permute-start(bf16[128,512]{1,0:T(8,128)(2,1)S(1)} %get-tuple-element.63), channel_id=1, source_target_pairs={{0,3},{2,5},{4,7},{6,1},{3,0},{5,2},{7,4},{1,6},{8,11},{10,13},{12... | collective-permute-start | bytes 393224 | tf_op jit(solution)/shard_map/ppermute | solution.py:322
  20.0 2.9 %collective-permute-start.7 = (bf16[2,2,64,1024]{3,2,1,0:T(8,128)(2,1)S(1)}, bf16[2,2,64,1024]{3,2,1,0:T(8,128)(2,1)S(1)}, u32[]{:S(2)}, u32[]{:S(2)}) collective-permute-start(bf16[2,2,64,1024]{3,2,1,0:T(8,128)(2,1)S(1)} %get-tuple-element.58), channel_id=1, source_target_pairs={{0,1},{1,0},{2,3},{3,2},{4,5},{5,4},{6,7},{7,6},{8,9},{9,8},{10,11... | collective-permute-start | bytes 1572872 | tf_op jit(solution)/shard_map/ppermute | solution.py:348
  21.4 10.1 %collective-permute-start.9 = (bf16[128,512]{1,0:T(8,128)(2,1)S(1)}, bf16[128,512]{1,0:T(8,128)(2,1)S(1)}, u32[]{:S(2)}, u32[]{:S(2)}) collective-permute-start(bf16[128,512]{1,0:T(8,128)(2,1)S(1)} %get-tuple-element.62), channel_id=1, source_target_pairs={{0,5},{2,7},{4,1},{6,3},{5,0},{7,2},{1,4},{3,6},{8,13},{10,15},{12... | collective-permute-start | bytes 393224 | tf_op jit(solution)/shard_map/ppermute | solution.py:322
  22.9 8.6 %collective-permute-start.8 = (bf16[128,512]{1,0:T(8,128)(2,1)S(1)}, bf16[128,512]{1,0:T(8,128)(2,1)S(1)}, u32[]{:S(2)}, u32[]{:S(2)}) collective-permute-start(bf16[128,512]{1,0:T(8,128)(2,1)S(1)} %get-tuple-element.61), channel_id=1, source_target_pairs={{0,7},{2,1},{4,3},{6,5},{7,0},{1,2},{3,4},{5,6},{8,15},{10,9},{12,... | collective-permute-start | bytes 393224 | tf_op jit(solution)/shard_map/ppermute | solution.py:322
  24.4 8.1 %collective-permute-start.11 = (bf16[64,1024]{1,0:T(8,128)(2,1)S(1)}, bf16[64,1024]{1,0:T(8,128)(2,1)S(1)}, u32[]{:S(2)}, u32[]{:S(2)}) collective-permute-start(bf16[64,1024]{1,0:T(8,128)(2,1)S(1)} %get-tuple-element.66), channel_id=1, source_target_pairs={{0,8},{8,0},{16,24},{24,16},{1,9},{9,1},{17,25},{25,17},{2,10},{10... | collective-permute-start | bytes 393224 | tf_op jit(solution)/shard_map/ppermute | solution.py:357
  25.6 7.8 %collective-permute-start.12 = (bf16[64,1024]{1,0:T(8,128)(2,1)S(1)}, bf16[64,1024]{1,0:T(8,128)(2,1)S(1)}, u32[]{:S(2)}, u32[]{:S(2)}) collective-permute-start(bf16[64,1024]{1,0:T(8,128)(2,1)S(1)} %get-tuple-element.67), channel_id=1, source_target_pairs={{0,16},{8,24},{16,0},{24,8},{1,17},{9,25},{17,1},{25,9},{2,18},{10... | collective-permute-start | bytes 393224 | tf_op jit(solution)/shard_map/ppermute | solution.py:357
  27.1 6.3 %collective-permute-start.13 = (bf16[64,1024]{1,0:T(8,128)(2,1)S(1)}, bf16[64,1024]{1,0:T(8,128)(2,1)S(1)}, u32[]{:S(2)}, u32[]{:S(2)}) collective-permute-start(bf16[64,1024]{1,0:T(8,128)(2,1)S(1)} %get-tuple-element.68), channel_id=1, source_target_pairs={{0,24},{8,16},{16,8},{24,0},{1,25},{9,17},{17,9},{25,1},{2,26},{10... | collective-permute-start | bytes 393224 | tf_op jit(solution)/shard_map/ppermute | solution.py:357

commit v5 on v4

--- a/solution.py
+++ b/solution.py
@@ -245,7 +245,7 @@
     row = lax.axis_index("row")
     y, x = lax.div(row, 2), lax.rem(row, 2)
     mine[...] = keep[y, x] + got[y, x].astype(F32)
-    for send, (dy, dx) in zip(sends, ((0, 1), (1, 0), (1, 1))):
+    for send, (dy, dx) in zip(sends, ((1, 1), (0, 1), (1, 0))):
         send[...] = (keep[y ^ dy, x ^ dx] + got[y ^ dy, x ^ dx].astype(F32)).astype(BF16)
 
 
@@ -308,8 +308,8 @@
     got = [chunks[0]] + [None] * (owners - 1)
     for k in range(owners - 1, 0, -1):
         got[k] = lax.ppermute(chunks[k], ("grp", "col"), partners(k))
+    far = lax.ppermute(outer, "row", outward("row"))
     near = lax.ppermute(inner, "row", swap("row", 1))
-    far = lax.ppermute(outer, "row", outward("row"))
 
     backs, acts, dpres = [None] * owners, [None] * owners, [None] * owners
 
@@ -354,7 +354,7 @@
             after=(gap,),
         )
         done = (mine,)
-        shares = [lax.ppermute(s, "row", swap("row", bit + 1)) for bit, s in enumerate(shares)]
+        shares = [lax.ppermute(s, "row", swap("row", bit)) for bit, s in zip((3, 1, 2), shares)]
         (summed,) = call(
             gather_kernel, [mine, *shares], [shape((block * hidden // 128, 128), F32)]
         )

time: 34.3 us -> 33.8 us (0.985)
  waiting for transfers between devices: 6.9 us -> 6.4 us
    ppermute x3, waiting for transfers between devices: 0.82 us -> 0.33 us  [local(): lax.ppermute(s, 'row', swap('row', bit))]
  transfers between devices with their start and end apart: 14 -> 14, of which waited for: 5 -> 6; matrix products, arithmetic and copies ran while one was open for 0% -> 0% of each run, Pallas kernels for 17% -> 17%
where the time goes in v5:
time: 33.8 us; the launch traced here: 33.7 us
  starting transfers between devices  18.6 us (55%)
  Pallas kernels  7.9 us (23%)
  waiting for transfers between devices  6.4 us (19%)
  between operations  0.72 us (2%)
    pallas_call x12, Pallas kernels, call(): pl.pallas_call(body, out_shape=list(outs), in_specs=specs + [ANY] * len(a...  7.9 us
    ppermute x3, starting transfers between devices, local(): got[k] = lax.ppermute(chunks[k], ('grp', 'col'), partners(k))  6.19 us
    ppermute x3, starting transfers between devices, physics(): backs[k] = lax.ppermute(backs[k], ('grp', 'col'), partners(k))  3.7 us
    ppermute x3, starting transfers between devices, local(): lax.ppermute(s, 'row', swap('row', bit))  3.55 us
    ppermute x3, waiting for transfers between devices, physics(): backs[k] = lax.ppermute(backs[k], ('grp', 'col'), partners(k))  2.82 us
    ppermute x1, waiting for transfers between devices, local(): far = lax.ppermute(outer, 'row', outward('row'))  2.39 us
    ppermute x1, starting transfers between devices, local(): near = lax.ppermute(inner, 'row', swap('row', 1))  1.49 us
    ppermute x1, starting transfers between devices, local(): far = lax.ppermute(outer, 'row', outward('row'))  1.49 us
  transfers between devices with their start and end apart: 14, of which 6 were waited for; matrix products, arithmetic and copies ran while one was open for 0% of the time, Pallas kernels for 17%

profile of v5, /device:TPU:0, one launch (start us, length us, event | category | flops | bytes accessed | tf_op | source)
XLA Modules:
  0.0 33.7 jit_solution(3793965768021606417)
XLA Ops:
  0.6 1.4 %shard_map.85 = (bf16[128,512]{1,0:T(8,128)(2,1)S(1)}, bf16[128,512]{1,0:T(8,128)(2,1)S(1)}, bf16[128,512]{1,0:T(8,128)(2,1)S(1)}, bf16[128,512]{1,0:T(8,128)(2,...) custom-call(s32[1,256]{1,0:T(1,128)} %bitcast.15, ...), custom_call_target="tpu_custom_call" | custom-call | tf_op jit(solution)/shard_map/pallas_call | solution.py:26
  2.1 2.5 %collective-permute-start.6 = (bf16[128,512]{1,0:T(8,128)(2,1)S(1)}, bf16[128,512]{1,0:T(8,128)(2,1)S(1)}, u32[]{:S(2)}, u32[]{:S(2)}) collective-permute-start(bf16[128,512]{1,0:T(8,128)(2,1)S(1)} %get-tuple-element.48), channel_id=1, source_target_pairs={{0,3},{2,5},{4,7},{6,1},{3,0},{5,2},{7,4},{1,6},{8,11},{10,13},{12... | collective-permute-start | bytes 393224 | tf_op jit(solution)/shard_map/ppermute | solution.py:310
  4.6 1.7 %collective-permute-start.5 = (bf16[128,512]{1,0:T(8,128)(2,1)S(1)}, bf16[128,512]{1,0:T(8,128)(2,1)S(1)}, u32[]{:S(2)}, u32[]{:S(2)}) collective-permute-start(bf16[128,512]{1,0:T(8,128)(2,1)S(1)} %get-tuple-element.47), channel_id=1, source_target_pairs={{0,5},{2,7},{4,1},{6,3},{5,0},{7,2},{1,4},{3,6},{8,13},{10,15},{12... | collective-permute-start | bytes 393224 | tf_op jit(solution)/shard_map/ppermute | solution.py:310
  6.3 1.9 %collective-permute-start.4 = (bf16[128,512]{1,0:T(8,128)(2,1)S(1)}, bf16[128,512]{1,0:T(8,128)(2,1)S(1)}, u32[]{:S(2)}, u32[]{:S(2)}) collective-permute-start(bf16[128,512]{1,0:T(8,128)(2,1)S(1)} %get-tuple-element.46), channel_id=1, source_target_pairs={{0,7},{2,1},{4,3},{6,5},{7,0},{1,2},{3,4},{5,6},{8,15},{10,9},{12,... | collective-permute-start | bytes 393224 | tf_op jit(solution)/shard_map/ppermute | solution.py:310
  8.3 1.5 %collective-permute-start = (bf16[64,384]{1,0:T(8,128)(2,1)S(1)}, bf16[64,384]{1,0:T(8,128)(2,1)S(1)}, u32[]{:S(2)}, u32[]{:S(2)}) collective-permute-start(bf16[64,384]{1,0:T(8,128)(2,1)S(1)} %get-tuple-element.37), channel_id=1, source_target_pairs={{0,8},{8,0},{16,24},{24,16},{1,9},{9,1},{17,25},{25,17},{2,10},{10... | collective-permute-start | bytes 147464 | tf_op jit(solution)/shard_map/ppermute | solution.py:312
  9.7 1.5 %collective-permute-start.1 = (bf16[64,384]{1,0:T(8,128)(2,1)S(1)}, bf16[64,384]{1,0:T(8,128)(2,1)S(1)}, u32[]{:S(2)}, u32[]{:S(2)}) collective-permute-start(bf16[64,384]{1,0:T(8,128)(2,1)S(1)} %get-tuple-element.38), channel_id=1, source_target_pairs={{0,24},{8,16},{16,8},{24,0},{1,25},{9,17},{17,9},{25,1},{2,26},{10... | collective-permute-start | bytes 147464 | tf_op jit(solution)/shard_map/ppermute | solution.py:311
  11.2 0.0 copy-start
  11.2 0.7 %shard_map.86 = (bf16[128,512]{1,0:T(8,128)(2,1)S(1)}, bf16[128,1024]{1,0:T(8,128)(2,1)S(1)}, bf16[128,1024]{1,0:T(8,128)(2,1)S(1)}) custom-call(bf16[128,512]{1,0:T(8,128)(2,1)S(1)} %get-tuple-element.40.refs_0_, bf16[256,1024]{1,0:T(8,128)(2,1)S(1)} %get-tuple-element.41.refs_1_, bf16[256,1024]{1,0:T(8,128)(2,1)S(1)} %get-tuple-element.42.refs_2_), custom_call_target="tpu_custom_call" | custom-call | tf_op jit(solution)/shard_map/pallas_call | solution.py:26
  12.0 0.4 %collective-permute-done.refs_2_ = bf16[64,384]{1,0:T(8,128)(2,1)S(1)} collective-permute-done((bf16[64,384]{1,0:T(8,128)(2,1)S(1)}, bf16[64,384]{1,0:T(8,128)(2,1)S(1)}, u32[]{:S(2)}, u32[]{:S(2)}) %collective-permute-start) | collective-permute-done | bytes 49184 | tf_op jit(solution)/shard_map/ppermute | solution.py:312
  12.3 2.4 %collective-permute-done.1.refs_3_ = bf16[64,384]{1,0:T(8,128)(2,1)S(1)} collective-permute-done((bf16[64,384]{1,0:T(8,128)(2,1)S(1)}, bf16[64,384]{1,0:T(8,128)(2,1)S(1)}, u32[]{:S(2)}, u32[]{:S(2)}) %collective-permute-start.1) | collective-permute-done | bytes 49184 | tf_op jit(solution)/shard_map/ppermute | solution.py:311
  14.7 0.0 copy-done
  14.7 0.2 shard_map.87
  14.9 0.1 collective-permute-start.2
  15.0 0.8 %collective-permute-start.3 = (bf16[96,384]{1,0:T(8,128)(2,1)S(1)}, bf16[96,384]{1,0:T(8,128)(2,1)S(1)}, u32[]{:S(2)}, u32[]{:S(2)}) collective-permute-start(bf16[96,384]{1,0:T(8,128)(2,1)S(1)} %get-tuple-element.45), channel_id=1, source_target_pairs={{0,7},{1,2},{2,1},{3,4},{4,3},{5,6},{6,5},{7,0},{8,15},{9,10},{10,... | collective-permute-start | bytes 221192 | tf_op jit(solution)/shard_map/ppermute | solution.py:334
  15.8 0.0 collective-permute-done.6.refs_0_.refs_3_
  15.8 0.7 %shard_map.88 = (bf16[128,512]{1,0:T(8,128)(2,1)S(1)}, bf16[128,1024]{1,0:T(8,128)(2,1)S(1)}, bf16[128,1024]{1,0:T(8,128)(2,1)S(1)}) custom-call(bf16[128,512]{1,0:T(8,128)(2,1)S(1)} %collective-permute-done.6.refs_0_.refs_3_, bf16[256,1024]{1,0:T(8,128)(2,1)S(1)} %get-tuple-element.41.refs_1_, bf16[256,1024]{1,0:T(8,128)(2,1)S(1)} %get-tuple-element.42.refs_2_, ...), custom_call_target="tpu_custom_call" | custom-call | tf_op jit(solution)/shard_map/pallas_call | solution.py:26
  16.5 1.2 %collective-permute-start.10 = (bf16[128,512]{1,0:T(8,128)(2,1)S(1)}, bf16[128,512]{1,0:T(8,128)(2,1)S(1)}, u32[]{:S(2)}, u32[]{:S(2)}) collective-permute-start(bf16[128,512]{1,0:T(8,128)(2,1)S(1)} %get-tuple-element.63), channel_id=1, source_target_pairs={{0,3},{2,5},{4,7},{6,1},{3,0},{5,2},{7,4},{1,6},{8,11},{10,13},{12... | collective-permute-start | bytes 393224 | tf_op jit(solution)/shard_map/ppermute | solution.py:322
  17.7 0.0 collective-permute-done.5.refs_0_.refs_2_
  17.7 0.7 %shard_map.89 = (bf16[128,512]{1,0:T(8,128)(2,1)S(1)}, bf16[128,1024]{1,0:T(8,128)(2,1)S(1)}, bf16[128,1024]{1,0:T(8,128)(2,1)S(1)}) custom-call(bf16[128,512]{1,0:T(8,128)(2,1)S(1)} %collective-permute-done.5.refs_0_.refs_2_, bf16[256,1024]{1,0:T(8,128)(2,1)S(1)} %get-tuple-element.41.refs_1_, bf16[256,1024]{1,0:T(8,128)(2,1)S(1)} %get-tuple-element.42.refs_2_, ...), custom_call_target="tpu_custom_call" | custom-call | tf_op jit(solution)/shard_map/pallas_call | solution.py:26
  18.4 0.0 collective-permute-done.4.refs_0_.refs_1_
  18.5 0.7 %shard_map.90 = (bf16[128,512]{1,0:T(8,128)(2,1)S(1)}, bf16[128,1024]{1,0:T(8,128)(2,1)S(1)}, bf16[128,1024]{1,0:T(8,128)(2,1)S(1)}) custom-call(bf16[128,512]{1,0:T(8,128)(2,1)S(1)} %collective-permute-done.4.refs_0_.refs_1_, bf16[256,1024]{1,0:T(8,128)(2,1)S(1)} %get-tuple-element.41.refs_1_, bf16[256,1024]{1,0:T(8,128)(2,1)S(1)} %get-tuple-element.42.refs_2_, ...), custom_call_target="tpu_custom_call" | custom-call | tf_op jit(solution)/shard_map/pallas_call | solution.py:26
  19.2 0.8 %shard_map.91 = (f32[2,2,64,1024]{3,2,1,0:T(8,128)S(1)}, bf16[2,2,64,1024]{3,2,1,0:T(8,128)(2,1)S(1)}) custom-call(bf16[128,512]{1,0:T(8,128)(2,1)S(1)} %get-tuple-element.40.refs_0_, bf16[128,512]{1,0:T(8,128)(2,1)S(1)} %collective-permute-done.4.refs_0_.refs_1_, bf16[128,512]{1,0:T(8,128)(2,1)S(1)} %collective-permute-done.5.refs_0_.refs_2_, ...), custom_call_target="tpu_custom_call" | custom-call | tf_op jit(solution)/shard_map/pallas_call | solution.py:26
  20.0 1.4 %collective-permute-start.7 = (bf16[2,2,64,1024]{3,2,1,0:T(8,128)(2,1)S(1)}, bf16[2,2,64,1024]{3,2,1,0:T(8,128)(2,1)S(1)}, u32[]{:S(2)}, u32[]{:S(2)}) collective-permute-start(bf16[2,2,64,1024]{3,2,1,0:T(8,128)(2,1)S(1)} %get-tuple-element.58), channel_id=1, source_target_pairs={{0,1},{1,0},{2,3},{3,2},{4,5},{5,4},{6,7},{7,6},{8,9},{9,8},{10,11... | collective-permute-start | bytes 1572872 | tf_op jit(solution)/shard_map/ppermute | solution.py:348
  21.4 1.1 %collective-permute-start.9 = (bf16[128,512]{1,0:T(8,128)(2,1)S(1)}, bf16[128,512]{1,0:T(8,128)(2,1)S(1)}, u32[]{:S(2)}, u32[]{:S(2)}) collective-permute-start(bf16[128,512]{1,0:T(8,128)(2,1)S(1)} %get-tuple-element.62), channel_id=1, source_target_pairs={{0,5},{2,7},{4,1},{6,3},{5,0},{7,2},{1,4},{3,6},{8,13},{10,15},{12... | collective-permute-start | bytes 393224 | tf_op jit(solution)/shard_map/ppermute | solution.py:322
  22.4 0.5 %collective-permute-done.7.refs_1_ = bf16[2,2,64,1024]{3,2,1,0:T(8,128)(2,1)S(1)} collective-permute-done((bf16[2,2,64,1024]{3,2,1,0:T(8,128)(2,1)S(1)}, bf16[2,2,64,1024]{3,2,1,0:T(8,128)(2,1)S(1)}, u32[]{:S(2)}, u32[]{:S(2)}) %collective-permute-start.7) | collective-permute-done | bytes 524320 | tf_op jit(solution)/shard_map/ppermute | solution.py:348
  22.9 1.4 %collective-permute-start.8 = (bf16[128,512]{1,0:T(8,128)(2,1)S(1)}, bf16[128,512]{1,0:T(8,128)(2,1)S(1)}, u32[]{:S(2)}, u32[]{:S(2)}) collective-permute-start(bf16[128,512]{1,0:T(8,128)(2,1)S(1)} %get-tuple-element.61), channel_id=1, source_target_pairs={{0,7},{2,1},{4,3},{6,5},{7,0},{1,2},{3,4},{5,6},{8,15},{10,9},{12,... | collective-permute-start | bytes 393224 | tf_op jit(solution)/shard_map/ppermute | solution.py:322
  24.3 0.1 shard_map.93
  24.4 0.0 collective-permute-done.2.refs_4_
  24.4 2.1 %collective-permute-start.11 = (bf16[64,1024]{1,0:T(8,128)(2,1)S(1)}, bf16[64,1024]{1,0:T(8,128)(2,1)S(1)}, u32[]{:S(2)}, u32[]{:S(2)}) collective-permute-start(bf16[64,1024]{1,0:T(8,128)(2,1)S(1)} %get-tuple-element.66), channel_id=1, source_target_pairs={{0,24},{8,16},{16,8},{24,0},{1,25},{9,17},{17,9},{25,1},{2,26},{10... | collective-permute-start | bytes 393224 | tf_op jit(solution)/shard_map/ppermute | solution.py:357
  26.6 0.0 collective-permute-done.3.refs_5_
  26.6 0.9 %collective-permute-start.12 = (bf16[64,1024]{1,0:T(8,128)(2,1)S(1)}, bf16[64,1024]{1,0:T(8,128)(2,1)S(1)}, u32[]{:S(2)}, u32[]{:S(2)}) collective-permute-start(bf16[64,1024]{1,0:T(8,128)(2,1)S(1)} %get-tuple-element.67), channel_id=1, source_target_pairs={{0,8},{8,0},{16,24},{24,16},{1,9},{9,1},{17,25},{25,17},{2,10},{10... | collective-permute-start | bytes 393224 | tf_op jit(solution)/shard_map/ppermute | solution.py:357
  27.5 0.0 collective-permute-done.10.refs_5_
  27.5 0.5 %collective-permute-start.13 = (bf16[64,1024]{1,0:T(8,128)(2,1)S(1)}, bf16[64,1024]{1,0:T(8,128)(2,1)S(1)}, u32[]{:S(2)}, u32[]{:S(2)}) collective-permute-start(bf16[64,1024]{1,0:T(8,128)(2,1)S(1)} %get-tuple-element.68), channel_id=1, source_target_pairs={{0,16},{8,24},{16,0},{24,8},{1,17},{9,25},{17,1},{25,9},{2,18},{10... | collective-permute-start | bytes 393224 | tf_op jit(solution)/shard_map/ppermute | solution.py:357
  28.0 0.7 %shard_map.94.refs_0_ = f32[256,256]{1,0:T(8,128)S(1)} custom-call(f32[256,256]{1,0:T(8,128)S(1)} %bitcast.10, f32[256,1]{1,0:T(8,128)S(1)} %get-tuple-element.36.refs_1_, bf16[64,384]{1,0:T(8,128)(2,1)S(1)} %collective-permute-done.refs_2_, bf16[64,384]{1,0:T(8,128)(2,1)S(1)} %collective-permute-done.1.refs_3_, ...), custom_call_target="tpu_custom_call" | custom-call | tf_op jit(solution)/shard_map/pallas_call | solution.py:26
  28.7 2.8 %collective-permute-done.9.refs_4_ = bf16[128,512]{1,0:T(8,128)(2,1)S(1)} collective-permute-done((bf16[128,512]{1,0:T(8,128)(2,1)S(1)}, bf16[128,512]{1,0:T(8,128)(2,1)S(1)}, u32[]{:S(2)}, u32[]{:S(2)}) %collective-permute-start.9) | collective-permute-done | bytes 131104 | tf_op jit(solution)/shard_map/ppermute | solution.py:322
  31.5 0.0 collective-permute-done.8.refs_3_
  31.5 1.1 %shard_map.95 = (f32[256,256]{1,0:T(8,128)}, bf16[256,256]{1,0:T(8,128)(2,1)}) custom-call(f32[256,256]{1,0:T(8,128)S(1)} %shard_map.94.refs_0_, bf16[256,512]{1,0:T(8,128)(2,1)S(1)} %get-tuple-element.49.refs_3_.refs_1_, bf16[128,512]{1,0:T(8,128)(2,1)S(1)} %get-tuple-element.60.refs_2_, bf16[128,512]{1,0:T(8,128)(2,1)S(1)} %collective-permute-done.8.refs_3_, ...), custom_call_target="tpu_custom_call" | custom-call | tf_op jit(solution)/shard_map/pallas_call | solution.py:26
  32.6 0.0 collective-permute-done.11.refs_1_
  32.6 0.3 collective-permute-done.12.refs_2_
  32.8 0.1 collective-permute-done.13.refs_3_
  32.9 0.8 %shard_map.96 = f32[512,128]{1,0:T(8,128)} custom-call(f32[64,1024]{1,0:T(8,128)S(1)} %get-tuple-element.59.refs_6_.refs_0_, bf16[64,1024]{1,0:T(8,128)(2,1)S(1)} %collective-permute-done.11.refs_1_, bf16[64,1024]{1,0:T(8,128)(2,1)S(1)} %collective-permute-done.12.refs_2_, bf16[64,1024]{1,0:T(8,128)(2,1)S(1)} %collective-permute-done.13.refs_3_), custom_call_target="tpu_custom_call" | custom-call | tf_op jit(solution)/shard_map/pallas_call | solution.py:26
  (1 shorter events, 0.0 us)
Async XLA Ops:
  2.1 13.7 %collective-permute-start.6 = (bf16[128,512]{1,0:T(8,128)(2,1)S(1)}, bf16[128,512]{1,0:T(8,128)(2,1)S(1)}, u32[]{:S(2)}, u32[]{:S(2)}) collective-permute-start(bf16[128,512]{1,0:T(8,128)(2,1)S(1)} %get-tuple-element.48), channel_id=1, source_target_pairs={{0,3},{2,5},{4,7},{6,1},{3,0},{5,2},{7,4},{1,6},{8,11},{10,13},{12... | collective-permute-start | bytes 393224 | tf_op jit(solution)/shard_map/ppermute | solution.py:310
  4.6 13.1 %collective-permute-start.5 = (bf16[128,512]{1,0:T(8,128)(2,1)S(1)}, bf16[128,512]{1,0:T(8,128)(2,1)S(1)}, u32[]{:S(2)}, u32[]{:S(2)}) collective-permute-start(bf16[128,512]{1,0:T(8,128)(2,1)S(1)} %get-tuple-element.47), channel_id=1, source_target_pairs={{0,5},{2,7},{4,1},{6,3},{5,0},{7,2},{1,4},{3,6},{8,13},{10,15},{12... | collective-permute-start | bytes 393224 | tf_op jit(solution)/shard_map/ppermute | solution.py:310
  6.3 12.1 %collective-permute-start.4 = (bf16[128,512]{1,0:T(8,128)(2,1)S(1)}, bf16[128,512]{1,0:T(8,128)(2,1)S(1)}, u32[]{:S(2)}, u32[]{:S(2)}) collective-permute-start(bf16[128,512]{1,0:T(8,128)(2,1)S(1)} %get-tuple-element.46), channel_id=1, source_target_pairs={{0,7},{2,1},{4,3},{6,5},{7,0},{1,2},{3,4},{5,6},{8,15},{10,9},{12,... | collective-permute-start | bytes 393224 | tf_op jit(solution)/shard_map/ppermute | solution.py:310
  8.3 4.1 %collective-permute-start = (bf16[64,384]{1,0:T(8,128)(2,1)S(1)}, bf16[64,384]{1,0:T(8,128)(2,1)S(1)}, u32[]{:S(2)}, u32[]{:S(2)}) collective-permute-start(bf16[64,384]{1,0:T(8,128)(2,1)S(1)} %get-tuple-element.37), channel_id=1, source_target_pairs={{0,8},{8,0},{16,24},{24,16},{1,9},{9,1},{17,25},{25,17},{2,10},{10... | collective-permute-start | bytes 147464 | tf_op jit(solution)/shard_map/ppermute | solution.py:312
  9.7 5.0 %collective-permute-start.1 = (bf16[64,384]{1,0:T(8,128)(2,1)S(1)}, bf16[64,384]{1,0:T(8,128)(2,1)S(1)}, u32[]{:S(2)}, u32[]{:S(2)}) collective-permute-start(bf16[64,384]{1,0:T(8,128)(2,1)S(1)} %get-tuple-element.38), channel_id=1, source_target_pairs={{0,24},{8,16},{16,8},{24,0},{1,25},{9,17},{17,9},{25,1},{2,26},{10... | collective-permute-start | bytes 147464 | tf_op jit(solution)/shard_map/ppermute | solution.py:311
  11.2 3.5 %copy-start = (f32[16,16,256]{2,1,0:T(8,128)S(1)}, f32[16,16,256]{2,1,0:T(8,128)}, u32[]{:S(2)}) copy-start(f32[16,16,256]{2,1,0:T(8,128)} %param.6) | copy-start | bytes 786436
  14.9 9.5 %collective-permute-start.2 = (bf16[96,384]{1,0:T(8,128)(2,1)S(1)}, bf16[96,384]{1,0:T(8,128)(2,1)S(1)}, u32[]{:S(2)}, u32[]{:S(2)}) collective-permute-start(bf16[96,384]{1,0:T(8,128)(2,1)S(1)} %get-tuple-element.44), channel_id=1, source_target_pairs={{0,1},{1,0},{2,3},{3,2},{4,5},{5,4},{6,7},{7,6},{8,9},{9,8},{10,11... | collective-permute-start | bytes 221192 | tf_op jit(solution)/shard_map/ppermute | solution.py:335
  15.0 11.6 %collective-permute-start.3 = (bf16[96,384]{1,0:T(8,128)(2,1)S(1)}, bf16[96,384]{1,0:T(8,128)(2,1)S(1)}, u32[]{:S(2)}, u32[]{:S(2)}) collective-permute-start(bf16[96,384]{1,0:T(8,128)(2,1)S(1)} %get-tuple-element.45), channel_id=1, source_target_pairs={{0,7},{1,2},{2,1},{3,4},{4,3},{5,6},{6,5},{7,0},{8,15},{9,10},{10,... | collective-permute-start | bytes 221192 | tf_op jit(solution)/shard_map/ppermute | solution.py:334
  16.5 11.0 %collective-permute-start.10 = (bf16[128,512]{1,0:T(8,128)(2,1)S(1)}, bf16[128,512]{1,0:T(8,128)(2,1)S(1)}, u32[]{:S(2)}, u32[]{:S(2)}) collective-permute-start(bf16[128,512]{1,0:T(8,128)(2,1)S(1)} %get-tuple-element.63), channel_id=1, source_target_pairs={{0,3},{2,5},{4,7},{6,1},{3,0},{5,2},{7,4},{1,6},{8,11},{10,13},{12... | collective-permute-start | bytes 393224 | tf_op jit(solution)/shard_map/ppermute | solution.py:322
  20.0 2.9 %collective-permute-start.7 = (bf16[2,2,64,1024]{3,2,1,0:T(8,128)(2,1)S(1)}, bf16[2,2,64,1024]{3,2,1,0:T(8,128)(2,1)S(1)}, u32[]{:S(2)}, u32[]{:S(2)}) collective-permute-start(bf16[2,2,64,1024]{3,2,1,0:T(8,128)(2,1)S(1)} %get-tuple-element.58), channel_id=1, source_target_pairs={{0,1},{1,0},{2,3},{3,2},{4,5},{5,4},{6,7},{7,6},{8,9},{9,8},{10,11... | collective-permute-start | bytes 1572872 | tf_op jit(solution)/shard_map/ppermute | solution.py:348
  21.4 10.1 %collective-permute-start.9 = (bf16[128,512]{1,0:T(8,128)(2,1)S(1)}, bf16[128,512]{1,0:T(8,128)(2,1)S(1)}, u32[]{:S(2)}, u32[]{:S(2)}) collective-permute-start(bf16[128,512]{1,0:T(8,128)(2,1)S(1)} %get-tuple-element.62), channel_id=1, source_target_pairs={{0,5},{2,7},{4,1},{6,3},{5,0},{7,2},{1,4},{3,6},{8,13},{10,15},{12... | collective-permute-start | bytes 393224 | tf_op jit(solution)/shard_map/ppermute | solution.py:322
  22.9 8.6 %collective-permute-start.8 = (bf16[128,512]{1,0:T(8,128)(2,1)S(1)}, bf16[128,512]{1,0:T(8,128)(2,1)S(1)}, u32[]{:S(2)}, u32[]{:S(2)}) collective-permute-start(bf16[128,512]{1,0:T(8,128)(2,1)S(1)} %get-tuple-element.61), channel_id=1, source_target_pairs={{0,7},{2,1},{4,3},{6,5},{7,0},{1,2},{3,4},{5,6},{8,15},{10,9},{12,... | collective-permute-start | bytes 393224 | tf_op jit(solution)/shard_map/ppermute | solution.py:322
  24.4 8.1 %collective-permute-start.11 = (bf16[64,1024]{1,0:T(8,128)(2,1)S(1)}, bf16[64,1024]{1,0:T(8,128)(2,1)S(1)}, u32[]{:S(2)}, u32[]{:S(2)}) collective-permute-start(bf16[64,1024]{1,0:T(8,128)(2,1)S(1)} %get-tuple-element.66), channel_id=1, source_target_pairs={{0,24},{8,16},{16,8},{24,0},{1,25},{9,17},{17,9},{25,1},{2,26},{10... | collective-permute-start | bytes 393224 | tf_op jit(solution)/shard_map/ppermute | solution.py:357
  26.6 6.3 %collective-permute-start.12 = (bf16[64,1024]{1,0:T(8,128)(2,1)S(1)}, bf16[64,1024]{1,0:T(8,128)(2,1)S(1)}, u32[]{:S(2)}, u32[]{:S(2)}) collective-permute-start(bf16[64,1024]{1,0:T(8,128)(2,1)S(1)} %get-tuple-element.67), channel_id=1, source_target_pairs={{0,8},{8,0},{16,24},{24,16},{1,9},{9,1},{17,25},{25,17},{2,10},{10... | collective-permute-start | bytes 393224 | tf_op jit(solution)/shard_map/ppermute | solution.py:357
  27.5 5.4 %collective-permute-start.13 = (bf16[64,1024]{1,0:T(8,128)(2,1)S(1)}, bf16[64,1024]{1,0:T(8,128)(2,1)S(1)}, u32[]{:S(2)}, u32[]{:S(2)}) collective-permute-start(bf16[64,1024]{1,0:T(8,128)(2,1)S(1)} %get-tuple-element.68), channel_id=1, source_target_pairs={{0,16},{8,24},{16,0},{24,8},{1,17},{9,25},{17,1},{25,9},{2,18},{10... | collective-permute-start | bytes 393224 | tf_op jit(solution)/shard_map/ppermute | solution.py:357

commit v6 on v5

--- a/solution.py
+++ b/solution.py
@@ -196,6 +196,10 @@
     back[:, feats:] = adjoint.astype(BF16)
 
 
+def hold_kernel(back, out):
+    out[...] = back[...]
+
+
 def grads_of(chunks, acts, dpres, h, piece, feats):
     dpre = jnp.concatenate([d[:, h : h + piece] for d in dpres], axis=0)
     act = jnp.concatenate([a[:, h : h + piece] for a in acts], axis=0)
@@ -313,17 +317,18 @@
 
     backs, acts, dpres = [None] * owners, [None] * owners, [None] * owners
 
-    def physics(k, after=()):
+    def physics(k, after=(), held=False):
         made = [shape((cap, 2 * feats), BF16)] + [shape((cap, hidden), BF16)] * 2
         backs[k], acts[k], dpres[k] = call(
             physics_kernel, [got[k], weight_in, weight_out], made, after=after
         )
-        if k > 0:
+        if k > 0 and not held:
             backs[k] = lax.ppermute(backs[k], ("grp", "col"), partners(k))
         return (acts[k],)
 
     physics(0)
     done = (acts[0],)
+    done = physics(3, done, True)
     side = shape(((high + 2 * STEPS) * STEPS, feats + 128), BF16)
     inner, outer, places = call(
         functools.partial(edge_kernel, wide, high),
@@ -334,7 +339,11 @@
     outer_back = lax.ppermute(outer, ("grp", "col"), outward(("grp", "col")))
     inner_back = lax.ppermute(inner, "col", swap("col", 1))
     done = (places,)
-    for k in (3, 2, 1, *range(4, owners)):
+    (back,) = call(hold_kernel, [backs[3]], [shape(backs[3].shape, BF16)], after=(places,))
+    backs[3] = lax.ppermute(back, ("grp", "col"), partners(3))
+    done = physics(2, done)
+    done = physics(1, done)
+    for k in range(4, owners):
         done = physics(k, done)
 
     parts = lax.axis_size("row") * lax.axis_size("col")

time: 33.8 us -> 33.4 us (0.988)
  waiting for transfers between devices: 6.4 us -> 5.24 us
  starting transfers between devices: 18.6 us -> 19.4 us
    ppermute x0 -> x1, starting transfers between devices: none -> 0.75 us  [local(): backs[3] = lax.ppermute(back, ('grp', 'col'), partners(3))]
    ppermute x3 -> x2, starting transfers between devices: 3.7 us -> 3.18 us  [physics(): backs[k] = lax.ppermute(backs[k], ('grp', 'col'), partners(k))]
    ppermute x1, starting transfers between devices: 0.76 us -> 1.24 us  [local(): outer_back = lax.ppermute(outer, ('grp', 'col'), outward(('grp', 'col')))]
    ppermute x1, waiting for transfers between devices: 0.48 us -> 0.05 us  [local(): arrived = lax.ppermute(send, 'col', swap('col', 1))]
    ppermute x1, waiting for transfers between devices: 2.39 us -> 1.99 us  [local(): far = lax.ppermute(outer, 'row', outward('row'))]
    ppermute x1, waiting for transfers between devices: 0.37 us -> 0.01 us  [local(): near = lax.ppermute(inner, 'row', swap('row', 1))]
    ppermute x3 -> x2, waiting for transfers between devices: 2.82 us -> 3.18 us  [physics(): backs[k] = lax.ppermute(backs[k], ('grp', 'col'), partners(k))]
    pallas_call x12 -> x13, Pallas kernels: 7.9 us -> 7.9 us  [call(): pl.pallas_call(body, out_shape=list(outs), in_specs=specs + [ANY] * len(a...]
  transfers between devices with their start and end apart: 14 -> 14, of which waited for: 6 -> 2; matrix products, arithmetic and copies ran while one was open for 0% -> 0% of each run, Pallas kernels for 17% -> 17%
where the time goes in v6:
time: 33.4 us; the launch traced here: 33.3 us
  starting transfers between devices  19.4 us (58%)
  Pallas kernels  7.9 us (24%)
  waiting for transfers between devices  5.24 us (16%)
  between operations  0.75 us (2%)
    pallas_call x13, Pallas kernels, call(): pl.pallas_call(body, out_shape=list(outs), in_specs=specs + [ANY] * len(a...  7.9 us
    ppermute x3, starting transfers between devices, local(): got[k] = lax.ppermute(chunks[k], ('grp', 'col'), partners(k))  6.19 us
    ppermute x3, starting transfers between devices, local(): lax.ppermute(s, 'row', swap('row', bit))  3.55 us
    ppermute x2, waiting for transfers between devices, physics(): backs[k] = lax.ppermute(backs[k], ('grp', 'col'), partners(k))  3.18 us
    ppermute x2, starting transfers between devices, physics(): backs[k] = lax.ppermute(backs[k], ('grp', 'col'), partners(k))  3.18 us
    ppermute x1, waiting for transfers between devices, local(): far = lax.ppermute(outer, 'row', outward('row'))  1.99 us
    ppermute x1, starting transfers between devices, local(): near = lax.ppermute(inner, 'row', swap('row', 1))  1.49 us
    ppermute x1, starting transfers between devices, local(): far = lax.ppermute(outer, 'row', outward('row'))  1.49 us
  transfers between devices with their start and end apart: 14, of which 2 were waited for; matrix products, arithmetic and copies ran while one was open for 0% of the time, Pallas kernels for 17%

profile of v6, /device:TPU:0, one launch (start us, length us, event | category | flops | bytes accessed | tf_op | source)
XLA Modules:
  0.0 33.3 jit_solution(9313583028334208389)
XLA Ops:
  0.6 1.4 %shard_map.85 = (bf16[128,512]{1,0:T(8,128)(2,1)S(1)}, bf16[128,512]{1,0:T(8,128)(2,1)S(1)}, bf16[128,512]{1,0:T(8,128)(2,1)S(1)}, bf16[128,512]{1,0:T(8,128)(2,...) custom-call(s32[1,256]{1,0:T(1,128)} %bitcast.15, ...), custom_call_target="tpu_custom_call" | custom-call | tf_op jit(solution)/shard_map/pallas_call | solution.py:26
  2.1 2.5 %collective-permute-start.2 = (bf16[128,512]{1,0:T(8,128)(2,1)S(1)}, bf16[128,512]{1,0:T(8,128)(2,1)S(1)}, u32[]{:S(2)}, u32[]{:S(2)}) collective-permute-start(bf16[128,512]{1,0:T(8,128)(2,1)S(1)} %get-tuple-element.40), channel_id=1, source_target_pairs={{0,3},{2,5},{4,7},{6,1},{3,0},{5,2},{7,4},{1,6},{8,11},{10,13},{12... | collective-permute-start | bytes 393224 | tf_op jit(solution)/shard_map/ppermute | solution.py:314
  4.6 1.7 %collective-permute-start.6 = (bf16[128,512]{1,0:T(8,128)(2,1)S(1)}, bf16[128,512]{1,0:T(8,128)(2,1)S(1)}, u32[]{:S(2)}, u32[]{:S(2)}) collective-permute-start(bf16[128,512]{1,0:T(8,128)(2,1)S(1)} %get-tuple-element.49), channel_id=1, source_target_pairs={{0,5},{2,7},{4,1},{6,3},{5,0},{7,2},{1,4},{3,6},{8,13},{10,15},{12... | collective-permute-start | bytes 393224 | tf_op jit(solution)/shard_map/ppermute | solution.py:314
  6.3 1.9 %collective-permute-start.5 = (bf16[128,512]{1,0:T(8,128)(2,1)S(1)}, bf16[128,512]{1,0:T(8,128)(2,1)S(1)}, u32[]{:S(2)}, u32[]{:S(2)}) collective-permute-start(bf16[128,512]{1,0:T(8,128)(2,1)S(1)} %get-tuple-element.48), channel_id=1, source_target_pairs={{0,7},{2,1},{4,3},{6,5},{7,0},{1,2},{3,4},{5,6},{8,15},{10,9},{12,... | collective-permute-start | bytes 393224 | tf_op jit(solution)/shard_map/ppermute | solution.py:314
  8.3 1.5 %collective-permute-start = (bf16[64,384]{1,0:T(8,128)(2,1)S(1)}, bf16[64,384]{1,0:T(8,128)(2,1)S(1)}, u32[]{:S(2)}, u32[]{:S(2)}) collective-permute-start(bf16[64,384]{1,0:T(8,128)(2,1)S(1)} %get-tuple-element.37), channel_id=1, source_target_pairs={{0,8},{8,0},{16,24},{24,16},{1,9},{9,1},{17,25},{25,17},{2,10},{10... | collective-permute-start | bytes 147464 | tf_op jit(solution)/shard_map/ppermute | solution.py:316
  9.7 1.5 %collective-permute-start.1 = (bf16[64,384]{1,0:T(8,128)(2,1)S(1)}, bf16[64,384]{1,0:T(8,128)(2,1)S(1)}, u32[]{:S(2)}, u32[]{:S(2)}) collective-permute-start(bf16[64,384]{1,0:T(8,128)(2,1)S(1)} %get-tuple-element.38), channel_id=1, source_target_pairs={{0,24},{8,16},{16,8},{24,0},{1,25},{9,17},{17,9},{25,1},{2,26},{10... | collective-permute-start | bytes 147464 | tf_op jit(solution)/shard_map/ppermute | solution.py:315
  11.2 0.7 %shard_map.86 = (bf16[128,512]{1,0:T(8,128)(2,1)S(1)}, bf16[128,1024]{1,0:T(8,128)(2,1)S(1)}, bf16[128,1024]{1,0:T(8,128)(2,1)S(1)}) custom-call(bf16[128,512]{1,0:T(8,128)(2,1)S(1)} %get-tuple-element.43.refs_0_, bf16[256,1024]{1,0:T(8,128)(2,1)S(1)} %get-tuple-element.41.refs_1_, bf16[256,1024]{1,0:T(8,128)(2,1)S(1)} %get-tuple-element.42.refs_2_), custom_call_target="tpu_custom_call" | custom-call | tf_op jit(solution)/shard_map/pallas_call | solution.py:26
  12.0 0.0 collective-permute-done.2.refs_0_.refs_3_
  12.0 0.0 copy-start
  12.0 0.7 %shard_map.87 = (bf16[128,512]{1,0:T(8,128)(2,1)S(1)}, bf16[128,1024]{1,0:T(8,128)(2,1)S(1)}, bf16[128,1024]{1,0:T(8,128)(2,1)S(1)}) custom-call(bf16[128,512]{1,0:T(8,128)(2,1)S(1)} %collective-permute-done.2.refs_0_.refs_3_, bf16[256,1024]{1,0:T(8,128)(2,1)S(1)} %get-tuple-element.41.refs_1_, bf16[256,1024]{1,0:T(8,128)(2,1)S(1)} %get-tuple-element.42.refs_2_, ...), custom_call_target="tpu_custom_call" | custom-call | tf_op jit(solution)/shard_map/pallas_call | solution.py:26
  12.7 0.0 collective-permute-done.refs_2_
  12.7 2.0 %collective-permute-done.1.refs_3_ = bf16[64,384]{1,0:T(8,128)(2,1)S(1)} collective-permute-done((bf16[64,384]{1,0:T(8,128)(2,1)S(1)}, bf16[64,384]{1,0:T(8,128)(2,1)S(1)}, u32[]{:S(2)}, u32[]{:S(2)}) %collective-permute-start.1) | collective-permute-done | bytes 49184 | tf_op jit(solution)/shard_map/ppermute | solution.py:315
  14.7 0.0 copy-done
  14.7 0.2 shard_map.88
  14.9 0.1 collective-permute-start.3
  15.0 1.2 %collective-permute-start.4 = (bf16[96,384]{1,0:T(8,128)(2,1)S(1)}, bf16[96,384]{1,0:T(8,128)(2,1)S(1)}, u32[]{:S(2)}, u32[]{:S(2)}) collective-permute-start(bf16[96,384]{1,0:T(8,128)(2,1)S(1)} %get-tuple-element.47), channel_id=1, source_target_pairs={{0,7},{1,2},{2,1},{3,4},{4,3},{5,6},{6,5},{7,0},{8,15},{9,10},{10,... | collective-permute-start | bytes 221192 | tf_op jit(solution)/shard_map/ppermute | solution.py:339
  16.2 0.7 %collective-permute-start.10 = (bf16[128,512]{1,0:T(8,128)(2,1)S(1)}, bf16[128,512]{1,0:T(8,128)(2,1)S(1)}, u32[]{:S(2)}, u32[]{:S(2)}) collective-permute-start(bf16[128,512]{1,0:T(8,128)(2,1)S(1)} %shard_map.95), channel_id=1, source_target_pairs={{0,3},{2,5},{4,7},{6,1},{3,0},{5,2},{7,4},{1,6},{8,11},{10,13},{12... | collective-permute-start | bytes 393224 | tf_op jit(solution)/shard_map/ppermute | solution.py:343
  17.0 0.0 collective-permute-done.6.refs_0_.refs_2_
  17.0 0.7 %shard_map.89 = (bf16[128,512]{1,0:T(8,128)(2,1)S(1)}, bf16[128,1024]{1,0:T(8,128)(2,1)S(1)}, bf16[128,1024]{1,0:T(8,128)(2,1)S(1)}) custom-call(bf16[128,512]{1,0:T(8,128)(2,1)S(1)} %collective-permute-done.6.refs_0_.refs_2_, bf16[256,1024]{1,0:T(8,128)(2,1)S(1)} %get-tuple-element.41.refs_1_, bf16[256,1024]{1,0:T(8,128)(2,1)S(1)} %get-tuple-element.42.refs_2_, ...), custom_call_target="tpu_custom_call" | custom-call | tf_op jit(solution)/shard_map/pallas_call | solution.py:26
  17.7 0.0 collective-permute-done.5.refs_0_.refs_1_
  17.7 0.7 %shard_map.90 = (bf16[128,512]{1,0:T(8,128)(2,1)S(1)}, bf16[128,1024]{1,0:T(8,128)(2,1)S(1)}, bf16[128,1024]{1,0:T(8,128)(2,1)S(1)}) custom-call(bf16[128,512]{1,0:T(8,128)(2,1)S(1)} %collective-permute-done.5.refs_0_.refs_1_, bf16[256,1024]{1,0:T(8,128)(2,1)S(1)} %get-tuple-element.41.refs_1_, bf16[256,1024]{1,0:T(8,128)(2,1)S(1)} %get-tuple-element.42.refs_2_, ...), custom_call_target="tpu_custom_call" | custom-call | tf_op jit(solution)/shard_map/pallas_call | solution.py:26
  18.5 0.8 %shard_map.91 = (f32[2,2,64,1024]{3,2,1,0:T(8,128)S(1)}, bf16[2,2,64,1024]{3,2,1,0:T(8,128)(2,1)S(1)}) custom-call(bf16[128,512]{1,0:T(8,128)(2,1)S(1)} %get-tuple-element.43.refs_0_, bf16[128,512]{1,0:T(8,128)(2,1)S(1)} %collective-permute-done.5.refs_0_.refs_1_, bf16[128,512]{1,0:T(8,128)(2,1)S(1)} %collective-permute-done.6.refs_0_.refs_2_, ...), custom_call_target="tpu_custom_call" | custom-call | tf_op jit(solution)/shard_map/pallas_call | solution.py:26
  19.2 1.4 %collective-permute-start.7 = (bf16[2,2,64,1024]{3,2,1,0:T(8,128)(2,1)S(1)}, bf16[2,2,64,1024]{3,2,1,0:T(8,128)(2,1)S(1)}, u32[]{:S(2)}, u32[]{:S(2)}) collective-permute-start(bf16[2,2,64,1024]{3,2,1,0:T(8,128)(2,1)S(1)} %get-tuple-element.58), channel_id=1, source_target_pairs={{0,1},{1,0},{2,3},{3,2},{4,5},{5,4},{6,7},{7,6},{8,9},{9,8},{10,11... | collective-permute-start | bytes 1572872 | tf_op jit(solution)/shard_map/ppermute | solution.py:357
  20.6 1.5 %collective-permute-start.9 = (bf16[128,512]{1,0:T(8,128)(2,1)S(1)}, bf16[128,512]{1,0:T(8,128)(2,1)S(1)}, u32[]{:S(2)}, u32[]{:S(2)}) collective-permute-start(bf16[128,512]{1,0:T(8,128)(2,1)S(1)} %get-tuple-element.62), channel_id=1, source_target_pairs={{0,5},{2,7},{4,1},{6,3},{5,0},{7,2},{1,4},{3,6},{8,13},{10,15},{12... | collective-permute-start | bytes 393224 | tf_op jit(solution)/shard_map/ppermute | solution.py:326
  22.1 0.0 collective-permute-done.7.refs_1_
  22.2 1.7 %collective-permute-start.8 = (bf16[128,512]{1,0:T(8,128)(2,1)S(1)}, bf16[128,512]{1,0:T(8,128)(2,1)S(1)}, u32[]{:S(2)}, u32[]{:S(2)}) collective-permute-start(bf16[128,512]{1,0:T(8,128)(2,1)S(1)} %get-tuple-element.61), channel_id=1, source_target_pairs={{0,7},{2,1},{4,3},{6,5},{7,0},{1,2},{3,4},{5,6},{8,15},{10,9},{12,... | collective-permute-start | bytes 393224 | tf_op jit(solution)/shard_map/ppermute | solution.py:326
  23.9 0.1 shard_map.93
  24.0 0.0 collective-permute-done.3.refs_4_
  24.0 2.5 %collective-permute-start.11 = (bf16[64,1024]{1,0:T(8,128)(2,1)S(1)}, bf16[64,1024]{1,0:T(8,128)(2,1)S(1)}, u32[]{:S(2)}, u32[]{:S(2)}) collective-permute-start(bf16[64,1024]{1,0:T(8,128)(2,1)S(1)} %get-tuple-element.66), channel_id=1, source_target_pairs={{0,24},{8,16},{16,8},{24,0},{1,25},{9,17},{17,9},{25,1},{2,26},{10... | collective-permute-start | bytes 393224 | tf_op jit(solution)/shard_map/ppermute | solution.py:366
  26.5 0.0 collective-permute-done.4.refs_5_
  26.5 0.5 %collective-permute-start.12 = (bf16[64,1024]{1,0:T(8,128)(2,1)S(1)}, bf16[64,1024]{1,0:T(8,128)(2,1)S(1)}, u32[]{:S(2)}, u32[]{:S(2)}) collective-permute-start(bf16[64,1024]{1,0:T(8,128)(2,1)S(1)} %get-tuple-element.67), channel_id=1, source_target_pairs={{0,8},{8,0},{16,24},{24,16},{1,9},{9,1},{17,25},{25,17},{2,10},{10... | collective-permute-start | bytes 393224 | tf_op jit(solution)/shard_map/ppermute | solution.py:366
  27.0 0.0 collective-permute-done.10.refs_5_
  27.0 0.5 %collective-permute-start.13 = (bf16[64,1024]{1,0:T(8,128)(2,1)S(1)}, bf16[64,1024]{1,0:T(8,128)(2,1)S(1)}, u32[]{:S(2)}, u32[]{:S(2)}) collective-permute-start(bf16[64,1024]{1,0:T(8,128)(2,1)S(1)} %get-tuple-element.68), channel_id=1, source_target_pairs={{0,16},{8,24},{16,0},{24,8},{1,17},{9,25},{17,1},{25,9},{2,18},{10... | collective-permute-start | bytes 393224 | tf_op jit(solution)/shard_map/ppermute | solution.py:366
  27.5 0.7 %shard_map.94.refs_0_ = f32[256,256]{1,0:T(8,128)S(1)} custom-call(f32[256,256]{1,0:T(8,128)S(1)} %bitcast.10, f32[256,1]{1,0:T(8,128)S(1)} %get-tuple-element.36.refs_1_, bf16[64,384]{1,0:T(8,128)(2,1)S(1)} %collective-permute-done.refs_2_, bf16[64,384]{1,0:T(8,128)(2,1)S(1)} %collective-permute-done.1.refs_3_, ...), custom_call_target="tpu_custom_call" | custom-call | tf_op jit(solution)/shard_map/pallas_call | solution.py:26
  28.2 3.2 %collective-permute-done.9.refs_4_ = bf16[128,512]{1,0:T(8,128)(2,1)S(1)} collective-permute-done((bf16[128,512]{1,0:T(8,128)(2,1)S(1)}, bf16[128,512]{1,0:T(8,128)(2,1)S(1)}, u32[]{:S(2)}, u32[]{:S(2)}) %collective-permute-start.9) | collective-permute-done | bytes 131104 | tf_op jit(solution)/shard_map/ppermute | solution.py:326
  31.4 0.0 collective-permute-done.8.refs_3_
  31.4 1.1 %shard_map.96 = (f32[256,256]{1,0:T(8,128)}, bf16[256,256]{1,0:T(8,128)(2,1)}) custom-call(f32[256,256]{1,0:T(8,128)S(1)} %shard_map.94.refs_0_, bf16[256,512]{1,0:T(8,128)(2,1)S(1)} %get-tuple-element.50.refs_3_.refs_1_, bf16[128,512]{1,0:T(8,128)(2,1)S(1)} %get-tuple-element.60.refs_2_, bf16[128,512]{1,0:T(8,128)(2,1)S(1)} %collective-permute-done.8.refs_3_, ...), custom_call_target="tpu_custom_call" | custom-call | tf_op jit(solution)/shard_map/pallas_call | solution.py:26
  32.5 0.0 collective-permute-done.11.refs_1_
  32.5 0.0 collective-permute-done.12.refs_2_
  32.5 0.0 collective-permute-done.13.refs_3_
  32.5 0.8 %shard_map.97 = f32[512,128]{1,0:T(8,128)} custom-call(f32[64,1024]{1,0:T(8,128)S(1)} %get-tuple-element.59.refs_6_.refs_0_, bf16[64,1024]{1,0:T(8,128)(2,1)S(1)} %collective-permute-done.11.refs_1_, bf16[64,1024]{1,0:T(8,128)(2,1)S(1)} %collective-permute-done.12.refs_2_, bf16[64,1024]{1,0:T(8,128)(2,1)S(1)} %collective-permute-done.13.refs_3_), custom_call_target="tpu_custom_call" | custom-call | tf_op jit(solution)/shard_map/pallas_call | solution.py:26
  (2 shorter events, 0.0 us)
Async XLA Ops:
  2.1 9.9 %collective-permute-start.2 = (bf16[128,512]{1,0:T(8,128)(2,1)S(1)}, bf16[128,512]{1,0:T(8,128)(2,1)S(1)}, u32[]{:S(2)}, u32[]{:S(2)}) collective-permute-start(bf16[128,512]{1,0:T(8,128)(2,1)S(1)} %get-tuple-element.40), channel_id=1, source_target_pairs={{0,3},{2,5},{4,7},{6,1},{3,0},{5,2},{7,4},{1,6},{8,11},{10,13},{12... | collective-permute-start | bytes 393224 | tf_op jit(solution)/shard_map/ppermute | solution.py:314
  4.6 12.4 %collective-permute-start.6 = (bf16[128,512]{1,0:T(8,128)(2,1)S(1)}, bf16[128,512]{1,0:T(8,128)(2,1)S(1)}, u32[]{:S(2)}, u32[]{:S(2)}) collective-permute-start(bf16[128,512]{1,0:T(8,128)(2,1)S(1)} %get-tuple-element.49), channel_id=1, source_target_pairs={{0,5},{2,7},{4,1},{6,3},{5,0},{7,2},{1,4},{3,6},{8,13},{10,15},{12... | collective-permute-start | bytes 393224 | tf_op jit(solution)/shard_map/ppermute | solution.py:314
  6.3 11.4 %collective-permute-start.5 = (bf16[128,512]{1,0:T(8,128)(2,1)S(1)}, bf16[128,512]{1,0:T(8,128)(2,1)S(1)}, u32[]{:S(2)}, u32[]{:S(2)}) collective-permute-start(bf16[128,512]{1,0:T(8,128)(2,1)S(1)} %get-tuple-element.48), channel_id=1, source_target_pairs={{0,7},{2,1},{4,3},{6,5},{7,0},{1,2},{3,4},{5,6},{8,15},{10,9},{12,... | collective-permute-start | bytes 393224 | tf_op jit(solution)/shard_map/ppermute | solution.py:314
  8.3 4.5 %collective-permute-start = (bf16[64,384]{1,0:T(8,128)(2,1)S(1)}, bf16[64,384]{1,0:T(8,128)(2,1)S(1)}, u32[]{:S(2)}, u32[]{:S(2)}) collective-permute-start(bf16[64,384]{1,0:T(8,128)(2,1)S(1)} %get-tuple-element.37), channel_id=1, source_target_pairs={{0,8},{8,0},{16,24},{24,16},{1,9},{9,1},{17,25},{25,17},{2,10},{10... | collective-permute-start | bytes 147464 | tf_op jit(solution)/shard_map/ppermute | solution.py:316
  9.7 5.0 %collective-permute-start.1 = (bf16[64,384]{1,0:T(8,128)(2,1)S(1)}, bf16[64,384]{1,0:T(8,128)(2,1)S(1)}, u32[]{:S(2)}, u32[]{:S(2)}) collective-permute-start(bf16[64,384]{1,0:T(8,128)(2,1)S(1)} %get-tuple-element.38), channel_id=1, source_target_pairs={{0,24},{8,16},{16,8},{24,0},{1,25},{9,17},{17,9},{25,1},{2,26},{10... | collective-permute-start | bytes 147464 | tf_op jit(solution)/shard_map/ppermute | solution.py:315
  12.0 2.8 %copy-start = (f32[16,16,256]{2,1,0:T(8,128)S(1)}, f32[16,16,256]{2,1,0:T(8,128)}, u32[]{:S(2)}) copy-start(f32[16,16,256]{2,1,0:T(8,128)} %param.6) | copy-start | bytes 786436
  14.9 9.1 %collective-permute-start.3 = (bf16[96,384]{1,0:T(8,128)(2,1)S(1)}, bf16[96,384]{1,0:T(8,128)(2,1)S(1)}, u32[]{:S(2)}, u32[]{:S(2)}) collective-permute-start(bf16[96,384]{1,0:T(8,128)(2,1)S(1)} %get-tuple-element.46), channel_id=1, source_target_pairs={{0,1},{1,0},{2,3},{3,2},{4,5},{5,4},{6,7},{7,6},{8,9},{9,8},{10,11... | collective-permute-start | bytes 221192 | tf_op jit(solution)/shard_map/ppermute | solution.py:340
  15.0 11.5 %collective-permute-start.4 = (bf16[96,384]{1,0:T(8,128)(2,1)S(1)}, bf16[96,384]{1,0:T(8,128)(2,1)S(1)}, u32[]{:S(2)}, u32[]{:S(2)}) collective-permute-start(bf16[96,384]{1,0:T(8,128)(2,1)S(1)} %get-tuple-element.47), channel_id=1, source_target_pairs={{0,7},{1,2},{2,1},{3,4},{4,3},{5,6},{6,5},{7,0},{8,15},{9,10},{10,... | collective-permute-start | bytes 221192 | tf_op jit(solution)/shard_map/ppermute | solution.py:339
  16.2 10.8 %collective-permute-start.10 = (bf16[128,512]{1,0:T(8,128)(2,1)S(1)}, bf16[128,512]{1,0:T(8,128)(2,1)S(1)}, u32[]{:S(2)}, u32[]{:S(2)}) collective-permute-start(bf16[128,512]{1,0:T(8,128)(2,1)S(1)} %shard_map.95), channel_id=1, source_target_pairs={{0,3},{2,5},{4,7},{6,1},{3,0},{5,2},{7,4},{1,6},{8,11},{10,13},{12... | collective-permute-start | bytes 393224 | tf_op jit(solution)/shard_map/ppermute | solution.py:343
  19.2 2.9 %collective-permute-start.7 = (bf16[2,2,64,1024]{3,2,1,0:T(8,128)(2,1)S(1)}, bf16[2,2,64,1024]{3,2,1,0:T(8,128)(2,1)S(1)}, u32[]{:S(2)}, u32[]{:S(2)}) collective-permute-start(bf16[2,2,64,1024]{3,2,1,0:T(8,128)(2,1)S(1)} %get-tuple-element.58), channel_id=1, source_target_pairs={{0,1},{1,0},{2,3},{3,2},{4,5},{5,4},{6,7},{7,6},{8,9},{9,8},{10,11... | collective-permute-start | bytes 1572872 | tf_op jit(solution)/shard_map/ppermute | solution.py:357
  20.6 10.8 %collective-permute-start.9 = (bf16[128,512]{1,0:T(8,128)(2,1)S(1)}, bf16[128,512]{1,0:T(8,128)(2,1)S(1)}, u32[]{:S(2)}, u32[]{:S(2)}) collective-permute-start(bf16[128,512]{1,0:T(8,128)(2,1)S(1)} %get-tuple-element.62), channel_id=1, source_target_pairs={{0,5},{2,7},{4,1},{6,3},{5,0},{7,2},{1,4},{3,6},{8,13},{10,15},{12... | collective-permute-start | bytes 393224 | tf_op jit(solution)/shard_map/ppermute | solution.py:326
  22.2 9.2 %collective-permute-start.8 = (bf16[128,512]{1,0:T(8,128)(2,1)S(1)}, bf16[128,512]{1,0:T(8,128)(2,1)S(1)}, u32[]{:S(2)}, u32[]{:S(2)}) collective-permute-start(bf16[128,512]{1,0:T(8,128)(2,1)S(1)} %get-tuple-element.61), channel_id=1, source_target_pairs={{0,7},{2,1},{4,3},{6,5},{7,0},{1,2},{3,4},{5,6},{8,15},{10,9},{12,... | collective-permute-start | bytes 393224 | tf_op jit(solution)/shard_map/ppermute | solution.py:326
  24.0 8.5 %collective-permute-start.11 = (bf16[64,1024]{1,0:T(8,128)(2,1)S(1)}, bf16[64,1024]{1,0:T(8,128)(2,1)S(1)}, u32[]{:S(2)}, u32[]{:S(2)}) collective-permute-start(bf16[64,1024]{1,0:T(8,128)(2,1)S(1)} %get-tuple-element.66), channel_id=1, source_target_pairs={{0,24},{8,16},{16,8},{24,0},{1,25},{9,17},{17,9},{25,1},{2,26},{10... | collective-permute-start | bytes 393224 | tf_op jit(solution)/shard_map/ppermute | solution.py:366
  26.5 6.0 %collective-permute-start.12 = (bf16[64,1024]{1,0:T(8,128)(2,1)S(1)}, bf16[64,1024]{1,0:T(8,128)(2,1)S(1)}, u32[]{:S(2)}, u32[]{:S(2)}) collective-permute-start(bf16[64,1024]{1,0:T(8,128)(2,1)S(1)} %get-tuple-element.67), channel_id=1, source_target_pairs={{0,8},{8,0},{16,24},{24,16},{1,9},{9,1},{17,25},{25,17},{2,10},{10... | collective-permute-start | bytes 393224 | tf_op jit(solution)/shard_map/ppermute | solution.py:366
  27.0 5.4 %collective-permute-start.13 = (bf16[64,1024]{1,0:T(8,128)(2,1)S(1)}, bf16[64,1024]{1,0:T(8,128)(2,1)S(1)}, u32[]{:S(2)}, u32[]{:S(2)}) collective-permute-start(bf16[64,1024]{1,0:T(8,128)(2,1)S(1)} %get-tuple-element.68), channel_id=1, source_target_pairs={{0,16},{8,24},{16,0},{24,8},{1,17},{9,25},{17,1},{25,9},{2,18},{10... | collective-permute-start | bytes 393224 | tf_op jit(solution)/shard_map/ppermute | solution.py:366

commit v7 on v6

--- a/solution.py
+++ b/solution.py
@@ -16,7 +16,10 @@
 
 
 def call(kernel, ins, outs, scratch=(), after=(), far=(), vmem=24 << 20, flops=None):
-    ins = [pltpu.with_memory_space_constraint(x, pltpu.HBM) if n in far else x for n, x in enumerate(ins)]
+    ins = [
+        pltpu.with_memory_space_constraint(x, pltpu.HBM) if n in far else x
+        for n, x in enumerate(ins)
+    ]
     specs = [HBM if n in far else VMEM for n in range(len(ins))]
     count = len(ins)
 
@@ -138,9 +141,9 @@
     odd, core = lax.rem(lax.axis_index("row"), 2), lax.axis_index("col")
     at = lax.broadcasted_iota(jnp.int32, (8, feats + 128), 0)
     low = jnp.where(core == 0, at, 7 - at) < STEPS
+    ones, twos = inner[...].astype(F32), outer[...].astype(F32)
     for i in range(half):
-        one = inner[i * 8 : i * 8 + 8].astype(F32)
-        two = outer[i * 8 : i * 8 + 8].astype(F32)
+        one, two = ones[i * 8 : i * 8 + 8], twos[i * 8 : i * 8 + 8]
         this = jnp.where(low, one, two)
         that = pltpu.roll(jnp.where(low, two, one), STEPS, 0)
         for r, tile in ((i, this), (i + half, that)):
@@ -299,7 +302,8 @@
     *chunks, inner, outer, rate_col, place_row, weight_in, weight_out = call(
         functools.partial(pack_kernel, owners, cap, wide, high),
         [dest.reshape(1, count), rate, flat_state, flat_cot, w_in[0], w_out[0]],
-        [shape((cap, 2 * feats), BF16)] * owners + [strip, strip, shape((count, 1), F32), shape((1, count), jnp.int32), weight, weight],
+        [shape((cap, 2 * feats), BF16)] * owners
+        + [strip, strip, shape((count, 1), F32), shape((1, count), jnp.int32), weight, weight],
         [
             pltpu.VMEM((1, count), jnp.int32),
             pltpu.VMEM((high, wide), F32),

time: 33.4 us -> 33.4 us (level)
  no operation moved by 1% of the time
where the time goes in v7:
time: 33.4 us; the launch traced here: 33.3 us
  starting transfers between devices  19.4 us (58%)
  Pallas kernels  7.9 us (24%)
  waiting for transfers between devices  5.24 us (16%)
  between operations  0.75 us (2%)
    pallas_call x13, Pallas kernels, call(): pl.pallas_call(body, out_shape=list(outs), in_specs=specs + [ANY] * len(a...  7.9 us
    ppermute x3, starting transfers between devices, local(): got[k] = lax.ppermute(chunks[k], ('grp', 'col'), partners(k))  6.19 us
    ppermute x3, starting transfers between devices, local(): lax.ppermute(s, 'row', swap('row', bit))  3.55 us
    ppermute x2, waiting for transfers between devices, physics(): backs[k] = lax.ppermute(backs[k], ('grp', 'col'), partners(k))  3.18 us
    ppermute x2, starting transfers between devices, physics(): backs[k] = lax.ppermute(backs[k], ('grp', 'col'), partners(k))  3.18 us
    ppermute x1, waiting for transfers between devices, local(): far = lax.ppermute(outer, 'row', outward('row'))  1.99 us
    ppermute x1, starting transfers between devices, local(): near = lax.ppermute(inner, 'row', swap('row', 1))  1.49 us
    ppermute x1, starting transfers between devices, local(): far = lax.ppermute(outer, 'row', outward('row'))  1.49 us
  transfers between devices with their start and end apart: 14, of which 2 were waited for; matrix products, arithmetic and copies ran while one was open for 0% of the time, Pallas kernels for 17%

profile of v7, /device:TPU:0, one launch (start us, length us, event | category | flops | bytes accessed | tf_op | source)
XLA Modules:
  0.0 33.3 jit_solution(11590836776133145008)
XLA Ops:
  0.6 1.4 %shard_map.85 = (bf16[128,512]{1,0:T(8,128)(2,1)S(1)}, bf16[128,512]{1,0:T(8,128)(2,1)S(1)}, bf16[128,512]{1,0:T(8,128)(2,1)S(1)}, bf16[128,512]{1,0:T(8,128)(2,...) custom-call(s32[1,256]{1,0:T(1,128)} %bitcast.15, ...), custom_call_target="tpu_custom_call" | custom-call | tf_op jit(solution)/shard_map/pallas_call | solution.py:29
  2.1 2.5 %collective-permute-start.2 = (bf16[128,512]{1,0:T(8,128)(2,1)S(1)}, bf16[128,512]{1,0:T(8,128)(2,1)S(1)}, u32[]{:S(2)}, u32[]{:S(2)}) collective-permute-start(bf16[128,512]{1,0:T(8,128)(2,1)S(1)} %get-tuple-element.40), channel_id=1, source_target_pairs={{0,3},{2,5},{4,7},{6,1},{3,0},{5,2},{7,4},{1,6},{8,11},{10,13},{12... | collective-permute-start | bytes 393224 | tf_op jit(solution)/shard_map/ppermute | solution.py:318
  4.6 1.7 %collective-permute-start.6 = (bf16[128,512]{1,0:T(8,128)(2,1)S(1)}, bf16[128,512]{1,0:T(8,128)(2,1)S(1)}, u32[]{:S(2)}, u32[]{:S(2)}) collective-permute-start(bf16[128,512]{1,0:T(8,128)(2,1)S(1)} %get-tuple-element.49), channel_id=1, source_target_pairs={{0,5},{2,7},{4,1},{6,3},{5,0},{7,2},{1,4},{3,6},{8,13},{10,15},{12... | collective-permute-start | bytes 393224 | tf_op jit(solution)/shard_map/ppermute | solution.py:318
  6.3 1.9 %collective-permute-start.5 = (bf16[128,512]{1,0:T(8,128)(2,1)S(1)}, bf16[128,512]{1,0:T(8,128)(2,1)S(1)}, u32[]{:S(2)}, u32[]{:S(2)}) collective-permute-start(bf16[128,512]{1,0:T(8,128)(2,1)S(1)} %get-tuple-element.48), channel_id=1, source_target_pairs={{0,7},{2,1},{4,3},{6,5},{7,0},{1,2},{3,4},{5,6},{8,15},{10,9},{12,... | collective-permute-start | bytes 393224 | tf_op jit(solution)/shard_map/ppermute | solution.py:318
  8.3 1.5 %collective-permute-start = (bf16[64,384]{1,0:T(8,128)(2,1)S(1)}, bf16[64,384]{1,0:T(8,128)(2,1)S(1)}, u32[]{:S(2)}, u32[]{:S(2)}) collective-permute-start(bf16[64,384]{1,0:T(8,128)(2,1)S(1)} %get-tuple-element.37), channel_id=1, source_target_pairs={{0,8},{8,0},{16,24},{24,16},{1,9},{9,1},{17,25},{25,17},{2,10},{10... | collective-permute-start | bytes 147464 | tf_op jit(solution)/shard_map/ppermute | solution.py:320
  9.7 1.5 %collective-permute-start.1 = (bf16[64,384]{1,0:T(8,128)(2,1)S(1)}, bf16[64,384]{1,0:T(8,128)(2,1)S(1)}, u32[]{:S(2)}, u32[]{:S(2)}) collective-permute-start(bf16[64,384]{1,0:T(8,128)(2,1)S(1)} %get-tuple-element.38), channel_id=1, source_target_pairs={{0,24},{8,16},{16,8},{24,0},{1,25},{9,17},{17,9},{25,1},{2,26},{10... | collective-permute-start | bytes 147464 | tf_op jit(solution)/shard_map/ppermute | solution.py:319
  11.2 0.7 %shard_map.86 = (bf16[128,512]{1,0:T(8,128)(2,1)S(1)}, bf16[128,1024]{1,0:T(8,128)(2,1)S(1)}, bf16[128,1024]{1,0:T(8,128)(2,1)S(1)}) custom-call(bf16[128,512]{1,0:T(8,128)(2,1)S(1)} %get-tuple-element.43.refs_0_, bf16[256,1024]{1,0:T(8,128)(2,1)S(1)} %get-tuple-element.41.refs_1_, bf16[256,1024]{1,0:T(8,128)(2,1)S(1)} %get-tuple-element.42.refs_2_), custom_call_target="tpu_custom_call" | custom-call | tf_op jit(solution)/shard_map/pallas_call | solution.py:29
  12.0 0.0 collective-permute-done.2.refs_0_.refs_3_
  12.0 0.0 copy-start
  12.0 0.7 %shard_map.87 = (bf16[128,512]{1,0:T(8,128)(2,1)S(1)}, bf16[128,1024]{1,0:T(8,128)(2,1)S(1)}, bf16[128,1024]{1,0:T(8,128)(2,1)S(1)}) custom-call(bf16[128,512]{1,0:T(8,128)(2,1)S(1)} %collective-permute-done.2.refs_0_.refs_3_, bf16[256,1024]{1,0:T(8,128)(2,1)S(1)} %get-tuple-element.41.refs_1_, bf16[256,1024]{1,0:T(8,128)(2,1)S(1)} %get-tuple-element.42.refs_2_, ...), custom_call_target="tpu_custom_call" | custom-call | tf_op jit(solution)/shard_map/pallas_call | solution.py:29
  12.7 0.0 collective-permute-done.refs_2_
  12.7 2.0 %collective-permute-done.1.refs_3_ = bf16[64,384]{1,0:T(8,128)(2,1)S(1)} collective-permute-done((bf16[64,384]{1,0:T(8,128)(2,1)S(1)}, bf16[64,384]{1,0:T(8,128)(2,1)S(1)}, u32[]{:S(2)}, u32[]{:S(2)}) %collective-permute-start.1) | collective-permute-done | bytes 49184 | tf_op jit(solution)/shard_map/ppermute | solution.py:319
  14.7 0.0 copy-done
  14.7 0.2 shard_map.88
  14.9 0.1 collective-permute-start.3
  15.0 1.2 %collective-permute-start.4 = (bf16[96,384]{1,0:T(8,128)(2,1)S(1)}, bf16[96,384]{1,0:T(8,128)(2,1)S(1)}, u32[]{:S(2)}, u32[]{:S(2)}) collective-permute-start(bf16[96,384]{1,0:T(8,128)(2,1)S(1)} %get-tuple-element.47), channel_id=1, source_target_pairs={{0,7},{1,2},{2,1},{3,4},{4,3},{5,6},{6,5},{7,0},{8,15},{9,10},{10,... | collective-permute-start | bytes 221192 | tf_op jit(solution)/shard_map/ppermute | solution.py:343
  16.2 0.7 %collective-permute-start.10 = (bf16[128,512]{1,0:T(8,128)(2,1)S(1)}, bf16[128,512]{1,0:T(8,128)(2,1)S(1)}, u32[]{:S(2)}, u32[]{:S(2)}) collective-permute-start(bf16[128,512]{1,0:T(8,128)(2,1)S(1)} %shard_map.95), channel_id=1, source_target_pairs={{0,3},{2,5},{4,7},{6,1},{3,0},{5,2},{7,4},{1,6},{8,11},{10,13},{12... | collective-permute-start | bytes 393224 | tf_op jit(solution)/shard_map/ppermute | solution.py:347
  17.0 0.0 collective-permute-done.6.refs_0_.refs_2_
  17.0 0.7 %shard_map.89 = (bf16[128,512]{1,0:T(8,128)(2,1)S(1)}, bf16[128,1024]{1,0:T(8,128)(2,1)S(1)}, bf16[128,1024]{1,0:T(8,128)(2,1)S(1)}) custom-call(bf16[128,512]{1,0:T(8,128)(2,1)S(1)} %collective-permute-done.6.refs_0_.refs_2_, bf16[256,1024]{1,0:T(8,128)(2,1)S(1)} %get-tuple-element.41.refs_1_, bf16[256,1024]{1,0:T(8,128)(2,1)S(1)} %get-tuple-element.42.refs_2_, ...), custom_call_target="tpu_custom_call" | custom-call | tf_op jit(solution)/shard_map/pallas_call | solution.py:29
  17.7 0.0 collective-permute-done.5.refs_0_.refs_1_
  17.7 0.7 %shard_map.90 = (bf16[128,512]{1,0:T(8,128)(2,1)S(1)}, bf16[128,1024]{1,0:T(8,128)(2,1)S(1)}, bf16[128,1024]{1,0:T(8,128)(2,1)S(1)}) custom-call(bf16[128,512]{1,0:T(8,128)(2,1)S(1)} %collective-permute-done.5.refs_0_.refs_1_, bf16[256,1024]{1,0:T(8,128)(2,1)S(1)} %get-tuple-element.41.refs_1_, bf16[256,1024]{1,0:T(8,128)(2,1)S(1)} %get-tuple-element.42.refs_2_, ...), custom_call_target="tpu_custom_call" | custom-call | tf_op jit(solution)/shard_map/pallas_call | solution.py:29
  18.5 0.8 %shard_map.91 = (f32[2,2,64,1024]{3,2,1,0:T(8,128)S(1)}, bf16[2,2,64,1024]{3,2,1,0:T(8,128)(2,1)S(1)}) custom-call(bf16[128,512]{1,0:T(8,128)(2,1)S(1)} %get-tuple-element.43.refs_0_, bf16[128,512]{1,0:T(8,128)(2,1)S(1)} %collective-permute-done.5.refs_0_.refs_1_, bf16[128,512]{1,0:T(8,128)(2,1)S(1)} %collective-permute-done.6.refs_0_.refs_2_, ...), custom_call_target="tpu_custom_call" | custom-call | tf_op jit(solution)/shard_map/pallas_call | solution.py:29
  19.2 1.4 %collective-permute-start.7 = (bf16[2,2,64,1024]{3,2,1,0:T(8,128)(2,1)S(1)}, bf16[2,2,64,1024]{3,2,1,0:T(8,128)(2,1)S(1)}, u32[]{:S(2)}, u32[]{:S(2)}) collective-permute-start(bf16[2,2,64,1024]{3,2,1,0:T(8,128)(2,1)S(1)} %get-tuple-element.58), channel_id=1, source_target_pairs={{0,1},{1,0},{2,3},{3,2},{4,5},{5,4},{6,7},{7,6},{8,9},{9,8},{10,11... | collective-permute-start | bytes 1572872 | tf_op jit(solution)/shard_map/ppermute | solution.py:361
  20.6 1.5 %collective-permute-start.9 = (bf16[128,512]{1,0:T(8,128)(2,1)S(1)}, bf16[128,512]{1,0:T(8,128)(2,1)S(1)}, u32[]{:S(2)}, u32[]{:S(2)}) collective-permute-start(bf16[128,512]{1,0:T(8,128)(2,1)S(1)} %get-tuple-element.62), channel_id=1, source_target_pairs={{0,5},{2,7},{4,1},{6,3},{5,0},{7,2},{1,4},{3,6},{8,13},{10,15},{12... | collective-permute-start | bytes 393224 | tf_op jit(solution)/shard_map/ppermute | solution.py:330
  22.1 0.0 collective-permute-done.7.refs_1_
  22.2 1.7 %collective-permute-start.8 = (bf16[128,512]{1,0:T(8,128)(2,1)S(1)}, bf16[128,512]{1,0:T(8,128)(2,1)S(1)}, u32[]{:S(2)}, u32[]{:S(2)}) collective-permute-start(bf16[128,512]{1,0:T(8,128)(2,1)S(1)} %get-tuple-element.61), channel_id=1, source_target_pairs={{0,7},{2,1},{4,3},{6,5},{7,0},{1,2},{3,4},{5,6},{8,15},{10,9},{12,... | collective-permute-start | bytes 393224 | tf_op jit(solution)/shard_map/ppermute | solution.py:330
  23.9 0.1 shard_map.93
  24.0 0.0 collective-permute-done.3.refs_4_
  24.0 2.5 %collective-permute-start.11 = (bf16[64,1024]{1,0:T(8,128)(2,1)S(1)}, bf16[64,1024]{1,0:T(8,128)(2,1)S(1)}, u32[]{:S(2)}, u32[]{:S(2)}) collective-permute-start(bf16[64,1024]{1,0:T(8,128)(2,1)S(1)} %get-tuple-element.66), channel_id=1, source_target_pairs={{0,24},{8,16},{16,8},{24,0},{1,25},{9,17},{17,9},{25,1},{2,26},{10... | collective-permute-start | bytes 393224 | tf_op jit(solution)/shard_map/ppermute | solution.py:370
  26.5 0.0 collective-permute-done.4.refs_5_
  26.5 0.5 %collective-permute-start.12 = (bf16[64,1024]{1,0:T(8,128)(2,1)S(1)}, bf16[64,1024]{1,0:T(8,128)(2,1)S(1)}, u32[]{:S(2)}, u32[]{:S(2)}) collective-permute-start(bf16[64,1024]{1,0:T(8,128)(2,1)S(1)} %get-tuple-element.67), channel_id=1, source_target_pairs={{0,8},{8,0},{16,24},{24,16},{1,9},{9,1},{17,25},{25,17},{2,10},{10... | collective-permute-start | bytes 393224 | tf_op jit(solution)/shard_map/ppermute | solution.py:370
  27.0 0.0 collective-permute-done.10.refs_5_
  27.0 0.5 %collective-permute-start.13 = (bf16[64,1024]{1,0:T(8,128)(2,1)S(1)}, bf16[64,1024]{1,0:T(8,128)(2,1)S(1)}, u32[]{:S(2)}, u32[]{:S(2)}) collective-permute-start(bf16[64,1024]{1,0:T(8,128)(2,1)S(1)} %get-tuple-element.68), channel_id=1, source_target_pairs={{0,16},{8,24},{16,0},{24,8},{1,17},{9,25},{17,1},{25,9},{2,18},{10... | collective-permute-start | bytes 393224 | tf_op jit(solution)/shard_map/ppermute | solution.py:370
  27.5 0.7 %shard_map.94.refs_0_ = f32[256,256]{1,0:T(8,128)S(1)} custom-call(f32[256,256]{1,0:T(8,128)S(1)} %bitcast.10, f32[256,1]{1,0:T(8,128)S(1)} %get-tuple-element.36.refs_1_, bf16[64,384]{1,0:T(8,128)(2,1)S(1)} %collective-permute-done.refs_2_, bf16[64,384]{1,0:T(8,128)(2,1)S(1)} %collective-permute-done.1.refs_3_, ...), custom_call_target="tpu_custom_call" | custom-call | tf_op jit(solution)/shard_map/pallas_call | solution.py:29
  28.2 3.2 %collective-permute-done.9.refs_4_ = bf16[128,512]{1,0:T(8,128)(2,1)S(1)} collective-permute-done((bf16[128,512]{1,0:T(8,128)(2,1)S(1)}, bf16[128,512]{1,0:T(8,128)(2,1)S(1)}, u32[]{:S(2)}, u32[]{:S(2)}) %collective-permute-start.9) | collective-permute-done | bytes 131104 | tf_op jit(solution)/shard_map/ppermute | solution.py:330
  31.4 0.0 collective-permute-done.8.refs_3_
  31.4 1.1 %shard_map.96 = (f32[256,256]{1,0:T(8,128)}, bf16[256,256]{1,0:T(8,128)(2,1)}) custom-call(f32[256,256]{1,0:T(8,128)S(1)} %shard_map.94.refs_0_, bf16[256,512]{1,0:T(8,128)(2,1)S(1)} %get-tuple-element.50.refs_3_.refs_1_, bf16[128,512]{1,0:T(8,128)(2,1)S(1)} %get-tuple-element.60.refs_2_, bf16[128,512]{1,0:T(8,128)(2,1)S(1)} %collective-permute-done.8.refs_3_, ...), custom_call_target="tpu_custom_call" | custom-call | tf_op jit(solution)/shard_map/pallas_call | solution.py:29
  32.5 0.0 collective-permute-done.11.refs_1_
  32.5 0.0 collective-permute-done.12.refs_2_
  32.5 0.0 collective-permute-done.13.refs_3_
  32.5 0.8 %shard_map.97 = f32[512,128]{1,0:T(8,128)} custom-call(f32[64,1024]{1,0:T(8,128)S(1)} %get-tuple-element.59.refs_6_.refs_0_, bf16[64,1024]{1,0:T(8,128)(2,1)S(1)} %collective-permute-done.11.refs_1_, bf16[64,1024]{1,0:T(8,128)(2,1)S(1)} %collective-permute-done.12.refs_2_, bf16[64,1024]{1,0:T(8,128)(2,1)S(1)} %collective-permute-done.13.refs_3_), custom_call_target="tpu_custom_call" | custom-call | tf_op jit(solution)/shard_map/pallas_call | solution.py:29
  (2 shorter events, 0.0 us)
Async XLA Ops:
  2.1 9.9 %collective-permute-start.2 = (bf16[128,512]{1,0:T(8,128)(2,1)S(1)}, bf16[128,512]{1,0:T(8,128)(2,1)S(1)}, u32[]{:S(2)}, u32[]{:S(2)}) collective-permute-start(bf16[128,512]{1,0:T(8,128)(2,1)S(1)} %get-tuple-element.40), channel_id=1, source_target_pairs={{0,3},{2,5},{4,7},{6,1},{3,0},{5,2},{7,4},{1,6},{8,11},{10,13},{12... | collective-permute-start | bytes 393224 | tf_op jit(solution)/shard_map/ppermute | solution.py:318
  4.6 12.4 %collective-permute-start.6 = (bf16[128,512]{1,0:T(8,128)(2,1)S(1)}, bf16[128,512]{1,0:T(8,128)(2,1)S(1)}, u32[]{:S(2)}, u32[]{:S(2)}) collective-permute-start(bf16[128,512]{1,0:T(8,128)(2,1)S(1)} %get-tuple-element.49), channel_id=1, source_target_pairs={{0,5},{2,7},{4,1},{6,3},{5,0},{7,2},{1,4},{3,6},{8,13},{10,15},{12... | collective-permute-start | bytes 393224 | tf_op jit(solution)/shard_map/ppermute | solution.py:318
  6.3 11.4 %collective-permute-start.5 = (bf16[128,512]{1,0:T(8,128)(2,1)S(1)}, bf16[128,512]{1,0:T(8,128)(2,1)S(1)}, u32[]{:S(2)}, u32[]{:S(2)}) collective-permute-start(bf16[128,512]{1,0:T(8,128)(2,1)S(1)} %get-tuple-element.48), channel_id=1, source_target_pairs={{0,7},{2,1},{4,3},{6,5},{7,0},{1,2},{3,4},{5,6},{8,15},{10,9},{12,... | collective-permute-start | bytes 393224 | tf_op jit(solution)/shard_map/ppermute | solution.py:318
  8.3 4.5 %collective-permute-start = (bf16[64,384]{1,0:T(8,128)(2,1)S(1)}, bf16[64,384]{1,0:T(8,128)(2,1)S(1)}, u32[]{:S(2)}, u32[]{:S(2)}) collective-permute-start(bf16[64,384]{1,0:T(8,128)(2,1)S(1)} %get-tuple-element.37), channel_id=1, source_target_pairs={{0,8},{8,0},{16,24},{24,16},{1,9},{9,1},{17,25},{25,17},{2,10},{10... | collective-permute-start | bytes 147464 | tf_op jit(solution)/shard_map/ppermute | solution.py:320
  9.7 5.0 %collective-permute-start.1 = (bf16[64,384]{1,0:T(8,128)(2,1)S(1)}, bf16[64,384]{1,0:T(8,128)(2,1)S(1)}, u32[]{:S(2)}, u32[]{:S(2)}) collective-permute-start(bf16[64,384]{1,0:T(8,128)(2,1)S(1)} %get-tuple-element.38), channel_id=1, source_target_pairs={{0,24},{8,16},{16,8},{24,0},{1,25},{9,17},{17,9},{25,1},{2,26},{10... | collective-permute-start | bytes 147464 | tf_op jit(solution)/shard_map/ppermute | solution.py:319
  12.0 2.8 %copy-start = (f32[16,16,256]{2,1,0:T(8,128)S(1)}, f32[16,16,256]{2,1,0:T(8,128)}, u32[]{:S(2)}) copy-start(f32[16,16,256]{2,1,0:T(8,128)} %param.6) | copy-start | bytes 786436
  14.9 9.1 %collective-permute-start.3 = (bf16[96,384]{1,0:T(8,128)(2,1)S(1)}, bf16[96,384]{1,0:T(8,128)(2,1)S(1)}, u32[]{:S(2)}, u32[]{:S(2)}) collective-permute-start(bf16[96,384]{1,0:T(8,128)(2,1)S(1)} %get-tuple-element.46), channel_id=1, source_target_pairs={{0,1},{1,0},{2,3},{3,2},{4,5},{5,4},{6,7},{7,6},{8,9},{9,8},{10,11... | collective-permute-start | bytes 221192 | tf_op jit(solution)/shard_map/ppermute | solution.py:344
  15.0 11.5 %collective-permute-start.4 = (bf16[96,384]{1,0:T(8,128)(2,1)S(1)}, bf16[96,384]{1,0:T(8,128)(2,1)S(1)}, u32[]{:S(2)}, u32[]{:S(2)}) collective-permute-start(bf16[96,384]{1,0:T(8,128)(2,1)S(1)} %get-tuple-element.47), channel_id=1, source_target_pairs={{0,7},{1,2},{2,1},{3,4},{4,3},{5,6},{6,5},{7,0},{8,15},{9,10},{10,... | collective-permute-start | bytes 221192 | tf_op jit(solution)/shard_map/ppermute | solution.py:343
  16.2 10.8 %collective-permute-start.10 = (bf16[128,512]{1,0:T(8,128)(2,1)S(1)}, bf16[128,512]{1,0:T(8,128)(2,1)S(1)}, u32[]{:S(2)}, u32[]{:S(2)}) collective-permute-start(bf16[128,512]{1,0:T(8,128)(2,1)S(1)} %shard_map.95), channel_id=1, source_target_pairs={{0,3},{2,5},{4,7},{6,1},{3,0},{5,2},{7,4},{1,6},{8,11},{10,13},{12... | collective-permute-start | bytes 393224 | tf_op jit(solution)/shard_map/ppermute | solution.py:347
  19.2 2.9 %collective-permute-start.7 = (bf16[2,2,64,1024]{3,2,1,0:T(8,128)(2,1)S(1)}, bf16[2,2,64,1024]{3,2,1,0:T(8,128)(2,1)S(1)}, u32[]{:S(2)}, u32[]{:S(2)}) collective-permute-start(bf16[2,2,64,1024]{3,2,1,0:T(8,128)(2,1)S(1)} %get-tuple-element.58), channel_id=1, source_target_pairs={{0,1},{1,0},{2,3},{3,2},{4,5},{5,4},{6,7},{7,6},{8,9},{9,8},{10,11... | collective-permute-start | bytes 1572872 | tf_op jit(solution)/shard_map/ppermute | solution.py:361
  20.6 10.8 %collective-permute-start.9 = (bf16[128,512]{1,0:T(8,128)(2,1)S(1)}, bf16[128,512]{1,0:T(8,128)(2,1)S(1)}, u32[]{:S(2)}, u32[]{:S(2)}) collective-permute-start(bf16[128,512]{1,0:T(8,128)(2,1)S(1)} %get-tuple-element.62), channel_id=1, source_target_pairs={{0,5},{2,7},{4,1},{6,3},{5,0},{7,2},{1,4},{3,6},{8,13},{10,15},{12... | collective-permute-start | bytes 393224 | tf_op jit(solution)/shard_map/ppermute | solution.py:330
  22.2 9.2 %collective-permute-start.8 = (bf16[128,512]{1,0:T(8,128)(2,1)S(1)}, bf16[128,512]{1,0:T(8,128)(2,1)S(1)}, u32[]{:S(2)}, u32[]{:S(2)}) collective-permute-start(bf16[128,512]{1,0:T(8,128)(2,1)S(1)} %get-tuple-element.61), channel_id=1, source_target_pairs={{0,7},{2,1},{4,3},{6,5},{7,0},{1,2},{3,4},{5,6},{8,15},{10,9},{12,... | collective-permute-start | bytes 393224 | tf_op jit(solution)/shard_map/ppermute | solution.py:330
  24.0 8.5 %collective-permute-start.11 = (bf16[64,1024]{1,0:T(8,128)(2,1)S(1)}, bf16[64,1024]{1,0:T(8,128)(2,1)S(1)}, u32[]{:S(2)}, u32[]{:S(2)}) collective-permute-start(bf16[64,1024]{1,0:T(8,128)(2,1)S(1)} %get-tuple-element.66), channel_id=1, source_target_pairs={{0,24},{8,16},{16,8},{24,0},{1,25},{9,17},{17,9},{25,1},{2,26},{10... | collective-permute-start | bytes 393224 | tf_op jit(solution)/shard_map/ppermute | solution.py:370
  26.5 6.0 %collective-permute-start.12 = (bf16[64,1024]{1,0:T(8,128)(2,1)S(1)}, bf16[64,1024]{1,0:T(8,128)(2,1)S(1)}, u32[]{:S(2)}, u32[]{:S(2)}) collective-permute-start(bf16[64,1024]{1,0:T(8,128)(2,1)S(1)} %get-tuple-element.67), channel_id=1, source_target_pairs={{0,8},{8,0},{16,24},{24,16},{1,9},{9,1},{17,25},{25,17},{2,10},{10... | collective-permute-start | bytes 393224 | tf_op jit(solution)/shard_map/ppermute | solution.py:370
  27.0 5.4 %collective-permute-start.13 = (bf16[64,1024]{1,0:T(8,128)(2,1)S(1)}, bf16[64,1024]{1,0:T(8,128)(2,1)S(1)}, u32[]{:S(2)}, u32[]{:S(2)}) collective-permute-start(bf16[64,1024]{1,0:T(8,128)(2,1)S(1)} %get-tuple-element.68), channel_id=1, source_target_pairs={{0,16},{8,24},{16,0},{24,8},{1,17},{9,25},{17,1},{25,9},{2,18},{10... | collective-permute-start | bytes 393224 | tf_op jit(solution)/shard_map/ppermute | solution.py:370

commit v8 on v7

--- a/solution.py
+++ b/solution.py
@@ -8,6 +8,7 @@
 from jax.sharding import PartitionSpec as P
 
 STEPS = 4
+LANES = 32
 BF16 = jnp.bfloat16
 F32 = jnp.float32
 VMEM = pl.BlockSpec(memory_space=pltpu.VMEM)
@@ -47,6 +48,21 @@
 
 def nn(a, b):
     return jnp.dot(a, b, preferred_element_type=F32)
+
+
+def sealed(fields, rates):
+    cells, feats = fields.shape
+    groups = [rates[g : g + 16, :LANES] for g in range(0, cells, 16)]
+    rest = jnp.zeros((16, feats - LANES * len(groups)), F32)
+    return jnp.concatenate([fields, jnp.concatenate([*groups, rest], axis=1)], axis=0).astype(BF16)
+
+
+def opened(message):
+    rows = message.astype(F32)
+    cells = rows.shape[0] - 16
+    lanes = range(0, cells // 16 * LANES, LANES)
+    rates = [jnp.broadcast_to(rows[cells:, at : at + 1], (16, 128)) for at in lanes]
+    return jnp.concatenate([rows[:cells], jnp.concatenate(rates, axis=0)], axis=1)
 
 
 def pack_kernel(owners, cap, wide, high, *refs):
@@ -84,8 +100,8 @@
     odd = lax.rem(lax.axis_index("row"), 2)
     for out, top in ((inner, odd), (outer, 1 - odd)):
         start = pl.multiple_of((1 - top) * (count - strip), strip)
-        out[:, :feats] = state[pl.ds(start, strip)].astype(BF16)
-        out[:, feats:] = jnp.broadcast_to(rate_cols[pl.ds(start, strip)], (strip, 128)).astype(BF16)
+        cells = pl.ds(start, strip)
+        out[...] = sealed(state[cells], jnp.broadcast_to(rate_cols[cells], (strip, 128)))
     for copy in copies[4:]:
         copy.wait()
 
@@ -96,6 +112,7 @@
     half = span // 2
     odd, core = lax.rem(lax.axis_index("row"), 2), lax.axis_index("col")
     low = lax.broadcasted_iota(jnp.int32, (8, feats + 128), 0) < STEPS
+    nears, fars = opened(near[...]), opened(far[...])
     tiles = []
     for r in range(span):
         if r < high:
@@ -112,7 +129,7 @@
         else:
             at = slice((r - high) % STEPS * wide, ((r - high) % STEPS + 1) * wide)
             is_near = (odd == 0) if r < high + STEPS else (odd == 1)
-            both = jnp.where(is_near, near[at].astype(F32), far[at].astype(F32))
+            both = jnp.where(is_near, nears[at], fars[at])
             first = [both[:8], both[wide - 8 :]]
         tiles.append(jnp.where(low, first[0], first[1]))
     lefts, rights = [], []
@@ -120,11 +137,9 @@
         turned = pltpu.roll(tiles[i + half], STEPS, 0)
         lefts.append(jnp.where(low, tiles[i], turned))
         rights.append(jnp.where(low, turned, tiles[i]))
-    for i in range(0, half, 2):
-        one = jnp.concatenate(lefts[i : i + 2], axis=0)
-        two = jnp.concatenate(rights[i : i + 2], axis=0)
-        inner[i * 8 : i * 8 + 16] = jnp.where(core == 0, two, one).astype(BF16)
-        outer[i * 8 : i * 8 + 16] = jnp.where(core == 0, one, two).astype(BF16)
+    one, two = jnp.concatenate(lefts, axis=0), jnp.concatenate(rights, axis=0)
+    for out, strip in ((inner, jnp.where(core == 0, two, one)), (outer, jnp.where(core == 0, one, two))):
+        out[...] = sealed(strip[:, :feats], strip[:, feats:])
     count = state.shape[0]
     same = lax.broadcasted_iota(jnp.int32, (count, count), 0) == lax.broadcasted_iota(
         jnp.int32, (count, count), 1
@@ -141,7 +156,7 @@
     odd, core = lax.rem(lax.axis_index("row"), 2), lax.axis_index("col")
     at = lax.broadcasted_iota(jnp.int32, (8, feats + 128), 0)
     low = jnp.where(core == 0, at, 7 - at) < STEPS
-    ones, twos = inner[...].astype(F32), outer[...].astype(F32)
+    ones, twos = opened(inner[...]), opened(outer[...])
     for i in range(half):
         one, two = ones[i * 8 : i * 8 + 8], twos[i * 8 : i * 8 + 8]
         this = jnp.where(low, one, two)
@@ -152,9 +167,10 @@
     for r in range(high):
         grid[0, r, :wide] = state[r * wide : (r + 1) * wide]
         rates[r, :wide] = jnp.broadcast_to(rate[r * wide : (r + 1) * wide], (wide, 128))
-    for at in range(STEPS):
-        for ref, start in ((near, high + STEPS * odd), (far, high + STEPS * (1 - odd))):
-            strip = ref[at * wide : (at + 1) * wide].astype(F32)
+    for ref, start in ((near, high + STEPS * odd), (far, high + STEPS * (1 - odd))):
+        cells = opened(ref[...])
+        for at in range(STEPS):
+            strip = cells[at * wide : (at + 1) * wide]
             grid[0, start + at, :wide] = strip[:, :feats]
             rates[start + at, :wide] = strip[:, feats:]
     for step in range(STEPS):
@@ -298,7 +314,7 @@
     flat_cot = cotangent.reshape(count, feats)
 
     weight = shape((feats, hidden), BF16)
-    strip = shape((STEPS * wide, feats + 128), BF16)
+    strip = shape((STEPS * wide + 16, feats), BF16)
     *chunks, inner, outer, rate_col, place_row, weight_in, weight_out = call(
         functools.partial(pack_kernel, owners, cap, wide, high),
         [dest.reshape(1, count), rate, flat_state, flat_cot, w_in[0], w_out[0]],
@@ -333,7 +349,7 @@
     physics(0)
     done = (acts[0],)
     done = physics(3, done, True)
-    side = shape(((high + 2 * STEPS) * STEPS, feats + 128), BF16)
+    side = shape(((high + 2 * STEPS) * STEPS + 16, feats), BF16)
     inner, outer, places = call(
         functools.partial(edge_kernel, wide, high),
         [flat_state, rate_col, near, far, place_row],

time: 33.4 us -> 33.4 us (level)
  no operation moved by 1% of the time
where the time goes in v8:
time: 33.4 us; the launch traced here: 33.2 us
  starting transfers between devices  19.4 us (58%)
  Pallas kernels  8.01 us (24%)
  waiting for transfers between devices  5.03 us (15%)
  between operations  0.75 us (2%)
    pallas_call x13, Pallas kernels, call(): pl.pallas_call(body, out_shape=list(outs), in_specs=specs + [ANY] * len(a...  8.01 us
    ppermute x3, starting transfers between devices, local(): got[k] = lax.ppermute(chunks[k], ('grp', 'col'), partners(k))  6.19 us
    ppermute x3, starting transfers between devices, local(): lax.ppermute(s, 'row', swap('row', bit))  3.55 us
    ppermute x2, starting transfers between devices, physics(): backs[k] = lax.ppermute(backs[k], ('grp', 'col'), partners(k))  3.26 us
    ppermute x2, waiting for transfers between devices, physics(): backs[k] = lax.ppermute(backs[k], ('grp', 'col'), partners(k))  3.1 us
    ppermute x1, waiting for transfers between devices, local(): far = lax.ppermute(outer, 'row', outward('row'))  1.9 us
    ppermute x1, starting transfers between devices, local(): near = lax.ppermute(inner, 'row', swap('row', 1))  1.49 us
    ppermute x1, starting transfers between devices, local(): far = lax.ppermute(outer, 'row', outward('row'))  1.49 us
  transfers between devices with their start and end apart: 14, of which 2 were waited for; matrix products, arithmetic and copies ran while one was open for 0% of the time, Pallas kernels for 17%

profile of v8, /device:TPU:0, one launch (start us, length us, event | category | flops | bytes accessed | tf_op | source)
XLA Modules:
  0.0 33.2 jit_solution(14486895546290974322)
XLA Ops:
  0.6 1.4 %shard_map.85 = (bf16[128,512]{1,0:T(8,128)(2,1)S(1)}, bf16[128,512]{1,0:T(8,128)(2,1)S(1)}, bf16[128,512]{1,0:T(8,128)(2,1)S(1)}, bf16[128,512]{1,0:T(8,128)(2,...) custom-call(s32[1,256]{1,0:T(1,128)} %bitcast.15, ...), custom_call_target="tpu_custom_call" | custom-call | tf_op jit(solution)/shard_map/pallas_call | solution.py:30
  2.1 2.5 %collective-permute-start.2 = (bf16[128,512]{1,0:T(8,128)(2,1)S(1)}, bf16[128,512]{1,0:T(8,128)(2,1)S(1)}, u32[]{:S(2)}, u32[]{:S(2)}) collective-permute-start(bf16[128,512]{1,0:T(8,128)(2,1)S(1)} %get-tuple-element.40), channel_id=1, source_target_pairs={{0,3},{2,5},{4,7},{6,1},{3,0},{5,2},{7,4},{1,6},{8,11},{10,13},{12... | collective-permute-start | bytes 393224 | tf_op jit(solution)/shard_map/ppermute | solution.py:334
  4.6 1.7 %collective-permute-start.6 = (bf16[128,512]{1,0:T(8,128)(2,1)S(1)}, bf16[128,512]{1,0:T(8,128)(2,1)S(1)}, u32[]{:S(2)}, u32[]{:S(2)}) collective-permute-start(bf16[128,512]{1,0:T(8,128)(2,1)S(1)} %get-tuple-element.49), channel_id=1, source_target_pairs={{0,5},{2,7},{4,1},{6,3},{5,0},{7,2},{1,4},{3,6},{8,13},{10,15},{12... | collective-permute-start | bytes 393224 | tf_op jit(solution)/shard_map/ppermute | solution.py:334
  6.3 1.9 %collective-permute-start.5 = (bf16[128,512]{1,0:T(8,128)(2,1)S(1)}, bf16[128,512]{1,0:T(8,128)(2,1)S(1)}, u32[]{:S(2)}, u32[]{:S(2)}) collective-permute-start(bf16[128,512]{1,0:T(8,128)(2,1)S(1)} %get-tuple-element.48), channel_id=1, source_target_pairs={{0,7},{2,1},{4,3},{6,5},{7,0},{1,2},{3,4},{5,6},{8,15},{10,9},{12,... | collective-permute-start | bytes 393224 | tf_op jit(solution)/shard_map/ppermute | solution.py:334
  8.3 1.5 %collective-permute-start = (bf16[80,256]{1,0:T(8,128)(2,1)S(1)}, bf16[80,256]{1,0:T(8,128)(2,1)S(1)}, u32[]{:S(2)}, u32[]{:S(2)}) collective-permute-start(bf16[80,256]{1,0:T(8,128)(2,1)S(1)} %get-tuple-element.37), channel_id=1, source_target_pairs={{0,8},{8,0},{16,24},{24,16},{1,9},{9,1},{17,25},{25,17},{2,10},{10... | collective-permute-start | bytes 122888 | tf_op jit(solution)/shard_map/ppermute | solution.py:336
  9.7 1.5 %collective-permute-start.1 = (bf16[80,256]{1,0:T(8,128)(2,1)S(1)}, bf16[80,256]{1,0:T(8,128)(2,1)S(1)}, u32[]{:S(2)}, u32[]{:S(2)}) collective-permute-start(bf16[80,256]{1,0:T(8,128)(2,1)S(1)} %get-tuple-element.38), channel_id=1, source_target_pairs={{0,24},{8,16},{16,8},{24,0},{1,25},{9,17},{17,9},{25,1},{2,26},{10... | collective-permute-start | bytes 122888 | tf_op jit(solution)/shard_map/ppermute | solution.py:335
  11.2 0.7 %shard_map.86 = (bf16[128,512]{1,0:T(8,128)(2,1)S(1)}, bf16[128,1024]{1,0:T(8,128)(2,1)S(1)}, bf16[128,1024]{1,0:T(8,128)(2,1)S(1)}) custom-call(bf16[128,512]{1,0:T(8,128)(2,1)S(1)} %get-tuple-element.43.refs_0_, bf16[256,1024]{1,0:T(8,128)(2,1)S(1)} %get-tuple-element.41.refs_1_, bf16[256,1024]{1,0:T(8,128)(2,1)S(1)} %get-tuple-element.42.refs_2_), custom_call_target="tpu_custom_call" | custom-call | tf_op jit(solution)/shard_map/pallas_call | solution.py:30
  12.0 0.0 collective-permute-done.2.refs_0_.refs_3_
  12.0 0.0 copy-start
  12.0 0.7 %shard_map.87 = (bf16[128,512]{1,0:T(8,128)(2,1)S(1)}, bf16[128,1024]{1,0:T(8,128)(2,1)S(1)}, bf16[128,1024]{1,0:T(8,128)(2,1)S(1)}) custom-call(bf16[128,512]{1,0:T(8,128)(2,1)S(1)} %collective-permute-done.2.refs_0_.refs_3_, bf16[256,1024]{1,0:T(8,128)(2,1)S(1)} %get-tuple-element.41.refs_1_, bf16[256,1024]{1,0:T(8,128)(2,1)S(1)} %get-tuple-element.42.refs_2_, ...), custom_call_target="tpu_custom_call" | custom-call | tf_op jit(solution)/shard_map/pallas_call | solution.py:30
  12.7 0.0 collective-permute-done.refs_2_
  12.7 1.9 %collective-permute-done.1.refs_3_ = bf16[80,256]{1,0:T(8,128)(2,1)S(1)} collective-permute-done((bf16[80,256]{1,0:T(8,128)(2,1)S(1)}, bf16[80,256]{1,0:T(8,128)(2,1)S(1)}, u32[]{:S(2)}, u32[]{:S(2)}) %collective-permute-start.1) | collective-permute-done | bytes 40992 | tf_op jit(solution)/shard_map/ppermute | solution.py:335
  14.6 0.0 copy-done
  14.7 0.2 shard_map.88
  14.9 0.1 collective-permute-start.3
  15.0 1.3 %collective-permute-start.4 = (bf16[112,256]{1,0:T(8,128)(2,1)S(1)}, bf16[112,256]{1,0:T(8,128)(2,1)S(1)}, u32[]{:S(2)}, u32[]{:S(2)}) collective-permute-start(bf16[112,256]{1,0:T(8,128)(2,1)S(1)} %get-tuple-element.47), channel_id=1, source_target_pairs={{0,7},{1,2},{2,1},{3,4},{4,3},{5,6},{6,5},{7,0},{8,15},{9,10},{10,... | collective-permute-start | bytes 172040 | tf_op jit(solution)/shard_map/ppermute | solution.py:359
  16.3 0.7 %collective-permute-start.10 = (bf16[128,512]{1,0:T(8,128)(2,1)S(1)}, bf16[128,512]{1,0:T(8,128)(2,1)S(1)}, u32[]{:S(2)}, u32[]{:S(2)}) collective-permute-start(bf16[128,512]{1,0:T(8,128)(2,1)S(1)} %shard_map.95), channel_id=1, source_target_pairs={{0,3},{2,5},{4,7},{6,1},{3,0},{5,2},{7,4},{1,6},{8,11},{10,13},{12... | collective-permute-start | bytes 393224 | tf_op jit(solution)/shard_map/ppermute | solution.py:363
  17.0 0.0 collective-permute-done.6.refs_0_.refs_2_
  17.0 0.7 %shard_map.89 = (bf16[128,512]{1,0:T(8,128)(2,1)S(1)}, bf16[128,1024]{1,0:T(8,128)(2,1)S(1)}, bf16[128,1024]{1,0:T(8,128)(2,1)S(1)}) custom-call(bf16[128,512]{1,0:T(8,128)(2,1)S(1)} %collective-permute-done.6.refs_0_.refs_2_, bf16[256,1024]{1,0:T(8,128)(2,1)S(1)} %get-tuple-element.41.refs_1_, bf16[256,1024]{1,0:T(8,128)(2,1)S(1)} %get-tuple-element.42.refs_2_, ...), custom_call_target="tpu_custom_call" | custom-call | tf_op jit(solution)/shard_map/pallas_call | solution.py:30
  17.7 0.0 collective-permute-done.5.refs_0_.refs_1_
  17.7 0.7 %shard_map.90 = (bf16[128,512]{1,0:T(8,128)(2,1)S(1)}, bf16[128,1024]{1,0:T(8,128)(2,1)S(1)}, bf16[128,1024]{1,0:T(8,128)(2,1)S(1)}) custom-call(bf16[128,512]{1,0:T(8,128)(2,1)S(1)} %collective-permute-done.5.refs_0_.refs_1_, bf16[256,1024]{1,0:T(8,128)(2,1)S(1)} %get-tuple-element.41.refs_1_, bf16[256,1024]{1,0:T(8,128)(2,1)S(1)} %get-tuple-element.42.refs_2_, ...), custom_call_target="tpu_custom_call" | custom-call | tf_op jit(solution)/shard_map/pallas_call | solution.py:30
  18.4 0.8 %shard_map.91 = (f32[2,2,64,1024]{3,2,1,0:T(8,128)S(1)}, bf16[2,2,64,1024]{3,2,1,0:T(8,128)(2,1)S(1)}) custom-call(bf16[128,512]{1,0:T(8,128)(2,1)S(1)} %get-tuple-element.43.refs_0_, bf16[128,512]{1,0:T(8,128)(2,1)S(1)} %collective-permute-done.5.refs_0_.refs_1_, bf16[128,512]{1,0:T(8,128)(2,1)S(1)} %collective-permute-done.6.refs_0_.refs_2_, ...), custom_call_target="tpu_custom_call" | custom-call | tf_op jit(solution)/shard_map/pallas_call | solution.py:30
  19.2 1.4 %collective-permute-start.7 = (bf16[2,2,64,1024]{3,2,1,0:T(8,128)(2,1)S(1)}, bf16[2,2,64,1024]{3,2,1,0:T(8,128)(2,1)S(1)}, u32[]{:S(2)}, u32[]{:S(2)}) collective-permute-start(bf16[2,2,64,1024]{3,2,1,0:T(8,128)(2,1)S(1)} %get-tuple-element.58), channel_id=1, source_target_pairs={{0,1},{1,0},{2,3},{3,2},{4,5},{5,4},{6,7},{7,6},{8,9},{9,8},{10,11... | collective-permute-start | bytes 1572872 | tf_op jit(solution)/shard_map/ppermute | solution.py:377
  20.6 1.6 %collective-permute-start.9 = (bf16[128,512]{1,0:T(8,128)(2,1)S(1)}, bf16[128,512]{1,0:T(8,128)(2,1)S(1)}, u32[]{:S(2)}, u32[]{:S(2)}) collective-permute-start(bf16[128,512]{1,0:T(8,128)(2,1)S(1)} %get-tuple-element.62), channel_id=1, source_target_pairs={{0,5},{2,7},{4,1},{6,3},{5,0},{7,2},{1,4},{3,6},{8,13},{10,15},{12... | collective-permute-start | bytes 393224 | tf_op jit(solution)/shard_map/ppermute | solution.py:346
  22.2 0.0 collective-permute-done.7.refs_1_
  22.2 1.7 %collective-permute-start.8 = (bf16[128,512]{1,0:T(8,128)(2,1)S(1)}, bf16[128,512]{1,0:T(8,128)(2,1)S(1)}, u32[]{:S(2)}, u32[]{:S(2)}) collective-permute-start(bf16[128,512]{1,0:T(8,128)(2,1)S(1)} %get-tuple-element.61), channel_id=1, source_target_pairs={{0,7},{2,1},{4,3},{6,5},{7,0},{1,2},{3,4},{5,6},{8,15},{10,9},{12,... | collective-permute-start | bytes 393224 | tf_op jit(solution)/shard_map/ppermute | solution.py:346
  23.9 0.1 shard_map.93
  24.0 0.0 collective-permute-done.3.refs_4_
  24.0 2.5 %collective-permute-start.11 = (bf16[64,1024]{1,0:T(8,128)(2,1)S(1)}, bf16[64,1024]{1,0:T(8,128)(2,1)S(1)}, u32[]{:S(2)}, u32[]{:S(2)}) collective-permute-start(bf16[64,1024]{1,0:T(8,128)(2,1)S(1)} %get-tuple-element.66), channel_id=1, source_target_pairs={{0,24},{8,16},{16,8},{24,0},{1,25},{9,17},{17,9},{25,1},{2,26},{10... | collective-permute-start | bytes 393224 | tf_op jit(solution)/shard_map/ppermute | solution.py:386
  26.5 0.0 collective-permute-done.4.refs_5_
  26.5 0.5 %collective-permute-start.12 = (bf16[64,1024]{1,0:T(8,128)(2,1)S(1)}, bf16[64,1024]{1,0:T(8,128)(2,1)S(1)}, u32[]{:S(2)}, u32[]{:S(2)}) collective-permute-start(bf16[64,1024]{1,0:T(8,128)(2,1)S(1)} %get-tuple-element.67), channel_id=1, source_target_pairs={{0,8},{8,0},{16,24},{24,16},{1,9},{9,1},{17,25},{25,17},{2,10},{10... | collective-permute-start | bytes 393224 | tf_op jit(solution)/shard_map/ppermute | solution.py:386
  27.0 0.0 collective-permute-done.10.refs_5_
  27.0 0.5 %collective-permute-start.13 = (bf16[64,1024]{1,0:T(8,128)(2,1)S(1)}, bf16[64,1024]{1,0:T(8,128)(2,1)S(1)}, u32[]{:S(2)}, u32[]{:S(2)}) collective-permute-start(bf16[64,1024]{1,0:T(8,128)(2,1)S(1)} %get-tuple-element.68), channel_id=1, source_target_pairs={{0,16},{8,24},{16,0},{24,8},{1,17},{9,25},{17,1},{25,9},{2,18},{10... | collective-permute-start | bytes 393224 | tf_op jit(solution)/shard_map/ppermute | solution.py:386
  27.5 0.8 %shard_map.94.refs_0_ = f32[256,256]{1,0:T(8,128)S(1)} custom-call(f32[256,256]{1,0:T(8,128)S(1)} %bitcast.10, f32[256,1]{1,0:T(8,128)S(1)} %get-tuple-element.36.refs_1_, bf16[80,256]{1,0:T(8,128)(2,1)S(1)} %collective-permute-done.refs_2_, bf16[80,256]{1,0:T(8,128)(2,1)S(1)} %collective-permute-done.1.refs_3_, ...), custom_call_target="tpu_custom_call" | custom-call | tf_op jit(solution)/shard_map/pallas_call | solution.py:30
  28.3 3.1 %collective-permute-done.9.refs_4_ = bf16[128,512]{1,0:T(8,128)(2,1)S(1)} collective-permute-done((bf16[128,512]{1,0:T(8,128)(2,1)S(1)}, bf16[128,512]{1,0:T(8,128)(2,1)S(1)}, u32[]{:S(2)}, u32[]{:S(2)}) %collective-permute-start.9) | collective-permute-done | bytes 131104 | tf_op jit(solution)/shard_map/ppermute | solution.py:346
  31.4 0.0 collective-permute-done.8.refs_3_
  31.4 1.1 %shard_map.96 = (f32[256,256]{1,0:T(8,128)}, bf16[256,256]{1,0:T(8,128)(2,1)}) custom-call(f32[256,256]{1,0:T(8,128)S(1)} %shard_map.94.refs_0_, bf16[256,512]{1,0:T(8,128)(2,1)S(1)} %get-tuple-element.50.refs_3_.refs_1_, bf16[128,512]{1,0:T(8,128)(2,1)S(1)} %get-tuple-element.60.refs_2_, bf16[128,512]{1,0:T(8,128)(2,1)S(1)} %collective-permute-done.8.refs_3_, ...), custom_call_target="tpu_custom_call" | custom-call | tf_op jit(solution)/shard_map/pallas_call | solution.py:30
  32.4 0.0 collective-permute-done.11.refs_1_
  32.5 0.0 collective-permute-done.12.refs_2_
  32.5 0.0 collective-permute-done.13.refs_3_
  32.5 0.8 %shard_map.97 = f32[512,128]{1,0:T(8,128)} custom-call(f32[64,1024]{1,0:T(8,128)S(1)} %get-tuple-element.59.refs_6_.refs_0_, bf16[64,1024]{1,0:T(8,128)(2,1)S(1)} %collective-permute-done.11.refs_1_, bf16[64,1024]{1,0:T(8,128)(2,1)S(1)} %collective-permute-done.12.refs_2_, bf16[64,1024]{1,0:T(8,128)(2,1)S(1)} %collective-permute-done.13.refs_3_), custom_call_target="tpu_custom_call" | custom-call | tf_op jit(solution)/shard_map/pallas_call | solution.py:30
  (2 shorter events, 0.0 us)
Async XLA Ops:
  2.1 9.9 %collective-permute-start.2 = (bf16[128,512]{1,0:T(8,128)(2,1)S(1)}, bf16[128,512]{1,0:T(8,128)(2,1)S(1)}, u32[]{:S(2)}, u32[]{:S(2)}) collective-permute-start(bf16[128,512]{1,0:T(8,128)(2,1)S(1)} %get-tuple-element.40), channel_id=1, source_target_pairs={{0,3},{2,5},{4,7},{6,1},{3,0},{5,2},{7,4},{1,6},{8,11},{10,13},{12... | collective-permute-start | bytes 393224 | tf_op jit(solution)/shard_map/ppermute | solution.py:334
  4.6 12.4 %collective-permute-start.6 = (bf16[128,512]{1,0:T(8,128)(2,1)S(1)}, bf16[128,512]{1,0:T(8,128)(2,1)S(1)}, u32[]{:S(2)}, u32[]{:S(2)}) collective-permute-start(bf16[128,512]{1,0:T(8,128)(2,1)S(1)} %get-tuple-element.49), channel_id=1, source_target_pairs={{0,5},{2,7},{4,1},{6,3},{5,0},{7,2},{1,4},{3,6},{8,13},{10,15},{12... | collective-permute-start | bytes 393224 | tf_op jit(solution)/shard_map/ppermute | solution.py:334
  6.3 11.4 %collective-permute-start.5 = (bf16[128,512]{1,0:T(8,128)(2,1)S(1)}, bf16[128,512]{1,0:T(8,128)(2,1)S(1)}, u32[]{:S(2)}, u32[]{:S(2)}) collective-permute-start(bf16[128,512]{1,0:T(8,128)(2,1)S(1)} %get-tuple-element.48), channel_id=1, source_target_pairs={{0,7},{2,1},{4,3},{6,5},{7,0},{1,2},{3,4},{5,6},{8,15},{10,9},{12,... | collective-permute-start | bytes 393224 | tf_op jit(solution)/shard_map/ppermute | solution.py:334
  8.3 4.5 %collective-permute-start = (bf16[80,256]{1,0:T(8,128)(2,1)S(1)}, bf16[80,256]{1,0:T(8,128)(2,1)S(1)}, u32[]{:S(2)}, u32[]{:S(2)}) collective-permute-start(bf16[80,256]{1,0:T(8,128)(2,1)S(1)} %get-tuple-element.37), channel_id=1, source_target_pairs={{0,8},{8,0},{16,24},{24,16},{1,9},{9,1},{17,25},{25,17},{2,10},{10... | collective-permute-start | bytes 122888 | tf_op jit(solution)/shard_map/ppermute | solution.py:336
  9.7 4.9 %collective-permute-start.1 = (bf16[80,256]{1,0:T(8,128)(2,1)S(1)}, bf16[80,256]{1,0:T(8,128)(2,1)S(1)}, u32[]{:S(2)}, u32[]{:S(2)}) collective-permute-start(bf16[80,256]{1,0:T(8,128)(2,1)S(1)} %get-tuple-element.38), channel_id=1, source_target_pairs={{0,24},{8,16},{16,8},{24,0},{1,25},{9,17},{17,9},{25,1},{2,26},{10... | collective-permute-start | bytes 122888 | tf_op jit(solution)/shard_map/ppermute | solution.py:335
  12.0 2.7 %copy-start = (f32[16,16,256]{2,1,0:T(8,128)S(1)}, f32[16,16,256]{2,1,0:T(8,128)}, u32[]{:S(2)}) copy-start(f32[16,16,256]{2,1,0:T(8,128)} %param.6) | copy-start | bytes 786436
  14.9 9.1 %collective-permute-start.3 = (bf16[112,256]{1,0:T(8,128)(2,1)S(1)}, bf16[112,256]{1,0:T(8,128)(2,1)S(1)}, u32[]{:S(2)}, u32[]{:S(2)}) collective-permute-start(bf16[112,256]{1,0:T(8,128)(2,1)S(1)} %get-tuple-element.46), channel_id=1, source_target_pairs={{0,1},{1,0},{2,3},{3,2},{4,5},{5,4},{6,7},{7,6},{8,9},{9,8},{10,11... | collective-permute-start | bytes 172040 | tf_op jit(solution)/shard_map/ppermute | solution.py:360
  15.0 11.5 %collective-permute-start.4 = (bf16[112,256]{1,0:T(8,128)(2,1)S(1)}, bf16[112,256]{1,0:T(8,128)(2,1)S(1)}, u32[]{:S(2)}, u32[]{:S(2)}) collective-permute-start(bf16[112,256]{1,0:T(8,128)(2,1)S(1)} %get-tuple-element.47), channel_id=1, source_target_pairs={{0,7},{1,2},{2,1},{3,4},{4,3},{5,6},{6,5},{7,0},{8,15},{9,10},{10,... | collective-permute-start | bytes 172040 | tf_op jit(solution)/shard_map/ppermute | solution.py:359
  16.3 10.7 %collective-permute-start.10 = (bf16[128,512]{1,0:T(8,128)(2,1)S(1)}, bf16[128,512]{1,0:T(8,128)(2,1)S(1)}, u32[]{:S(2)}, u32[]{:S(2)}) collective-permute-start(bf16[128,512]{1,0:T(8,128)(2,1)S(1)} %shard_map.95), channel_id=1, source_target_pairs={{0,3},{2,5},{4,7},{6,1},{3,0},{5,2},{7,4},{1,6},{8,11},{10,13},{12... | collective-permute-start | bytes 393224 | tf_op jit(solution)/shard_map/ppermute | solution.py:363
  19.2 3.0 %collective-permute-start.7 = (bf16[2,2,64,1024]{3,2,1,0:T(8,128)(2,1)S(1)}, bf16[2,2,64,1024]{3,2,1,0:T(8,128)(2,1)S(1)}, u32[]{:S(2)}, u32[]{:S(2)}) collective-permute-start(bf16[2,2,64,1024]{3,2,1,0:T(8,128)(2,1)S(1)} %get-tuple-element.58), channel_id=1, source_target_pairs={{0,1},{1,0},{2,3},{3,2},{4,5},{5,4},{6,7},{7,6},{8,9},{9,8},{10,11... | collective-permute-start | bytes 1572872 | tf_op jit(solution)/shard_map/ppermute | solution.py:377
  20.6 10.8 %collective-permute-start.9 = (bf16[128,512]{1,0:T(8,128)(2,1)S(1)}, bf16[128,512]{1,0:T(8,128)(2,1)S(1)}, u32[]{:S(2)}, u32[]{:S(2)}) collective-permute-start(bf16[128,512]{1,0:T(8,128)(2,1)S(1)} %get-tuple-element.62), channel_id=1, source_target_pairs={{0,5},{2,7},{4,1},{6,3},{5,0},{7,2},{1,4},{3,6},{8,13},{10,15},{12... | collective-permute-start | bytes 393224 | tf_op jit(solution)/shard_map/ppermute | solution.py:346
  22.2 9.2 %collective-permute-start.8 = (bf16[128,512]{1,0:T(8,128)(2,1)S(1)}, bf16[128,512]{1,0:T(8,128)(2,1)S(1)}, u32[]{:S(2)}, u32[]{:S(2)}) collective-permute-start(bf16[128,512]{1,0:T(8,128)(2,1)S(1)} %get-tuple-element.61), channel_id=1, source_target_pairs={{0,7},{2,1},{4,3},{6,5},{7,0},{1,2},{3,4},{5,6},{8,15},{10,9},{12,... | collective-permute-start | bytes 393224 | tf_op jit(solution)/shard_map/ppermute | solution.py:346
  24.0 8.5 %collective-permute-start.11 = (bf16[64,1024]{1,0:T(8,128)(2,1)S(1)}, bf16[64,1024]{1,0:T(8,128)(2,1)S(1)}, u32[]{:S(2)}, u32[]{:S(2)}) collective-permute-start(bf16[64,1024]{1,0:T(8,128)(2,1)S(1)} %get-tuple-element.66), channel_id=1, source_target_pairs={{0,24},{8,16},{16,8},{24,0},{1,25},{9,17},{17,9},{25,1},{2,26},{10... | collective-permute-start | bytes 393224 | tf_op jit(solution)/shard_map/ppermute | solution.py:386
  26.5 6.0 %collective-permute-start.12 = (bf16[64,1024]{1,0:T(8,128)(2,1)S(1)}, bf16[64,1024]{1,0:T(8,128)(2,1)S(1)}, u32[]{:S(2)}, u32[]{:S(2)}) collective-permute-start(bf16[64,1024]{1,0:T(8,128)(2,1)S(1)} %get-tuple-element.67), channel_id=1, source_target_pairs={{0,8},{8,0},{16,24},{24,16},{1,9},{9,1},{17,25},{25,17},{2,10},{10... | collective-permute-start | bytes 393224 | tf_op jit(solution)/shard_map/ppermute | solution.py:386
  27.0 5.4 %collective-permute-start.13 = (bf16[64,1024]{1,0:T(8,128)(2,1)S(1)}, bf16[64,1024]{1,0:T(8,128)(2,1)S(1)}, u32[]{:S(2)}, u32[]{:S(2)}) collective-permute-start(bf16[64,1024]{1,0:T(8,128)(2,1)S(1)} %get-tuple-element.68), channel_id=1, source_target_pairs={{0,16},{8,24},{16,0},{24,8},{1,17},{9,25},{17,1},{25,9},{2,18},{10... | collective-permute-start | bytes 393224 | tf_op jit(solution)/shard_map/ppermute | solution.py:386

commit v9 on v8

--- a/solution.py
+++ b/solution.py
@@ -106,7 +106,7 @@
         copy.wait()
 
 
-def edge_kernel(wide, high, state, rate, near, far, place_row, inner, outer, places):
+def edge_kernel(wide, high, state, rate, near, far, inner, outer):
     feats = state.shape[1]
     span = high + 2 * STEPS
     half = span // 2
@@ -140,6 +140,9 @@
     one, two = jnp.concatenate(lefts, axis=0), jnp.concatenate(rights, axis=0)
     for out, strip in ((inner, jnp.where(core == 0, two, one)), (outer, jnp.where(core == 0, one, two))):
         out[...] = sealed(strip[:, :feats], strip[:, feats:])
+
+
+def flow_kernel(wide, high, state, rate, near, far, inner, outer, place_row, out, places, grid, rates):
     count = state.shape[0]
     same = lax.broadcasted_iota(jnp.int32, (count, count), 0) == lax.broadcasted_iota(
         jnp.int32, (count, count), 1
@@ -147,9 +150,6 @@
     place = jnp.sum(jnp.where(same, place_row[...], 0).astype(F32), axis=1, keepdims=True)
     hits = lax.broadcasted_iota(jnp.int32, places.shape, 1) == place.astype(jnp.int32)
     places[...] = hits.astype(F32).astype(BF16)
-
-
-def flow_kernel(wide, high, state, rate, near, far, inner, outer, out, grid, rates):
     feats = state.shape[1]
     span, across = high + 2 * STEPS, wide + 2 * STEPS
     half = span // 2
@@ -350,16 +350,16 @@
     done = (acts[0],)
     done = physics(3, done, True)
     side = shape(((high + 2 * STEPS) * STEPS + 16, feats), BF16)
-    inner, outer, places = call(
+    inner, outer = call(
         functools.partial(edge_kernel, wide, high),
-        [flat_state, rate_col, near, far, place_row],
-        [side, side, shape((count, owners * cap), BF16)],
+        [flat_state, rate_col, near, far],
+        [side, side],
         after=done,
     )
     outer_back = lax.ppermute(outer, ("grp", "col"), outward(("grp", "col")))
     inner_back = lax.ppermute(inner, "col", swap("col", 1))
-    done = (places,)
-    (back,) = call(hold_kernel, [backs[3]], [shape(backs[3].shape, BF16)], after=(places,))
+    done = (inner,)
+    (back,) = call(hold_kernel, [backs[3]], [shape(backs[3].shape, BF16)], after=(inner,))
     backs[3] = lax.ppermute(back, ("grp", "col"), partners(3))
     done = physics(2, done)
     done = physics(1, done)
@@ -397,10 +397,10 @@
         summed = lax.psum_scatter(
             flat.reshape(-1, 128), ("row", "col"), scatter_dimension=0, tiled=True
         )
-    (field,) = call(
+    field, places = call(
         functools.partial(flow_kernel, wide, high),
-        [flat_state, rate_col, near, far, inner_back, outer_back],
-        [shape((count, feats), F32)],
+        [flat_state, rate_col, near, far, inner_back, outer_back, place_row],
+        [shape((count, feats), F32), shape((count, owners * cap), BF16)],
         [
             pltpu.VMEM((2, high + 2 * STEPS, wide + 2 * STEPS, feats), F32),
             pltpu.VMEM((high + 2 * STEPS, wide + 2 * STEPS, 128), F32),

time: 33.4 us -> 33.4 us (level)
  transfers between devices with their start and end apart: 14 -> 14, of which waited for: 2 -> 2; matrix products, arithmetic and copies ran while one was open for 0% -> 0% of each run, Pallas kernels for 17% -> 18%
where the time goes in v9:
time: 33.4 us; the launch traced here: 33.2 us
  starting transfers between devices  19.5 us (58%)
  Pallas kernels  8.07 us (24%)
  waiting for transfers between devices  4.92 us (15%)
  between operations  0.75 us (2%)
    pallas_call x13, Pallas kernels, call(): pl.pallas_call(body, out_shape=list(outs), in_specs=specs + [ANY] * len(a...  8.07 us
    ppermute x3, starting transfers between devices, local(): got[k] = lax.ppermute(chunks[k], ('grp', 'col'), partners(k))  6.19 us
    ppermute x3, starting transfers between devices, local(): lax.ppermute(s, 'row', swap('row', bit))  3.55 us
    ppermute x2, starting transfers between devices, physics(): backs[k] = lax.ppermute(backs[k], ('grp', 'col'), partners(k))  3.31 us
    ppermute x2, waiting for transfers between devices, physics(): backs[k] = lax.ppermute(backs[k], ('grp', 'col'), partners(k))  2.98 us
    ppermute x1, waiting for transfers between devices, local(): far = lax.ppermute(outer, 'row', outward('row'))  1.91 us
    ppermute x1, starting transfers between devices, local(): near = lax.ppermute(inner, 'row', swap('row', 1))  1.49 us
    ppermute x1, starting transfers between devices, local(): far = lax.ppermute(outer, 'row', outward('row'))  1.49 us
  transfers between devices with their start and end apart: 14, of which 2 were waited for; matrix products, arithmetic and copies ran while one was open for 0% of the time, Pallas kernels for 18%

profile of v9, /device:TPU:0, one launch (start us, length us, event | category | flops | bytes accessed | tf_op | source)
XLA Modules:
  0.0 33.2 jit_solution(10160682114255008208)
XLA Ops:
  0.6 1.4 %shard_map.85 = (bf16[128,512]{1,0:T(8,128)(2,1)S(1)}, bf16[128,512]{1,0:T(8,128)(2,1)S(1)}, bf16[128,512]{1,0:T(8,128)(2,1)S(1)}, bf16[128,512]{1,0:T(8,128)(2,...) custom-call(s32[1,256]{1,0:T(1,128)} %bitcast.15, ...), custom_call_target="tpu_custom_call" | custom-call | tf_op jit(solution)/shard_map/pallas_call | solution.py:30
  2.1 2.5 %collective-permute-start.2 = (bf16[128,512]{1,0:T(8,128)(2,1)S(1)}, bf16[128,512]{1,0:T(8,128)(2,1)S(1)}, u32[]{:S(2)}, u32[]{:S(2)}) collective-permute-start(bf16[128,512]{1,0:T(8,128)(2,1)S(1)} %get-tuple-element.40), channel_id=1, source_target_pairs={{0,3},{2,5},{4,7},{6,1},{3,0},{5,2},{7,4},{1,6},{8,11},{10,13},{12... | collective-permute-start | bytes 393224 | tf_op jit(solution)/shard_map/ppermute | solution.py:334
  4.6 1.7 %collective-permute-start.6 = (bf16[128,512]{1,0:T(8,128)(2,1)S(1)}, bf16[128,512]{1,0:T(8,128)(2,1)S(1)}, u32[]{:S(2)}, u32[]{:S(2)}) collective-permute-start(bf16[128,512]{1,0:T(8,128)(2,1)S(1)} %get-tuple-element.50), channel_id=1, source_target_pairs={{0,5},{2,7},{4,1},{6,3},{5,0},{7,2},{1,4},{3,6},{8,13},{10,15},{12... | collective-permute-start | bytes 393224 | tf_op jit(solution)/shard_map/ppermute | solution.py:334
  6.3 1.9 %collective-permute-start.5 = (bf16[128,512]{1,0:T(8,128)(2,1)S(1)}, bf16[128,512]{1,0:T(8,128)(2,1)S(1)}, u32[]{:S(2)}, u32[]{:S(2)}) collective-permute-start(bf16[128,512]{1,0:T(8,128)(2,1)S(1)} %get-tuple-element.49), channel_id=1, source_target_pairs={{0,7},{2,1},{4,3},{6,5},{7,0},{1,2},{3,4},{5,6},{8,15},{10,9},{12,... | collective-permute-start | bytes 393224 | tf_op jit(solution)/shard_map/ppermute | solution.py:334
  8.3 1.5 %collective-permute-start = (bf16[80,256]{1,0:T(8,128)(2,1)S(1)}, bf16[80,256]{1,0:T(8,128)(2,1)S(1)}, u32[]{:S(2)}, u32[]{:S(2)}) collective-permute-start(bf16[80,256]{1,0:T(8,128)(2,1)S(1)} %get-tuple-element.38), channel_id=1, source_target_pairs={{0,8},{8,0},{16,24},{24,16},{1,9},{9,1},{17,25},{25,17},{2,10},{10... | collective-permute-start | bytes 122888 | tf_op jit(solution)/shard_map/ppermute | solution.py:336
  9.7 1.5 %collective-permute-start.1 = (bf16[80,256]{1,0:T(8,128)(2,1)S(1)}, bf16[80,256]{1,0:T(8,128)(2,1)S(1)}, u32[]{:S(2)}, u32[]{:S(2)}) collective-permute-start(bf16[80,256]{1,0:T(8,128)(2,1)S(1)} %get-tuple-element.39), channel_id=1, source_target_pairs={{0,24},{8,16},{16,8},{24,0},{1,25},{9,17},{17,9},{25,1},{2,26},{10... | collective-permute-start | bytes 122888 | tf_op jit(solution)/shard_map/ppermute | solution.py:335
  11.2 0.7 %shard_map.86 = (bf16[128,512]{1,0:T(8,128)(2,1)S(1)}, bf16[128,1024]{1,0:T(8,128)(2,1)S(1)}, bf16[128,1024]{1,0:T(8,128)(2,1)S(1)}) custom-call(bf16[128,512]{1,0:T(8,128)(2,1)S(1)} %get-tuple-element.43.refs_0_, bf16[256,1024]{1,0:T(8,128)(2,1)S(1)} %get-tuple-element.41.refs_1_, bf16[256,1024]{1,0:T(8,128)(2,1)S(1)} %get-tuple-element.42.refs_2_), custom_call_target="tpu_custom_call" | custom-call | tf_op jit(solution)/shard_map/pallas_call | solution.py:30
  12.0 0.0 collective-permute-done.2.refs_0_.refs_3_
  12.0 0.0 copy-start
  12.0 0.7 %shard_map.87 = (bf16[128,512]{1,0:T(8,128)(2,1)S(1)}, bf16[128,1024]{1,0:T(8,128)(2,1)S(1)}, bf16[128,1024]{1,0:T(8,128)(2,1)S(1)}) custom-call(bf16[128,512]{1,0:T(8,128)(2,1)S(1)} %collective-permute-done.2.refs_0_.refs_3_, bf16[256,1024]{1,0:T(8,128)(2,1)S(1)} %get-tuple-element.41.refs_1_, bf16[256,1024]{1,0:T(8,128)(2,1)S(1)} %get-tuple-element.42.refs_2_, ...), custom_call_target="tpu_custom_call" | custom-call | tf_op jit(solution)/shard_map/pallas_call | solution.py:30
  12.7 0.0 collective-permute-done.refs_2_
  12.7 1.9 %collective-permute-done.1.refs_3_ = bf16[80,256]{1,0:T(8,128)(2,1)S(1)} collective-permute-done((bf16[80,256]{1,0:T(8,128)(2,1)S(1)}, bf16[80,256]{1,0:T(8,128)(2,1)S(1)}, u32[]{:S(2)}, u32[]{:S(2)}) %collective-permute-start.1) | collective-permute-done | bytes 40992 | tf_op jit(solution)/shard_map/ppermute | solution.py:335
  14.6 0.0 copy-done
  14.7 0.2 shard_map.88
  14.8 0.1 collective-permute-start.3
  14.9 1.4 %collective-permute-start.4 = (bf16[112,256]{1,0:T(8,128)(2,1)S(1)}, bf16[112,256]{1,0:T(8,128)(2,1)S(1)}, u32[]{:S(2)}, u32[]{:S(2)}) collective-permute-start(bf16[112,256]{1,0:T(8,128)(2,1)S(1)} %get-tuple-element.47), channel_id=1, source_target_pairs={{0,7},{1,2},{2,1},{3,4},{4,3},{5,6},{6,5},{7,0},{8,15},{9,10},{10,... | collective-permute-start | bytes 172040 | tf_op jit(solution)/shard_map/ppermute | solution.py:359
  16.3 0.5 %collective-permute-start.10 = (bf16[128,512]{1,0:T(8,128)(2,1)S(1)}, bf16[128,512]{1,0:T(8,128)(2,1)S(1)}, u32[]{:S(2)}, u32[]{:S(2)}) collective-permute-start(bf16[128,512]{1,0:T(8,128)(2,1)S(1)} %shard_map.95), channel_id=1, source_target_pairs={{0,3},{2,5},{4,7},{6,1},{3,0},{5,2},{7,4},{1,6},{8,11},{10,13},{12... | collective-permute-start | bytes 393224 | tf_op jit(solution)/shard_map/ppermute | solution.py:363
  16.9 0.0 collective-permute-done.6.refs_0_.refs_2_
  16.9 0.7 %shard_map.89 = (bf16[128,512]{1,0:T(8,128)(2,1)S(1)}, bf16[128,1024]{1,0:T(8,128)(2,1)S(1)}, bf16[128,1024]{1,0:T(8,128)(2,1)S(1)}) custom-call(bf16[128,512]{1,0:T(8,128)(2,1)S(1)} %collective-permute-done.6.refs_0_.refs_2_, bf16[256,1024]{1,0:T(8,128)(2,1)S(1)} %get-tuple-element.41.refs_1_, bf16[256,1024]{1,0:T(8,128)(2,1)S(1)} %get-tuple-element.42.refs_2_, ...), custom_call_target="tpu_custom_call" | custom-call | tf_op jit(solution)/shard_map/pallas_call | solution.py:30
  17.6 0.0 collective-permute-done.5.refs_0_.refs_1_
  17.6 0.7 %shard_map.90 = (bf16[128,512]{1,0:T(8,128)(2,1)S(1)}, bf16[128,1024]{1,0:T(8,128)(2,1)S(1)}, bf16[128,1024]{1,0:T(8,128)(2,1)S(1)}) custom-call(bf16[128,512]{1,0:T(8,128)(2,1)S(1)} %collective-permute-done.5.refs_0_.refs_1_, bf16[256,1024]{1,0:T(8,128)(2,1)S(1)} %get-tuple-element.41.refs_1_, bf16[256,1024]{1,0:T(8,128)(2,1)S(1)} %get-tuple-element.42.refs_2_, ...), custom_call_target="tpu_custom_call" | custom-call | tf_op jit(solution)/shard_map/pallas_call | solution.py:30
  18.3 0.8 %shard_map.91 = (f32[2,2,64,1024]{3,2,1,0:T(8,128)S(1)}, bf16[2,2,64,1024]{3,2,1,0:T(8,128)(2,1)S(1)}) custom-call(bf16[128,512]{1,0:T(8,128)(2,1)S(1)} %get-tuple-element.43.refs_0_, bf16[128,512]{1,0:T(8,128)(2,1)S(1)} %collective-permute-done.5.refs_0_.refs_1_, bf16[128,512]{1,0:T(8,128)(2,1)S(1)} %collective-permute-done.6.refs_0_.refs_2_, ...), custom_call_target="tpu_custom_call" | custom-call | tf_op jit(solution)/shard_map/pallas_call | solution.py:30
  19.1 1.5 %collective-permute-start.7 = (bf16[2,2,64,1024]{3,2,1,0:T(8,128)(2,1)S(1)}, bf16[2,2,64,1024]{3,2,1,0:T(8,128)(2,1)S(1)}, u32[]{:S(2)}, u32[]{:S(2)}) collective-permute-start(bf16[2,2,64,1024]{3,2,1,0:T(8,128)(2,1)S(1)} %get-tuple-element.58), channel_id=1, source_target_pairs={{0,1},{1,0},{2,3},{3,2},{4,5},{5,4},{6,7},{7,6},{8,9},{9,8},{10,11... | collective-permute-start | bytes 1572872 | tf_op jit(solution)/shard_map/ppermute | solution.py:377
  20.6 1.6 %collective-permute-start.9 = (bf16[128,512]{1,0:T(8,128)(2,1)S(1)}, bf16[128,512]{1,0:T(8,128)(2,1)S(1)}, u32[]{:S(2)}, u32[]{:S(2)}) collective-permute-start(bf16[128,512]{1,0:T(8,128)(2,1)S(1)} %get-tuple-element.64), channel_id=1, source_target_pairs={{0,5},{2,7},{4,1},{6,3},{5,0},{7,2},{1,4},{3,6},{8,13},{10,15},{12... | collective-permute-start | bytes 393224 | tf_op jit(solution)/shard_map/ppermute | solution.py:346
  22.1 0.0 collective-permute-done.7.refs_1_
  22.1 1.7 %collective-permute-start.8 = (bf16[128,512]{1,0:T(8,128)(2,1)S(1)}, bf16[128,512]{1,0:T(8,128)(2,1)S(1)}, u32[]{:S(2)}, u32[]{:S(2)}) collective-permute-start(bf16[128,512]{1,0:T(8,128)(2,1)S(1)} %get-tuple-element.63), channel_id=1, source_target_pairs={{0,7},{2,1},{4,3},{6,5},{7,0},{1,2},{3,4},{5,6},{8,15},{10,9},{12,... | collective-permute-start | bytes 393224 | tf_op jit(solution)/shard_map/ppermute | solution.py:346
  23.9 0.1 shard_map.93
  24.0 0.0 collective-permute-done.4.refs_5_
  24.0 2.5 %collective-permute-start.11 = (bf16[64,1024]{1,0:T(8,128)(2,1)S(1)}, bf16[64,1024]{1,0:T(8,128)(2,1)S(1)}, u32[]{:S(2)}, u32[]{:S(2)}) collective-permute-start(bf16[64,1024]{1,0:T(8,128)(2,1)S(1)} %get-tuple-element.68), channel_id=1, source_target_pairs={{0,24},{8,16},{16,8},{24,0},{1,25},{9,17},{17,9},{25,1},{2,26},{10... | collective-permute-start | bytes 393224 | tf_op jit(solution)/shard_map/ppermute | solution.py:386
  26.5 0.0 collective-permute-done.3.refs_4_
  26.5 0.5 %collective-permute-start.12 = (bf16[64,1024]{1,0:T(8,128)(2,1)S(1)}, bf16[64,1024]{1,0:T(8,128)(2,1)S(1)}, u32[]{:S(2)}, u32[]{:S(2)}) collective-permute-start(bf16[64,1024]{1,0:T(8,128)(2,1)S(1)} %get-tuple-element.69), channel_id=1, source_target_pairs={{0,8},{8,0},{16,24},{24,16},{1,9},{9,1},{17,25},{25,17},{2,10},{10... | collective-permute-start | bytes 393224 | tf_op jit(solution)/shard_map/ppermute | solution.py:386
  27.0 0.0 collective-permute-done.10.refs_5_
  27.0 0.5 %collective-permute-start.13 = (bf16[64,1024]{1,0:T(8,128)(2,1)S(1)}, bf16[64,1024]{1,0:T(8,128)(2,1)S(1)}, u32[]{:S(2)}, u32[]{:S(2)}) collective-permute-start(bf16[64,1024]{1,0:T(8,128)(2,1)S(1)} %get-tuple-element.70), channel_id=1, source_target_pairs={{0,16},{8,24},{16,0},{24,8},{1,17},{9,25},{17,1},{25,9},{2,18},{10... | collective-permute-start | bytes 393224 | tf_op jit(solution)/shard_map/ppermute | solution.py:386
  27.5 0.9 %shard_map.94 = (f32[256,256]{1,0:T(8,128)S(1)}, bf16[256,512]{1,0:T(8,128)(2,1)S(1)}) custom-call(f32[256,256]{1,0:T(8,128)S(1)} %bitcast.10, f32[256,1]{1,0:T(8,128)S(1)} %get-tuple-element.37.refs_1_, bf16[80,256]{1,0:T(8,128)(2,1)S(1)} %collective-permute-done.refs_2_, bf16[80,256]{1,0:T(8,128)(2,1)S(1)} %collective-permute-done.1.refs_3_, ...), custom_call_target="tpu_custom_call" | custom-call | tf_op jit(solution)/shard_map/pallas_call | solution.py:30
  28.4 3.0 %collective-permute-done.9.refs_4_ = bf16[128,512]{1,0:T(8,128)(2,1)S(1)} collective-permute-done((bf16[128,512]{1,0:T(8,128)(2,1)S(1)}, bf16[128,512]{1,0:T(8,128)(2,1)S(1)}, u32[]{:S(2)}, u32[]{:S(2)}) %collective-permute-start.9) | collective-permute-done | bytes 131104 | tf_op jit(solution)/shard_map/ppermute | solution.py:346
  31.4 0.0 collective-permute-done.8.refs_3_
  31.4 1.1 %shard_map.96 = (f32[256,256]{1,0:T(8,128)}, bf16[256,256]{1,0:T(8,128)(2,1)}) custom-call(f32[256,256]{1,0:T(8,128)S(1)} %get-tuple-element.60.refs_0_, bf16[256,512]{1,0:T(8,128)(2,1)S(1)} %get-tuple-element.61.refs_1_, bf16[128,512]{1,0:T(8,128)(2,1)S(1)} %get-tuple-element.62.refs_2_, bf16[128,512]{1,0:T(8,128)(2,1)S(1)} %collective-permute-done.8.refs_3_, ...), custom_call_target="tpu_custom_call" | custom-call | tf_op jit(solution)/shard_map/pallas_call | solution.py:30
  32.4 0.0 collective-permute-done.11.refs_1_
  32.4 0.0 collective-permute-done.12.refs_2_
  32.5 0.0 collective-permute-done.13.refs_3_
  32.5 0.8 %shard_map.97 = f32[512,128]{1,0:T(8,128)} custom-call(f32[64,1024]{1,0:T(8,128)S(1)} %get-tuple-element.59.refs_7_.refs_0_, bf16[64,1024]{1,0:T(8,128)(2,1)S(1)} %collective-permute-done.11.refs_1_, bf16[64,1024]{1,0:T(8,128)(2,1)S(1)} %collective-permute-done.12.refs_2_, bf16[64,1024]{1,0:T(8,128)(2,1)S(1)} %collective-permute-done.13.refs_3_), custom_call_target="tpu_custom_call" | custom-call | tf_op jit(solution)/shard_map/pallas_call | solution.py:30
  (2 shorter events, 0.0 us)
Async XLA Ops:
  2.1 9.9 %collective-permute-start.2 = (bf16[128,512]{1,0:T(8,128)(2,1)S(1)}, bf16[128,512]{1,0:T(8,128)(2,1)S(1)}, u32[]{:S(2)}, u32[]{:S(2)}) collective-permute-start(bf16[128,512]{1,0:T(8,128)(2,1)S(1)} %get-tuple-element.40), channel_id=1, source_target_pairs={{0,3},{2,5},{4,7},{6,1},{3,0},{5,2},{7,4},{1,6},{8,11},{10,13},{12... | collective-permute-start | bytes 393224 | tf_op jit(solution)/shard_map/ppermute | solution.py:334
  4.6 12.3 %collective-permute-start.6 = (bf16[128,512]{1,0:T(8,128)(2,1)S(1)}, bf16[128,512]{1,0:T(8,128)(2,1)S(1)}, u32[]{:S(2)}, u32[]{:S(2)}) collective-permute-start(bf16[128,512]{1,0:T(8,128)(2,1)S(1)} %get-tuple-element.50), channel_id=1, source_target_pairs={{0,5},{2,7},{4,1},{6,3},{5,0},{7,2},{1,4},{3,6},{8,13},{10,15},{12... | collective-permute-start | bytes 393224 | tf_op jit(solution)/shard_map/ppermute | solution.py:334
  6.3 11.2 %collective-permute-start.5 = (bf16[128,512]{1,0:T(8,128)(2,1)S(1)}, bf16[128,512]{1,0:T(8,128)(2,1)S(1)}, u32[]{:S(2)}, u32[]{:S(2)}) collective-permute-start(bf16[128,512]{1,0:T(8,128)(2,1)S(1)} %get-tuple-element.49), channel_id=1, source_target_pairs={{0,7},{2,1},{4,3},{6,5},{7,0},{1,2},{3,4},{5,6},{8,15},{10,9},{12,... | collective-permute-start | bytes 393224 | tf_op jit(solution)/shard_map/ppermute | solution.py:334
  8.3 4.5 %collective-permute-start = (bf16[80,256]{1,0:T(8,128)(2,1)S(1)}, bf16[80,256]{1,0:T(8,128)(2,1)S(1)}, u32[]{:S(2)}, u32[]{:S(2)}) collective-permute-start(bf16[80,256]{1,0:T(8,128)(2,1)S(1)} %get-tuple-element.38), channel_id=1, source_target_pairs={{0,8},{8,0},{16,24},{24,16},{1,9},{9,1},{17,25},{25,17},{2,10},{10... | collective-permute-start | bytes 122888 | tf_op jit(solution)/shard_map/ppermute | solution.py:336
  9.7 4.9 %collective-permute-start.1 = (bf16[80,256]{1,0:T(8,128)(2,1)S(1)}, bf16[80,256]{1,0:T(8,128)(2,1)S(1)}, u32[]{:S(2)}, u32[]{:S(2)}) collective-permute-start(bf16[80,256]{1,0:T(8,128)(2,1)S(1)} %get-tuple-element.39), channel_id=1, source_target_pairs={{0,24},{8,16},{16,8},{24,0},{1,25},{9,17},{17,9},{25,1},{2,26},{10... | collective-permute-start | bytes 122888 | tf_op jit(solution)/shard_map/ppermute | solution.py:335
  12.0 2.7 %copy-start = (f32[16,16,256]{2,1,0:T(8,128)S(1)}, f32[16,16,256]{2,1,0:T(8,128)}, u32[]{:S(2)}) copy-start(f32[16,16,256]{2,1,0:T(8,128)} %param.6) | copy-start | bytes 786436
  14.8 11.7 %collective-permute-start.3 = (bf16[112,256]{1,0:T(8,128)(2,1)S(1)}, bf16[112,256]{1,0:T(8,128)(2,1)S(1)}, u32[]{:S(2)}, u32[]{:S(2)}) collective-permute-start(bf16[112,256]{1,0:T(8,128)(2,1)S(1)} %get-tuple-element.46.refs_3_.refs_1_), channel_id=1, source_target_pairs={{0,1},{1,0},{2,3},{3,2},{4,5},{5,4},{6,7},{7,6},{8,9},{9,8},{10,11... | collective-permute-start | bytes 172040 | tf_op jit(solution)/shard_map/ppermute | solution.py:360
  14.9 9.0 %collective-permute-start.4 = (bf16[112,256]{1,0:T(8,128)(2,1)S(1)}, bf16[112,256]{1,0:T(8,128)(2,1)S(1)}, u32[]{:S(2)}, u32[]{:S(2)}) collective-permute-start(bf16[112,256]{1,0:T(8,128)(2,1)S(1)} %get-tuple-element.47), channel_id=1, source_target_pairs={{0,7},{1,2},{2,1},{3,4},{4,3},{5,6},{6,5},{7,0},{8,15},{9,10},{10,... | collective-permute-start | bytes 172040 | tf_op jit(solution)/shard_map/ppermute | solution.py:359
  16.3 10.7 %collective-permute-start.10 = (bf16[128,512]{1,0:T(8,128)(2,1)S(1)}, bf16[128,512]{1,0:T(8,128)(2,1)S(1)}, u32[]{:S(2)}, u32[]{:S(2)}) collective-permute-start(bf16[128,512]{1,0:T(8,128)(2,1)S(1)} %shard_map.95), channel_id=1, source_target_pairs={{0,3},{2,5},{4,7},{6,1},{3,0},{5,2},{7,4},{1,6},{8,11},{10,13},{12... | collective-permute-start | bytes 393224 | tf_op jit(solution)/shard_map/ppermute | solution.py:363
  19.1 3.1 %collective-permute-start.7 = (bf16[2,2,64,1024]{3,2,1,0:T(8,128)(2,1)S(1)}, bf16[2,2,64,1024]{3,2,1,0:T(8,128)(2,1)S(1)}, u32[]{:S(2)}, u32[]{:S(2)}) collective-permute-start(bf16[2,2,64,1024]{3,2,1,0:T(8,128)(2,1)S(1)} %get-tuple-element.58), channel_id=1, source_target_pairs={{0,1},{1,0},{2,3},{3,2},{4,5},{5,4},{6,7},{7,6},{8,9},{9,8},{10,11... | collective-permute-start | bytes 1572872 | tf_op jit(solution)/shard_map/ppermute | solution.py:377
  20.6 10.8 %collective-permute-start.9 = (bf16[128,512]{1,0:T(8,128)(2,1)S(1)}, bf16[128,512]{1,0:T(8,128)(2,1)S(1)}, u32[]{:S(2)}, u32[]{:S(2)}) collective-permute-start(bf16[128,512]{1,0:T(8,128)(2,1)S(1)} %get-tuple-element.64), channel_id=1, source_target_pairs={{0,5},{2,7},{4,1},{6,3},{5,0},{7,2},{1,4},{3,6},{8,13},{10,15},{12... | collective-permute-start | bytes 393224 | tf_op jit(solution)/shard_map/ppermute | solution.py:346
  22.1 9.2 %collective-permute-start.8 = (bf16[128,512]{1,0:T(8,128)(2,1)S(1)}, bf16[128,512]{1,0:T(8,128)(2,1)S(1)}, u32[]{:S(2)}, u32[]{:S(2)}) collective-permute-start(bf16[128,512]{1,0:T(8,128)(2,1)S(1)} %get-tuple-element.63), channel_id=1, source_target_pairs={{0,7},{2,1},{4,3},{6,5},{7,0},{1,2},{3,4},{5,6},{8,15},{10,9},{12,... | collective-permute-start | bytes 393224 | tf_op jit(solution)/shard_map/ppermute | solution.py:346
  24.0 8.5 %collective-permute-start.11 = (bf16[64,1024]{1,0:T(8,128)(2,1)S(1)}, bf16[64,1024]{1,0:T(8,128)(2,1)S(1)}, u32[]{:S(2)}, u32[]{:S(2)}) collective-permute-start(bf16[64,1024]{1,0:T(8,128)(2,1)S(1)} %get-tuple-element.68), channel_id=1, source_target_pairs={{0,24},{8,16},{16,8},{24,0},{1,25},{9,17},{17,9},{25,1},{2,26},{10... | collective-permute-start | bytes 393224 | tf_op jit(solution)/shard_map/ppermute | solution.py:386
  26.5 6.0 %collective-permute-start.12 = (bf16[64,1024]{1,0:T(8,128)(2,1)S(1)}, bf16[64,1024]{1,0:T(8,128)(2,1)S(1)}, u32[]{:S(2)}, u32[]{:S(2)}) collective-permute-start(bf16[64,1024]{1,0:T(8,128)(2,1)S(1)} %get-tuple-element.69), channel_id=1, source_target_pairs={{0,8},{8,0},{16,24},{24,16},{1,9},{9,1},{17,25},{25,17},{2,10},{10... | collective-permute-start | bytes 393224 | tf_op jit(solution)/shard_map/ppermute | solution.py:386
  27.0 5.4 %collective-permute-start.13 = (bf16[64,1024]{1,0:T(8,128)(2,1)S(1)}, bf16[64,1024]{1,0:T(8,128)(2,1)S(1)}, u32[]{:S(2)}, u32[]{:S(2)}) collective-permute-start(bf16[64,1024]{1,0:T(8,128)(2,1)S(1)} %get-tuple-element.70), channel_id=1, source_target_pairs={{0,16},{8,24},{16,0},{24,8},{1,17},{9,25},{17,1},{25,9},{2,18},{10... | collective-permute-start | bytes 393224 | tf_op jit(solution)/shard_map/ppermute | solution.py:386
